TPU v7x, 32 devices: a whole 2x2x4 slice. The times are simulated.
32 devices in a mesh: dp: 2 (over y), rot: 16 (over z, x, core).
Axes of the slice: x: 2, y: 2, z: 4, core: 2. Of those that a mesh axis runs over, the one named last changes fastest.
Arguments:
- frames: int32 [32, 128, 512], P('dp'), may hold values from 0 to 8, as said below
- slices: float32 [32, 128, 512], P('rot'), may hold values from 0.125 to 8, as said below
Outputs:
- log_resp: float32 [32, 32, 512], P('dp', 'rot')
- new_slices: float32 [32, 128, 512], P('rot', 'dp')
Inputs may be any that keep to these rules, and one draw needn't show every extreme that they name: `frames`: photon counts; each frame has its own brightness level. `slices`: positive intensities.
All inputs are finite; a program needn't handle non-finite values.
Results may differ from a plain program's by a relative error of at most 0.0012.
Values sent between devices are 32-bit elements; how exact they have to be, the bound alone decides.
No kernel may reach another device: no remote copies, remote signals or barrier semaphores. Data moves between devices by JAX's collectives and lax.ppermute only.
A program may use at most 64 MiB of HBM per device.

v0:
```python
import functools
import math

import jax
import jax.numpy as jnp
import ml_dtypes
import numpy as np
from jax import lax
from jax.experimental import pallas as pl
from jax.experimental.pallas import tpu as pltpu
from jax.sharding import PartitionSpec as P

BF = jnp.bfloat16
F32 = jnp.float32
LANES = 128
SUB = 8
VMEM_BYTES = 24 * 1024 * 1024


def spectrum_tables(n):
    half, quarter = n // 2, n // 4
    index = np.arange(half)
    pieces = []
    for odd in (0, 1):
        theta = (np.outer(index, 2 * np.arange(quarter) + odd) % n) * (2.0 * np.pi / n)
        table = np.concatenate([np.cos(theta), -np.sin(theta)], axis=1)
        if not odd:
            table[:, quarter] = np.where(index % 2 == 0, 1.0, -1.0)
        table = table.astype(np.float32)
        head = table.astype(ml_dtypes.bfloat16)
        pieces += [head, (table - head.astype(np.float32)).astype(ml_dtypes.bfloat16)]
    return np.stack(pieces)


def split2(x):
    head = x.astype(BF)
    return head, (x - head.astype(F32)).astype(BF)


def mm(a, b):
    return jnp.dot(a, b, preferred_element_type=F32)


def mm_t(a, b):
    return lax.dot_general(a, b, (((1,), (1,)), ((), ())), preferred_element_type=F32)


def times_table(x, table, odd, product=mm):
    rows = x.shape[0]
    x0, x1 = split2(x)
    both = product(jnp.concatenate([x0, x1], axis=0), table[2 * odd])
    return both[:rows] + (both[rows:] + product(x0, table[2 * odd + 1]))


def fold(x):
    half = x.shape[-1] // 2
    low, high = x[..., :half], x[..., half:]
    return low + high, low - high


def to_half_spectrum(x, table):
    return [times_table(part, table, odd) for odd, part in enumerate(fold(x))]


def from_half_spectrum(even, odd, table):
    n = 2 * even.shape[1]
    lane = lax.broadcasted_iota(jnp.int32, even.shape, 1)
    weight = jnp.where((lane == 0) | (lane == n // 4), 1.0 / n, 2.0 / n)
    even = times_table(even * weight, table, 0, mm_t)
    odd = times_table(odd * (2.0 / n), table, 1, mm_t)
    return jnp.concatenate([even + odd, even - odd], axis=1)


def sublane_sums(parts):
    row = lax.broadcasted_iota(jnp.int32, parts[0].shape, 0)
    width = SUB // 2
    while width:
        low = (row & width) == 0
        merged = []
        for i in range(width):
            a, b = parts[i], parts[i + width]
            kept, moved = jnp.where(low, a, b), jnp.where(low, b, a)
            if 2 * width == SUB:
                moved = pltpu.roll(moved, width, 0)
            else:
                moved = jnp.where(low, pltpu.roll(moved, SUB - width, 0), pltpu.roll(moved, width, 0))
            merged.append(kept + moved)
        parts = merged
        width //= 2
    return parts[0]


def lane_zero(shape):
    return lax.broadcasted_iota(jnp.int32, shape, len(shape) - 1) == 0


def even_forms(re, im):
    first = lane_zero(re.shape)
    return re, jnp.where(first, 0.0, im), jnp.where(first, im, re)


def expect_kernel(anneal, chunk, groups, mine, frames, slices, table, *refs):
    count, shells, angles = frames.shape
    tilts = slices.shape[0]
    half = angles // 2
    quarter = angles // 4
    chunks = count // chunk
    share = shells // groups
    rows = tilts * shells
    other, refs = refs[: groups - 1], refs[groups - 1 :]
    own_out, scores, local, own, fbuf, sbuf, tv, ya, yb, yc, cross, sems = refs
    spec = (own, *other)
    bases = [pl.multiple_of(lax.rem(mine[0] + s, groups) * share, SUB) for s in range(groups)]

    def frame_copy(c):
        at = pl.ds(c * chunk, chunk)
        return pltpu.make_async_copy(frames.at[at], fbuf.at[at], sems.at[2 + c])

    def own_copy(c):
        at = pl.ds(c * chunk, chunk)
        return pltpu.make_async_copy(own.at[at], own_out.at[at], sems.at[2 + chunks + c])

    table_copy = pltpu.make_async_copy(table, tv, sems.at[0])
    slice_copy = pltpu.make_async_copy(slices, sbuf, sems.at[1])
    table_copy.start()
    slice_copy.start()
    for c in range(chunks):
        frame_copy(c).start()

    table_copy.wait()
    slice_copy.wait()
    logs = jnp.log(sbuf[...]).reshape(rows, angles)
    even, odd = to_half_spectrum(logs, tv)
    a, b, c = even_forms(even[:, :quarter], even[:, quarter:])
    ya[:, :quarter] = jnp.where(lane_zero(a.shape), jnp.sum(logs, axis=1, keepdims=True), a)
    yb[:, :quarter] = b
    yc[...] = c
    ya[:, quarter:] = odd[:, :quarter]
    yb[:, quarter:] = odd[:, quarter:]

    def transform(c):
        at = pl.ds(c * chunk, chunk)
        folded = [fold(fbuf[at, pl.ds(base, share), :]) for base in bases]
        for odd in range(2):
            counts = [part[odd].astype(F32).astype(BF).reshape(chunk * share, half) for part in folded]
            result = mm(jnp.concatenate(counts, axis=0), tv[2 * odd])
            for s in range(groups):
                spec[s][at, :, odd * half : (odd + 1) * half] = result[
                    s * chunk * share : (s + 1) * chunk * share
                ].reshape(chunk, share, half)

    def correlate(c):
        out = pl.ds(c * SUB, SUB)
        for odd in range(2):
            for lanes in range(0, quarter, LANES):
                re_l = pl.ds(odd * half + lanes, LANES)
                im_l = pl.ds(odd * half + quarter + lanes, LANES)
                y_l = pl.ds(odd * quarter + lanes, LANES)
                re, im = [None] * SUB, [None] * SUB
                for pair in range(0, chunk, 2):
                    for s in range(groups):
                        for g in range(share // SUB):
                            r = pl.ds(g * SUB, SUB)
                            ks = [c * chunk + pair + q for q in range(2)]
                            xs = [(spec[s][k, r, re_l], spec[s][k, r, im_l]) for k in ks]
                            for t in range(tilts):
                                y = pl.ds(bases[s] + (t * shells + g * SUB), SUB)
                                a, b = ya[y, y_l], yb[y, y_l]
                                c_ = a if odd else yc[y, pl.ds(lanes, LANES)]
                                for q in range(2):
                                    xr, xi = xs[q]
                                    u = xr * a + xi * b
                                    v = xi * c_ - xr * b
                                    at = t * chunk + pair + q
                                    re[at] = u if re[at] is None else re[at] + u
                                    im[at] = v if im[at] is None else im[at] + v
                cross[out, re_l] = sublane_sums(re)
                cross[out, im_l] = sublane_sums(im)

    frame_copy(0).wait()
    transform(0)
    for c in range(1, chunks):
        frame_copy(c).wait()
        correlate(c - 1)
        transform(c)
        own_copy(c - 1).start()
    own_copy(chunks - 1).start()
    correlate(chunks - 1)

    spectrum = cross[...]
    dc = spectrum[:, :1]
    even = spectrum[:, :half]
    even = jnp.where(lane_zero(even.shape), 0.0, even)
    corr = from_half_spectrum(even, spectrum[:, half:], tv) + dc * (1.0 / angles)
    totals = [
        jnp.broadcast_to(jnp.sum(jnp.sum(sbuf[t], axis=0, keepdims=True), axis=1, keepdims=True), (chunk, 1))
        for t in range(tilts)
    ]
    part = anneal * (corr - jnp.concatenate(totals * chunks, axis=0))
    scores[...] = part

    def over_tilts(x, join):
        parts = []
        for c in range(chunks):
            group = x[c * SUB : (c + 1) * SUB]
            shift = chunk
            while shift < SUB:
                group = join(group, pltpu.roll(group, shift, 0))
                shift *= 2
            parts.append(group)
        return jnp.concatenate(parts, axis=0)

    wide = local.shape
    top = over_tilts(jnp.broadcast_to(jnp.max(part, axis=1, keepdims=True), wide), jnp.maximum)
    total = jnp.sum(jnp.exp(part - top[:, :1]), axis=1, keepdims=True)
    local[...] = top + jnp.log(over_tilts(jnp.broadcast_to(total, wide), jnp.add))
    for c in range(chunks):
        own_copy(c).wait()


def in_hbm(x):
    return pltpu.with_memory_space_constraint(x, pltpu.HBM)


def expect(frames, slices, table, anneal, mine, groups):
    count, shells, angles = frames.shape
    tilts = slices.shape[0]
    half = angles // 2
    chunk = SUB // tilts
    share = shells // groups
    hbm = pl.BlockSpec(memory_space=pltpu.HBM)
    vm = pl.BlockSpec(memory_space=pltpu.VMEM)
    form = pltpu.VMEM((tilts * shells, half), F32)
    *other, own, scores, local = pl.pallas_call(
        functools.partial(expect_kernel, anneal, chunk, groups),
        out_shape=(
            *[pltpu.VMEM((count, share, angles), F32)] * (groups - 1),
            pltpu.HBM((count, share, angles), F32),
            pltpu.VMEM((tilts * count, angles), F32),
            pltpu.VMEM((tilts * count, LANES), F32),
        ),
        in_specs=[pl.BlockSpec(memory_space=pltpu.SMEM)] + [hbm] * 3,
        out_specs=(*[vm] * (groups - 1), hbm, vm, vm),
        scratch_shapes=[
            pltpu.VMEM((count, share, angles), F32),
            pltpu.VMEM((count, shells, angles), jnp.int32),
            pltpu.VMEM((tilts, shells, angles), F32),
            pltpu.VMEM(table.shape, BF),
            form,
            form,
            pltpu.VMEM((tilts * shells, half // 2), F32),
            pltpu.VMEM((tilts * count, angles), F32),
            pltpu.SemaphoreType.DMA((2 + 2 * (count // chunk),)),
        ],
        compiler_params=pltpu.CompilerParams(vmem_limit_bytes=VMEM_BYTES),
        name="expect",
    )(mine[None], *(in_hbm(x) for x in (frames, slices, table)))
    return (own, *other), scores, local


def weights_kernel(scores, local, table, out):
    own = jnp.exp(scores[...] - local[:, :1])
    out[...] = jnp.concatenate(to_half_spectrum(own, table), axis=1)


def row_of(k, t, tilts):
    chunk = SUB // tilts
    return k // chunk * SUB + t * chunk + k % chunk


def back_kernel(spec, transformed, local, lse, out, fa, fb, fc):
    count, share, angles = spec.shape
    half, quarter = angles // 2, angles // 4
    sections = angles // LANES
    tilts = transformed.shape[0] // count
    rows = tilts * share
    scaled = transformed[...] * jnp.exp(local[:, :1] - lse[:, :1])
    a, b, c = even_forms(scaled[:, :quarter], scaled[:, quarter:half])
    fa[:, :quarter] = a
    fb[:, :quarter] = b
    fc[...] = c
    fa[:, quarter:] = scaled[:, half : half + quarter]
    fb[:, quarter:] = scaled[:, half + quarter :]
    for odd in range(2):
        for lanes in range(0, quarter, LANES):
            re_l = pl.ds(odd * half + lanes, LANES)
            im_l = pl.ds(odd * half + quarter + lanes, LANES)
            p_l = pl.ds(odd * quarter + lanes, LANES)
            for g in range(share // SUB):
                r = pl.ds(g * SUB, SUB)
                re, im = [None] * tilts, [None] * tilts
                for k in range(count):
                    xr, xi = spec[k, r, re_l], spec[k, r, im_l]
                    for t in range(tilts):
                        row = pl.ds(row_of(k, t, tilts), 1)
                        a, b = fa[row, p_l], fb[row, p_l]
                        c = a if odd else fc[row, pl.ds(lanes, LANES)]
                        u = xr * a + xi * b
                        v = xi * c - xr * b
                        re[t] = u if k == 0 else re[t] + u
                        im[t] = v if k == 0 else im[t] + v
                for t in range(tilts):
                    at = t * share + g * SUB
                    out[pl.ds((odd * half + lanes) // LANES * rows + at, SUB), :] = re[t]
                    out[pl.ds((odd * half + quarter + lanes) // LANES * rows + at, SUB), :] = im[t]
    tilt_of = lax.broadcasted_iota(jnp.int32, (tilts * count, 1), 0) % SUB // (SUB // tilts)
    sums = [jnp.sum(jnp.where(tilt_of == t, scaled[:, :1], 0.0), axis=0, keepdims=True) for t in range(tilts)]
    tail = jnp.concatenate(sums + [jnp.zeros((out.shape[0] - sections * rows - tilts, 1), F32)], axis=0)
    out[pl.ds(sections * rows, tail.shape[0]), :] = jnp.broadcast_to(tail, (tail.shape[0], LANES))


def back(spec, transformed, local, lse):
    count, share, angles = spec.shape
    half = angles // 2
    tilts = transformed.shape[0] // count
    rows = tilts * share * (angles // LANES) + -(-tilts // SUB) * SUB
    vm = pl.BlockSpec(memory_space=pltpu.VMEM)
    form = pltpu.VMEM((tilts * count, half), F32)
    return pl.pallas_call(
        back_kernel,
        out_shape=pltpu.VMEM((rows, LANES), F32),
        in_specs=[vm] * 4,
        out_specs=vm,
        scratch_shapes=[form, form, pltpu.VMEM((tilts * count, half // 2), F32)],
        compiler_params=pltpu.CompilerParams(vmem_limit_bytes=VMEM_BYTES),
        cost_estimate=pl.CostEstimate(flops=8 * count * tilts * share * half, bytes_accessed=count * share * angles * 4, transcendentals=0),
        name="back",
    )(spec, transformed, local, lse)


def log_kernel(scores, lse, out):
    count, tilts, _ = out.shape
    chunk = SUB // tilts
    value = scores[...] - lse[:, :1]
    for c in range(count // chunk):
        for t in range(tilts):
            at = c * SUB + t * chunk
            out[pl.ds(c * chunk, chunk), t, :] = value[at : at + chunk]


def update_kernel(mine, own, other, slices, table, out):
    tilts, share, angles = out.shape
    half = angles // 2
    sections = angles // LANES
    rows = tilts * share

    def columns(first, last):
        at = [pl.ds(s * rows, rows) for s in range(first, last)]
        return jnp.concatenate([own[r, :] + other[r, :] for r in at], axis=1)

    numer = from_half_spectrum(columns(0, sections // 2), columns(sections // 2, sections), table)
    base = pl.multiple_of(mine[0] * share, SUB)
    for t in range(tilts):
        at = pl.ds(sections * rows + t, 1)
        weight = own[at, :1] + other[at, :1]
        out[t] = (numer[t * share : (t + 1) * share] + slices[t, pl.ds(base, share), :]) / (weight + 1.0)


def log_sum(a, b):
    return jnp.maximum(a, b) + jnp.log(1.0 + jnp.exp(-jnp.abs(a - b)))


def over_axis(value, axis):
    size = lax.axis_size(axis)
    if size & (size - 1):
        return jax.nn.logsumexp(lax.all_gather(value, axis), axis=0)
    bit = 1
    while bit < size:
        step = bit | 1
        value = log_sum(value, lax.ppermute(value, axis, [(i, i ^ step) for i in range(size)]))
        bit *= 2
    return value


def on_device(frames, slices):
    count, shells, angles = frames.shape
    tilts = slices.shape[0]
    anneal = 4.0 / math.sqrt(shells * angles)
    groups = lax.axis_size("dp")
    mine = lax.axis_index("dp").astype(jnp.int32)
    share = shells // groups
    table = jnp.asarray(spectrum_tables(angles))
    vm = pl.BlockSpec(memory_space=pltpu.VMEM)
    params = pltpu.CompilerParams(vmem_limit_bytes=VMEM_BYTES)

    spec, scores, local = expect(frames, slices, table, anneal, mine, groups)
    transformed = pl.pallas_call(
        weights_kernel,
        out_shape=pltpu.VMEM((tilts * count, angles), F32),
        in_specs=[vm] * 3,
        out_specs=vm,
        compiler_params=params,
        cost_estimate=pl.CostEstimate(flops=3 * tilts * count * angles * angles, bytes_accessed=2 * angles * angles, transcendentals=0),
        name="transform",
    )(scores, local, table)
    lse = over_axis(local, "rot")

    others = None
    for step in range(1, groups):
        block = back(spec[step], transformed, local, lse)
        got = lax.ppermute(block, "dp", [(i, (i + step) % groups) for i in range(groups)])
        others = got if others is None else others + got
    own = back(spec[0], transformed, local, lse)
    if others is None:
        others = jnp.zeros_like(own)
    log_resp = pl.pallas_call(
        log_kernel,
        out_shape=jax.ShapeDtypeStruct((count, tilts, angles), F32),
        in_specs=[vm, vm],
        out_specs=vm,
        compiler_params=params,
        name="log_resp",
    )(scores, lse)
    new_slices = pl.pallas_call(
        update_kernel,
        out_shape=jax.ShapeDtypeStruct((tilts, share, angles), F32),
        in_specs=[pl.BlockSpec(memory_space=pltpu.SMEM)] + [vm] * 4,
        out_specs=vm,
        compiler_params=params,
        name="update",
    )(mine[None], own, others, slices, table)
    return (log_resp, new_slices)


def solution(mesh):
    in_specs = (P("dp", None, None), P("rot", None, None))
    out_specs = (P("dp", "rot", None), P("rot", "dp", None))
    return jax.shard_map(on_device, mesh=mesh, in_specs=in_specs, out_specs=out_specs, check_vma=False)
```

profile of v0, /device:TPU:0, one launch (start us, length us, event | category | flops | bytes accessed | tf_op | source)
XLA Modules:
  0.0 29.4 jit_solution(2897049221479239597)
XLA Ops:
  0.6 0.0 copy-start
  0.6 5.2 %expect.1 = (f32[16,64,512]{2,1,0:T(8,128)S(1)}, f32[16,64,512]{2,1,0:T(8,128)}, f32[32,512]{1,0:T(8,128)S(1)}, f32[32,128]{1,0:T(8,128)S(1)}) custom-call(s32[1]{0:T(128)} %bitcast.mine, s32[16,128,512]{2,1,0:T(8,128)} %frames.1, f32[2,128,512]{2,1,0:T(8,128)} %slices.3, bf16[4,256,256]{2,1,0:T(8,128)(2,1)} %constant.10.clone.table), custom_call_target="tpu_custom_call" | custom-call | tf_op jit(solution)/shard_map/expect/pallas_call | solution.py:234
  5.8 0.0 copy-start.1
  5.8 0.5 %collective-permute-start = (f32[32,128]{1,0:T(8,128)S(1)}, f32[32,128]{1,0:T(8,128)S(1)}, u32[]{:S(2)}, u32[]{:S(2)}) collective-permute-start(f32[32,128]{1,0:T(8,128)S(1)} %get-tuple-element.7.local), channel_id=1, source_target_pairs={{0,1},{1,0},{2,3},{3,2},{4,5},{5,4},{6,7},{7,6},{8,9},{9,8},{10,11... | collective-permute-start | bytes 49160 | tf_op jit(solution)/shard_map/ppermute | solution.py:370
  6.4 0.8 %collective-permute-done = f32[32,128]{1,0:T(8,128)S(1)} collective-permute-done((f32[32,128]{1,0:T(8,128)S(1)}, f32[32,128]{1,0:T(8,128)S(1)}, u32[]{:S(2)}, u32[]{:S(2)}) %collective-permute-start) | collective-permute-done | bytes 16416 | tf_op jit(solution)/shard_map/ppermute | solution.py:370
  7.2 2.7 %collective-permute-start.1 = (f32[32,128]{1,0:T(8,128)S(1)}, f32[32,128]{1,0:T(8,128)S(1)}, u32[]{:S(2)}, u32[]{:S(2)}) collective-permute-start(f32[32,128]{1,0:T(8,128)S(1)} %log_add_fusion.3), channel_id=1, source_target_pairs={{0,3},{1,2},{2,1},{3,0},{4,7},{5,6},{6,5},{7,4},{8,11},{9,10},{10,... | collective-permute-start | bytes 49160 | tf_op jit(solution)/shard_map/ppermute | solution.py:370
  9.9 1.4 %collective-permute-done.1 = f32[32,128]{1,0:T(8,128)S(1)} collective-permute-done((f32[32,128]{1,0:T(8,128)S(1)}, f32[32,128]{1,0:T(8,128)S(1)}, u32[]{:S(2)}, u32[]{:S(2)}) %collective-permute-start.1) | collective-permute-done | bytes 16416 | tf_op jit(solution)/shard_map/ppermute | solution.py:370
  11.3 1.9 %collective-permute-start.2 = (f32[32,128]{1,0:T(8,128)S(1)}, f32[32,128]{1,0:T(8,128)S(1)}, u32[]{:S(2)}, u32[]{:S(2)}) collective-permute-start(f32[32,128]{1,0:T(8,128)S(1)} %log_add_fusion.2), channel_id=1, source_target_pairs={{0,5},{1,4},{2,7},{3,6},{4,1},{5,0},{6,3},{7,2},{8,13},{9,12},{10,... | collective-permute-start | bytes 49160 | tf_op jit(solution)/shard_map/ppermute | solution.py:370
  13.2 1.4 %collective-permute-done.2 = f32[32,128]{1,0:T(8,128)S(1)} collective-permute-done((f32[32,128]{1,0:T(8,128)S(1)}, f32[32,128]{1,0:T(8,128)S(1)}, u32[]{:S(2)}, u32[]{:S(2)}) %collective-permute-start.2) | collective-permute-done | bytes 16416 | tf_op jit(solution)/shard_map/ppermute | solution.py:370
  14.7 2.8 %collective-permute-start.3 = (f32[32,128]{1,0:T(8,128)S(1)}, f32[32,128]{1,0:T(8,128)S(1)}, u32[]{:S(2)}, u32[]{:S(2)}) collective-permute-start(f32[32,128]{1,0:T(8,128)S(1)} %log_add_fusion.1), channel_id=1, source_target_pairs={{0,9},{1,8},{2,11},{3,10},{4,13},{5,12},{6,15},{7,14},{8,1},{9,0},... | collective-permute-start | bytes 49160 | tf_op jit(solution)/shard_map/ppermute | solution.py:370
  17.5 0.0 copy-done
  17.5 0.2 transform.1.transformed
  17.7 1.2 %collective-permute-done.3 = f32[32,128]{1,0:T(8,128)S(1)} collective-permute-done((f32[32,128]{1,0:T(8,128)S(1)}, f32[32,128]{1,0:T(8,128)S(1)}, u32[]{:S(2)}, u32[]{:S(2)}) %collective-permute-start.3) | collective-permute-done | bytes 16416 | tf_op jit(solution)/shard_map/ppermute | solution.py:370
  18.9 0.0 copy-start.2
  19.0 0.7 %back.3 = f32[520,128]{1,0:T(8,128)S(1)} custom-call(f32[16,64,512]{2,1,0:T(8,128)S(1)} %get-tuple-element.9.spec, f32[32,512]{1,0:T(8,128)S(1)} %transform.1.transformed, f32[32,128]{1,0:T(8,128)S(1)} %get-tuple-element.7.local, f32[32,128]{1,0:T(8,128)S(1)} %log_add_fusion.lse), custom_call_target="tpu_custom_call" | custom-call | flops 4194304 | bytes 2097152 | tf_op jit(solution)/shard_map/back/pallas_call | solution.py:319
  19.6 1.8 %collective-permute-start.4 = (f32[520,128]{1,0:T(8,128)S(1)}, f32[520,128]{1,0:T(8,128)S(1)}, u32[]{:S(2)}, u32[]{:S(2)}) collective-permute-start(f32[520,128]{1,0:T(8,128)S(1)} %back.3), channel_id=1, source_target_pairs={{0,16},{16,0},{1,17},{17,1},{2,18},{18,2},{3,19},{19,3},{4,20},{20... | collective-permute-start | bytes 798728 | tf_op jit(solution)/shard_map/ppermute | solution.py:401
  21.5 0.7 %log_resp.1 = f32[16,2,512]{2,1,0:T(2,128)} custom-call(f32[32,512]{1,0:T(8,128)S(1)} %get-tuple-element.6.scores, f32[32,128]{1,0:T(8,128)S(1)} %log_add_fusion.lse), custom_call_target="tpu_custom_call" | custom-call | tf_op jit(solution)/shard_map/log_resp/pallas_call | solution.py:406
  22.2 0.0 copy-done.1
  22.2 0.7 %back.2.own = f32[520,128]{1,0:T(8,128)S(1)} custom-call(f32[16,64,512]{2,1,0:T(8,128)S(1)} %copy-done.1, f32[32,512]{1,0:T(8,128)S(1)} %transform.1.transformed, f32[32,128]{1,0:T(8,128)S(1)} %get-tuple-element.7.local, f32[32,128]{1,0:T(8,128)S(1)} %log_add_fusion.lse), custom_call_target="tpu_custom_call" | custom-call | flops 4194304 | bytes 2097152 | tf_op jit(solution)/shard_map/back/pallas_call | solution.py:319
  22.9 5.5 %collective-permute-done.4.other = f32[520,128]{1,0:T(8,128)S(1)} collective-permute-done((f32[520,128]{1,0:T(8,128)S(1)}, f32[520,128]{1,0:T(8,128)S(1)}, u32[]{:S(2)}, u32[]{:S(2)}) %collective-permute-start.4) | collective-permute-done | bytes 266272 | tf_op jit(solution)/shard_map/ppermute | solution.py:401
  28.3 0.0 copy-done.2
  28.3 1.0 %update.1 = f32[2,64,512]{2,1,0:T(8,128)} custom-call(s32[1]{0:T(128)} %bitcast.mine, f32[520,128]{1,0:T(8,128)S(1)} %back.2.own, f32[520,128]{1,0:T(8,128)S(1)} %collective-permute-done.4.other, f32[2,128,512]{2,1,0:T(8,128)S(1)} %copy-done.2, bf16[4,256,256]{2,1,0:T(8,128)(2,1)S(1)} %copy-done), custom_call_target="tpu_custom_call" | custom-call | tf_op jit(solution)/shard_map/update/pallas_call | solution.py:414
  (4 shorter events, 0.1 us)
Async XLA Ops:
  0.6 16.9 %copy-start = (bf16[4,256,256]{2,1,0:T(8,128)(2,1)S(1)}, bf16[4,256,256]{2,1,0:T(8,128)(2,1)}, u32[]{:S(2)}) copy-start(bf16[4,256,256]{2,1,0:T(8,128)(2,1)} %constant.10.clone.table) | copy-start | bytes 1572868
  5.8 16.4 %copy-start.1 = (f32[16,64,512]{2,1,0:T(8,128)S(1)}, f32[16,64,512]{2,1,0:T(8,128)}, u32[]{:S(2)}) copy-start(f32[16,64,512]{2,1,0:T(8,128)} %get-tuple-element.8.spec) | copy-start | bytes 6291460
  5.8 1.4 %collective-permute-start = (f32[32,128]{1,0:T(8,128)S(1)}, f32[32,128]{1,0:T(8,128)S(1)}, u32[]{:S(2)}, u32[]{:S(2)}) collective-permute-start(f32[32,128]{1,0:T(8,128)S(1)} %get-tuple-element.7.local), channel_id=1, source_target_pairs={{0,1},{1,0},{2,3},{3,2},{4,5},{5,4},{6,7},{7,6},{8,9},{9,8},{10,11... | collective-permute-start | bytes 49160 | tf_op jit(solution)/shard_map/ppermute | solution.py:370
  7.2 4.1 %collective-permute-start.1 = (f32[32,128]{1,0:T(8,128)S(1)}, f32[32,128]{1,0:T(8,128)S(1)}, u32[]{:S(2)}, u32[]{:S(2)}) collective-permute-start(f32[32,128]{1,0:T(8,128)S(1)} %log_add_fusion.3), channel_id=1, source_target_pairs={{0,3},{1,2},{2,1},{3,0},{4,7},{5,6},{6,5},{7,4},{8,11},{9,10},{10,... | collective-permute-start | bytes 49160 | tf_op jit(solution)/shard_map/ppermute | solution.py:370
  11.3 3.3 %collective-permute-start.2 = (f32[32,128]{1,0:T(8,128)S(1)}, f32[32,128]{1,0:T(8,128)S(1)}, u32[]{:S(2)}, u32[]{:S(2)}) collective-permute-start(f32[32,128]{1,0:T(8,128)S(1)} %log_add_fusion.2), channel_id=1, source_target_pairs={{0,5},{1,4},{2,7},{3,6},{4,1},{5,0},{6,3},{7,2},{8,13},{9,12},{10,... | collective-permute-start | bytes 49160 | tf_op jit(solution)/shard_map/ppermute | solution.py:370
  14.7 4.3 %collective-permute-start.3 = (f32[32,128]{1,0:T(8,128)S(1)}, f32[32,128]{1,0:T(8,128)S(1)}, u32[]{:S(2)}, u32[]{:S(2)}) collective-permute-start(f32[32,128]{1,0:T(8,128)S(1)} %log_add_fusion.1), channel_id=1, source_target_pairs={{0,9},{1,8},{2,11},{3,10},{4,13},{5,12},{6,15},{7,14},{8,1},{9,0},... | collective-permute-start | bytes 49160 | tf_op jit(solution)/shard_map/ppermute | solution.py:370
  18.9 9.4 %copy-start.2 = (f32[2,128,512]{2,1,0:T(8,128)S(1)}, f32[2,128,512]{2,1,0:T(8,128)}, u32[]{:S(2)}) copy-start(f32[2,128,512]{2,1,0:T(8,128)} %slices.3) | copy-start | bytes 1572868
  19.6 8.7 %collective-permute-start.4 = (f32[520,128]{1,0:T(8,128)S(1)}, f32[520,128]{1,0:T(8,128)S(1)}, u32[]{:S(2)}, u32[]{:S(2)}) collective-permute-start(f32[520,128]{1,0:T(8,128)S(1)} %back.3), channel_id=1, source_target_pairs={{0,16},{16,0},{1,17},{17,1},{2,18},{18,2},{3,19},{19,3},{4,20},{20... | collective-permute-start | bytes 798728 | tf_op jit(solution)/shard_map/ppermute | solution.py:401
where the time goes:
time: 29.5 us; the launch traced here: 29.4 us
  waiting for transfers between devices  10.4 us (35%)
  starting transfers between devices  9.7 us (33%)
  Pallas kernels  8.51 us (29%)
  between operations  0.69 us (2%)
    ppermute x4, starting transfers between devices, over_axis(): lax.ppermute(value, axis, [(i, i ^ step) for i in range(size)])  7.87 us
    ppermute x1, waiting for transfers between devices, on_device(): lax.ppermute(block, 'dp', [(i, (i + step) % groups) for i in range(groups)])  5.46 us
    pallas_call x1, Pallas kernels, expect(): pl.pallas_call(functools.partial(expect_kernel, anneal, chunk, groups), o...  5.16 us
    ppermute x4, waiting for transfers between devices, over_axis(): lax.ppermute(value, axis, [(i, i ^ step) for i in range(size)])  4.94 us
    ppermute x1, starting transfers between devices, on_device(): lax.ppermute(block, 'dp', [(i, (i + step) % groups) for i in range(groups)])  1.83 us
    pallas_call x2, Pallas kernels, back(): pl.pallas_call(back_kernel, out_shape=pltpu.VMEM((rows, LANES), F32), in_...  1.37 us
    pallas_call x1, Pallas kernels, on_device(): pl.pallas_call(update_kernel, out_shape=jax.ShapeDtypeStruct((tilts, shar...  1.03 us
    pallas_call x1, Pallas kernels, on_device(): pl.pallas_call(log_kernel, out_shape=jax.ShapeDtypeStruct((count, tilts,...  0.71 us
  transfers between devices with their start and end apart: 5, of which 5 were waited for; matrix products, arithmetic and copies ran while one was open for 0% of the time, Pallas kernels for 6%

commit v1 on v0

v1 whole, which is shorter than its diff:
```python
import functools
import math

import jax
import jax.numpy as jnp
import ml_dtypes
import numpy as np
from jax import lax
from jax.experimental import pallas as pl
from jax.experimental.pallas import tpu as pltpu
from jax.sharding import PartitionSpec as P

BF = jnp.bfloat16
F32 = jnp.float32
LANES = 128
SUB = 8
VMEM_BYTES = 24 * 1024 * 1024


def spectrum_tables(n):
    half, quarter = n // 2, n // 4
    index = np.arange(half)
    pieces = []
    for odd in (0, 1):
        theta = (np.outer(index, 2 * np.arange(quarter) + odd) % n) * (2.0 * np.pi / n)
        table = np.concatenate([np.cos(theta), -np.sin(theta)], axis=1)
        if not odd:
            table[:, quarter] = np.where(index % 2 == 0, 1.0, -1.0)
        table = table.astype(np.float32)
        head = table.astype(ml_dtypes.bfloat16)
        pieces += [head, (table - head.astype(np.float32)).astype(ml_dtypes.bfloat16)]
    return np.stack(pieces)


def split2(x):
    head = x.astype(BF)
    return head, (x - head.astype(F32)).astype(BF)


def mm(a, b):
    return jnp.dot(a, b, preferred_element_type=F32)


def mm_t(a, b):
    return lax.dot_general(a, b, (((1,), (1,)), ((), ())), preferred_element_type=F32)


def times_table(x, table, odd, product=mm):
    rows = x.shape[0]
    x0, x1 = split2(x)
    both = product(jnp.concatenate([x0, x1], axis=0), table[2 * odd])
    return both[:rows] + (both[rows:] + product(x0, table[2 * odd + 1]))


def fold(x):
    half = x.shape[-1] // 2
    low, high = x[..., :half], x[..., half:]
    return low + high, low - high


def to_half_spectrum(x, table):
    return [times_table(part, table, odd) for odd, part in enumerate(fold(x))]


def from_half_spectrum(even, odd, table):
    n = 2 * even.shape[1]
    lane = lax.broadcasted_iota(jnp.int32, even.shape, 1)
    weight = jnp.where((lane == 0) | (lane == n // 4), 1.0 / n, 2.0 / n)
    even = times_table(even * weight, table, 0, mm_t)
    odd = times_table(odd * (2.0 / n), table, 1, mm_t)
    return jnp.concatenate([even + odd, even - odd], axis=1)


def sublane_sums(parts):
    row = lax.broadcasted_iota(jnp.int32, parts[0].shape, 0)
    width = SUB // 2
    while width:
        low = (row & width) == 0
        merged = []
        for i in range(width):
            a, b = parts[i], parts[i + width]
            kept, moved = jnp.where(low, a, b), jnp.where(low, b, a)
            if 2 * width == SUB:
                moved = pltpu.roll(moved, width, 0)
            else:
                moved = jnp.where(low, pltpu.roll(moved, SUB - width, 0), pltpu.roll(moved, width, 0))
            merged.append(kept + moved)
        parts = merged
        width //= 2
    return parts[0]


def pack_rows(x):
    groups = x.shape[0] // SUB
    lane = lax.broadcasted_iota(jnp.int32, (SUB, LANES), 1)
    packed = x[:SUB]
    for i in range(1, groups):
        packed = jnp.where(lane >= i * (LANES // groups), x[i * SUB : (i + 1) * SUB], packed)
    return packed


def unpack_rows(packed, groups):
    step = LANES // groups
    return jnp.concatenate([packed[:, i * step : i * step + 1] for i in range(groups)], axis=0)


def lane_zero(shape):
    return lax.broadcasted_iota(jnp.int32, shape, len(shape) - 1) == 0


def even_forms(re, im):
    first = lane_zero(re.shape)
    return re, jnp.where(first, 0.0, im), jnp.where(first, im, re)


def spectra(counts, table):
    shape = counts.shape[:2]
    half = counts.shape[2] // 2
    return [
        mm(part.reshape(-1, half), table[2 * odd]).reshape(*shape, half)
        for odd, part in enumerate(fold(counts.astype(F32).astype(BF)))
    ]


def own_shells(step, share):
    groups = lax.axis_size("dp")
    return pl.multiple_of(lax.rem(lax.axis_index("dp") + step, groups) * share, SUB)


def expect_kernel(anneal, chunk, groups, frames, slices, table, *refs):
    count, shells, angles = frames.shape
    tilts = slices.shape[0]
    half, quarter = angles // 2, angles // 4
    chunks = count // chunk
    share = shells // groups
    rows = tilts * shells
    other, refs = refs[: groups - 1], refs[groups - 1 :]
    scores, local, own, fbuf, sbuf, tv, ya, yb, yc, cross, sems = refs
    spec = (own, *other)
    bases = [own_shells(s, share) for s in range(groups)]

    def frame_copy(c):
        at = pl.ds(c * chunk, chunk)
        return pltpu.make_async_copy(frames.at[at], fbuf.at[at], sems.at[2 + c])

    table_copy = pltpu.make_async_copy(table, tv, sems.at[0])
    slice_copy = pltpu.make_async_copy(slices, sbuf, sems.at[1])

    def transform(c):
        at = pl.ds(c * chunk, chunk)
        counts = jnp.concatenate([fbuf[at, pl.ds(base, share), :] for base in bases], axis=1)
        for odd, part in enumerate(spectra(counts, tv)):
            for s in range(groups):
                spec[s][at, :, odd * half : (odd + 1) * half] = part[:, s * share : (s + 1) * share]

    def correlate(c):
        out = pl.ds(c * SUB, SUB)
        for odd in range(2):
            for lanes in range(0, quarter, LANES):
                re_l = pl.ds(odd * half + lanes, LANES)
                im_l = pl.ds(odd * half + quarter + lanes, LANES)
                y_l = pl.ds(odd * quarter + lanes, LANES)
                sums = [[None] * SUB for _ in range(3)]
                for pair in range(0, chunk, 2):
                    for s in range(groups):
                        for g in range(share // SUB):
                            r = pl.ds(g * SUB, SUB)
                            ks = [c * chunk + pair + q for q in range(2)]
                            xs = [(spec[s][k, r, re_l], spec[s][k, r, im_l]) for k in ks]
                            xs = [(xr, xi, xr + xi) for xr, xi in xs]
                            for t in range(tilts):
                                y = pl.ds(bases[s] + (t * shells + g * SUB), SUB)
                                ys = ya[y, y_l], yb[y, y_l], yc[y, y_l]
                                for q in range(2):
                                    at = t * chunk + pair + q
                                    for i in range(3):
                                        u = xs[q][i] * ys[i]
                                        sums[i][at] = u if sums[i][at] is None else sums[i][at] + u
                m = [sublane_sums(part) for part in sums]
                re, im = m[0] + m[1], m[2] - m[0] + m[1]
                if lanes == 0 and not odd:
                    first = lane_zero(re.shape)
                    re, im = jnp.where(first, m[0], re), jnp.where(first, m[1], im)
                cross[out, re_l] = re
                cross[out, im_l] = im

    slice_copy.start()
    table_copy.start()
    for c in range(chunks):
        frame_copy(c).start()

    slice_copy.wait()
    logs = jnp.log(sbuf[...]).reshape(rows, angles)
    folded = fold(logs)
    dc = jnp.sum(logs, axis=1, keepdims=True)
    table_copy.wait()
    even, odd = [times_table(part, tv, i) for i, part in enumerate(folded)]
    even_re = jnp.where(lane_zero((rows, quarter)), dc, even[:, :quarter])
    for i, (re, im) in enumerate(((even_re, even[:, quarter:]), (odd[:, :quarter], odd[:, quarter:]))):
        at = slice(i * quarter, (i + 1) * quarter)
        ya[:, at] = re
        yb[:, at] = im
        yc[:, at] = re - im

    frame_copy(0).wait()
    transform(0)
    for c in range(1, chunks):
        frame_copy(c).wait()
        transform(c)
        correlate(c - 1)
    correlate(chunks - 1)

    spectrum = cross[...]
    dc = spectrum[:, :1]
    even = spectrum[:, :half]
    even = jnp.where(lane_zero(even.shape), 0.0, even)
    corr = from_half_spectrum(even, spectrum[:, half:], tv) + dc * (1.0 / angles)
    totals = [
        jnp.broadcast_to(jnp.sum(jnp.sum(sbuf[t], axis=0, keepdims=True), axis=1, keepdims=True), (chunk, 1))
        for t in range(tilts)
    ]
    part = anneal * (corr - jnp.concatenate(totals * chunks, axis=0))
    scores[...] = part

    def over_tilts(x, join):
        parts = []
        for c in range(chunks):
            group = x[c * SUB : (c + 1) * SUB]
            shift = chunk
            while shift < SUB:
                group = join(group, pltpu.roll(group, shift, 0))
                shift *= 2
            parts.append(group)
        return jnp.concatenate(parts, axis=0)

    wide = (tilts * count, LANES)
    top = over_tilts(jnp.broadcast_to(jnp.max(part, axis=1, keepdims=True), wide), jnp.maximum)
    total = jnp.sum(jnp.exp(part - top[:, :1]), axis=1, keepdims=True)
    local[...] = pack_rows(top + jnp.log(over_tilts(jnp.broadcast_to(total, wide), jnp.add)))


def in_hbm(x):
    return pltpu.with_memory_space_constraint(x, pltpu.HBM)


def expect(frames, slices, table, anneal, groups):
    count, shells, angles = frames.shape
    tilts = slices.shape[0]
    half = angles // 2
    chunk = SUB // tilts
    share = shells // groups
    hbm = pl.BlockSpec(memory_space=pltpu.HBM)
    vm = pl.BlockSpec(memory_space=pltpu.VMEM)
    form = pltpu.VMEM((tilts * shells, half), F32)
    *other, scores, local = pl.pallas_call(
        functools.partial(expect_kernel, anneal, chunk, groups),
        out_shape=(
            *[pltpu.VMEM((count, share, angles), F32)] * (groups - 1),
            pltpu.VMEM((tilts * count, angles), F32),
            pltpu.VMEM((SUB, LANES), F32),
        ),
        in_specs=[hbm] * 3,
        out_specs=(*[vm] * (groups - 1), vm, vm),
        scratch_shapes=[
            pltpu.VMEM((count, share, angles), F32),
            pltpu.VMEM((count, shells, angles), jnp.int32),
            pltpu.VMEM((tilts, shells, angles), F32),
            pltpu.VMEM(table.shape, BF),
            form,
            form,
            form,
            pltpu.VMEM((tilts * count, angles), F32),
            pltpu.SemaphoreType.DMA((2 + count // chunk,)),
        ],
        compiler_params=pltpu.CompilerParams(vmem_limit_bytes=VMEM_BYTES),
        name="expect",
    )(*(in_hbm(x) for x in (frames, slices, table)))
    return other, scores, local


def weights_kernel(scores, local, table, out):
    own = jnp.exp(scores[...] - unpack_rows(local[...], scores.shape[0] // SUB))
    out[...] = jnp.concatenate(to_half_spectrum(own, table), axis=1)


def row_of(k, t, tilts):
    chunk = SUB // tilts
    return k // chunk * SUB + t * chunk + k % chunk


def back_project(spec, transformed, local, lse, out, fa, fb, fc):
    count, share, angles = spec.shape
    half, quarter = angles // 2, angles // 4
    sections = angles // LANES
    tilts = transformed.shape[0] // count
    rows = tilts * share
    scaled = transformed[...] * unpack_rows(jnp.exp(local[...] - lse[...]), tilts * count // SUB)
    for odd in range(2):
        re, im = scaled[:, odd * half : odd * half + quarter], scaled[:, odd * half + quarter : (odd + 1) * half]
        at = slice(odd * quarter, (odd + 1) * quarter)
        fa[:, at] = re
        fb[:, at] = im
        fc[:, at] = re - im
    for odd in range(2):
        for lanes in range(0, quarter, LANES):
            re_l = pl.ds(odd * half + lanes, LANES)
            im_l = pl.ds(odd * half + quarter + lanes, LANES)
            p_l = pl.ds(odd * quarter + lanes, LANES)
            for g in range(share // SUB):
                r = pl.ds(g * SUB, SUB)
                sums = [[None] * tilts for _ in range(3)]
                for k in range(count):
                    xr, xi = spec[k, r, re_l], spec[k, r, im_l]
                    xs = xr, xi, xr + xi
                    for t in range(tilts):
                        row = pl.ds(row_of(k, t, tilts), 1)
                        for i, form in enumerate((fa, fb, fc)):
                            u = xs[i] * form[row, p_l]
                            sums[i][t] = u if k == 0 else sums[i][t] + u
                for t in range(tilts):
                    m = [part[t] for part in sums]
                    re, im = m[0] + m[1], m[2] - m[0] + m[1]
                    if lanes == 0 and not odd:
                        first = lane_zero(re.shape)
                        re, im = jnp.where(first, m[0], re), jnp.where(first, m[1], im)
                    at = t * share + g * SUB
                    out[pl.ds((odd * half + lanes) // LANES * rows + at, SUB), :] = re
                    out[pl.ds((odd * half + quarter + lanes) // LANES * rows + at, SUB), :] = im
    tilt_of = lax.broadcasted_iota(jnp.int32, (tilts * count, 1), 0) % SUB // (SUB // tilts)
    sums = [jnp.sum(jnp.where(tilt_of == t, scaled[:, :1], 0.0), axis=0, keepdims=True) for t in range(tilts)]
    tail = jnp.concatenate(sums + [jnp.zeros((out.shape[0] - sections * rows - tilts, 1), F32)], axis=0)
    out[pl.ds(sections * rows, tail.shape[0]), :] = jnp.broadcast_to(tail, (tail.shape[0], LANES))


def back_own_kernel(transformed, local, lse, frames, table, out, counts, spec, fa, fb, fc, sem):
    count, share, angles = spec.shape
    half = angles // 2
    copy = pltpu.make_async_copy(frames.at[:, pl.ds(own_shells(0, share), share), :], counts, sem)
    copy.start()
    copy.wait()
    chunk = min(count, 8)

    def step(c, carry):
        at = pl.ds(c * chunk, chunk)
        for odd, part in enumerate(spectra(counts[at], table)):
            spec[at, :, odd * half : (odd + 1) * half] = part
        return carry

    lax.fori_loop(0, count // chunk, step, 0)
    back_project(spec, transformed, local, lse, out, fa, fb, fc)


def back(shape, transformed, local, lse, spec=None, frames=None, table=None):
    count, share, angles = shape
    half = angles // 2
    tilts = transformed.shape[0] // count
    rows = tilts * share * (angles // LANES) + -(-tilts // SUB) * SUB
    vm = pl.BlockSpec(memory_space=pltpu.VMEM)
    forms = [pltpu.VMEM((tilts * count, half), F32)] * 3
    call = functools.partial(
        pl.pallas_call,
        out_shape=pltpu.VMEM((rows, LANES), F32),
        out_specs=vm,
        compiler_params=pltpu.CompilerParams(vmem_limit_bytes=VMEM_BYTES),
        cost_estimate=pl.CostEstimate(flops=8 * count * tilts * share * half, bytes_accessed=count * share * angles * 4, transcendentals=0),
    )
    if spec is not None:
        return call(back_project, in_specs=[vm] * 4, scratch_shapes=forms, name="back")(spec, transformed, local, lse)
    return call(
        back_own_kernel,
        in_specs=[vm] * 3 + [pl.BlockSpec(memory_space=pltpu.HBM), vm],
        scratch_shapes=[
            pltpu.VMEM(shape, jnp.int32),
            pltpu.VMEM(shape, F32),
            *forms,
            pltpu.SemaphoreType.DMA,
        ],
        name="back_own",
    )(transformed, local, lse, in_hbm(frames), table)


def log_kernel(scores, lse, out):
    count, tilts, _ = out.shape
    chunk = SUB // tilts
    value = scores[...] - unpack_rows(lse[...], scores.shape[0] // SUB)
    for c in range(count // chunk):
        for t in range(tilts):
            at = c * SUB + t * chunk
            out[pl.ds(c * chunk, chunk), t, :] = value[at : at + chunk]


def update_kernel(own, other, slices, table, out):
    tilts, share, angles = out.shape
    half = angles // 2
    sections = angles // LANES
    rows = tilts * share

    def columns(first, last):
        at = [pl.ds(s * rows, rows) for s in range(first, last)]
        return jnp.concatenate([own[r, :] + other[r, :] for r in at], axis=1)

    numer = from_half_spectrum(columns(0, sections // 2), columns(sections // 2, sections), table)
    base = own_shells(0, share)
    for t in range(tilts):
        at = pl.ds(sections * rows + t, 1)
        weight = own[at, :1] + other[at, :1]
        out[t] = (numer[t * share : (t + 1) * share] + slices[t, pl.ds(base, share), :]) / (weight + 1.0)


def log_sum(a, b):
    return jnp.maximum(a, b) + jnp.log(1.0 + jnp.exp(-jnp.abs(a - b)))


def over_axis(value, axis):
    size = lax.axis_size(axis)
    if size & (size - 1):
        return jax.nn.logsumexp(lax.all_gather(value, axis), axis=0)
    bit = 1
    while bit < size:
        step = bit | 1
        value = log_sum(value, lax.ppermute(value, axis, [(i, i ^ step) for i in range(size)]))
        bit *= 2
    return value


def on_device(frames, slices):
    count, shells, angles = frames.shape
    tilts = slices.shape[0]
    anneal = 4.0 / math.sqrt(shells * angles)
    groups = lax.axis_size("dp")
    share = shells // groups
    table = jnp.asarray(spectrum_tables(angles))
    vm = pl.BlockSpec(memory_space=pltpu.VMEM)
    params = pltpu.CompilerParams(vmem_limit_bytes=VMEM_BYTES)

    spec, scores, local = expect(frames, slices, table, anneal, groups)
    transformed = pl.pallas_call(
        weights_kernel,
        out_shape=pltpu.VMEM((tilts * count, angles), F32),
        in_specs=[vm] * 3,
        out_specs=vm,
        compiler_params=params,
        cost_estimate=pl.CostEstimate(flops=3 * tilts * count * angles * angles, bytes_accessed=2 * angles * angles, transcendentals=0),
        name="transform",
    )(scores, local, table)
    lse = over_axis(local, "rot")

    shape = (count, share, angles)
    others = None
    for step in range(1, groups):
        block = back(shape, transformed, local, lse, spec=spec[step - 1])
        got = lax.ppermute(block, "dp", [(i, (i + step) % groups) for i in range(groups)])
        others = got if others is None else others + got
    own = back(shape, transformed, local, lse, frames=frames, table=table)
    if others is None:
        others = jnp.zeros_like(own)
    log_resp = pl.pallas_call(
        log_kernel,
        out_shape=jax.ShapeDtypeStruct((count, tilts, angles), F32),
        in_specs=[vm, vm],
        out_specs=vm,
        compiler_params=params,
        name="log_resp",
    )(scores, lse)
    new_slices = pl.pallas_call(
        update_kernel,
        out_shape=jax.ShapeDtypeStruct((tilts, share, angles), F32),
        in_specs=[vm] * 4,
        out_specs=vm,
        compiler_params=params,
        name="update",
    )(own, others, slices, table)
    return (log_resp, new_slices)


def solution(mesh):
    in_specs = (P("dp", None, None), P("rot", None, None))
    out_specs = (P("dp", "rot", None), P("rot", "dp", None))
    return jax.shard_map(on_device, mesh=mesh, in_specs=in_specs, out_specs=out_specs, check_vma=False)
```

time: 29.5 us -> 28.2 us (0.956)
  waiting for transfers between devices: 10.4 us -> 7.79 us
  Pallas kernels: 8.51 us -> 9.89 us
    ppermute x1, waiting for transfers between devices: 5.46 us -> 3.28 us  [on_device(): lax.ppermute(block, 'dp', [(i, (i + step) % groups) for i in range(groups)])]
    pallas_call x2, Pallas kernels: 1.37 us -> 3.44 us  [the longest x1 2.78 us: back(): call(back_own_kernel, in_specs=[vm] * 3 + [pl.BlockSpec(memory_space=pltp...]
    pallas_call x1, Pallas kernels: 5.16 us -> 4.35 us  [expect(): pl.pallas_call(functools.partial(expect_kernel, anneal, chunk, groups), o...]
    ppermute x4, waiting for transfers between devices: 4.94 us -> 4.51 us  [over_axis(): lax.ppermute(value, axis, [(i, i ^ step) for i in range(size)])]
  transfers between devices with their start and end apart: 5 -> 5, of which waited for: 5 -> 5; matrix products, arithmetic and copies ran while one was open for 0% -> 0% of each run, Pallas kernels for 6% -> 14%
where the time goes in v1:
time: 28.2 us; the launch traced here: 28.1 us
  Pallas kernels  9.89 us (35%)
  starting transfers between devices  9.64 us (34%)
  waiting for transfers between devices  7.79 us (28%)
  between operations  0.68 us (2%)
    ppermute x4, starting transfers between devices, over_axis(): lax.ppermute(value, axis, [(i, i ^ step) for i in range(size)])  7.77 us
    ppermute x4, waiting for transfers between devices, over_axis(): lax.ppermute(value, axis, [(i, i ^ step) for i in range(size)])  4.51 us
    pallas_call x1, Pallas kernels, expect(): pl.pallas_call(functools.partial(expect_kernel, anneal, chunk, groups), o...  4.35 us
    ppermute x1, waiting for transfers between devices, on_device(): lax.ppermute(block, 'dp', [(i, (i + step) % groups) for i in range(groups)])  3.28 us
    pallas_call x1, Pallas kernels, back(): call(back_own_kernel, in_specs=[vm] * 3 + [pl.BlockSpec(memory_space=pltp...  2.78 us
    ppermute x1, starting transfers between devices, on_device(): lax.ppermute(block, 'dp', [(i, (i + step) % groups) for i in range(groups)])  1.87 us
    pallas_call x1, Pallas kernels, on_device(): pl.pallas_call(update_kernel, out_shape=jax.ShapeDtypeStruct((tilts, shar...  1.02 us
    pallas_call x1, Pallas kernels, on_device(): pl.pallas_call(log_kernel, out_shape=jax.ShapeDtypeStruct((count, tilts,...  0.78 us
  transfers between devices with their start and end apart: 5, of which 5 were waited for; matrix products, arithmetic and copies ran while one was open for 0% of the time, Pallas kernels for 14%

profile of v1, /device:TPU:0, one launch (start us, length us, event | category | flops | bytes accessed | tf_op | source)
XLA Modules:
  0.0 28.1 jit_solution(13628633466452650332)
XLA Ops:
  0.6 0.0 copy-start
  0.6 4.3 %expect.1 = (f32[16,64,512]{2,1,0:T(8,128)S(1)}, f32[32,512]{1,0:T(8,128)S(1)}, f32[8,128]{1,0:T(8,128)S(1)}) custom-call(s32[16,128,512]{2,1,0:T(8,128)} %frames.3, f32[2,128,512]{2,1,0:T(8,128)} %slices.3, bf16[4,256,256]{2,1,0:T(8,128)(2,1)} %constant.4.clone.table), custom_call_target="tpu_custom_call" | custom-call | tf_op jit(solution)/shard_map/expect/pallas_call | solution.py:255
  5.0 0.0 copy-start.1
  5.0 0.5 %collective-permute-start = (f32[8,128]{1,0:T(8,128)S(1)}, f32[8,128]{1,0:T(8,128)S(1)}, u32[]{:S(2)}, u32[]{:S(2)}) collective-permute-start(f32[8,128]{1,0:T(8,128)S(1)} %get-tuple-element.6.local), channel_id=1, source_target_pairs={{0,1},{1,0},{2,3},{3,2},{4,5},{5,4},{6,7},{7,6},{8,9},{9,8},{10,11... | collective-permute-start | bytes 12296 | tf_op jit(solution)/shard_map/ppermute | solution.py:421
  5.5 0.8 %collective-permute-done = f32[8,128]{1,0:T(8,128)S(1)} collective-permute-done((f32[8,128]{1,0:T(8,128)S(1)}, f32[8,128]{1,0:T(8,128)S(1)}, u32[]{:S(2)}, u32[]{:S(2)}) %collective-permute-start) | collective-permute-done | bytes 4128 | tf_op jit(solution)/shard_map/ppermute | solution.py:421
  6.4 2.6 %collective-permute-start.1 = (f32[8,128]{1,0:T(8,128)S(1)}, f32[8,128]{1,0:T(8,128)S(1)}, u32[]{:S(2)}, u32[]{:S(2)}) collective-permute-start(f32[8,128]{1,0:T(8,128)S(1)} %log_add_fusion.3), channel_id=1, source_target_pairs={{0,3},{1,2},{2,1},{3,0},{4,7},{5,6},{6,5},{7,4},{8,11},{9,10},{10,... | collective-permute-start | bytes 12296 | tf_op jit(solution)/shard_map/ppermute | solution.py:421
  9.0 1.3 %collective-permute-done.1 = f32[8,128]{1,0:T(8,128)S(1)} collective-permute-done((f32[8,128]{1,0:T(8,128)S(1)}, f32[8,128]{1,0:T(8,128)S(1)}, u32[]{:S(2)}, u32[]{:S(2)}) %collective-permute-start.1) | collective-permute-done | bytes 4128 | tf_op jit(solution)/shard_map/ppermute | solution.py:421
  10.3 1.8 %collective-permute-start.2 = (f32[8,128]{1,0:T(8,128)S(1)}, f32[8,128]{1,0:T(8,128)S(1)}, u32[]{:S(2)}, u32[]{:S(2)}) collective-permute-start(f32[8,128]{1,0:T(8,128)S(1)} %log_add_fusion.2), channel_id=1, source_target_pairs={{0,5},{1,4},{2,7},{3,6},{4,1},{5,0},{6,3},{7,2},{8,13},{9,12},{10,... | collective-permute-start | bytes 12296 | tf_op jit(solution)/shard_map/ppermute | solution.py:421
  12.2 1.3 %collective-permute-done.2 = f32[8,128]{1,0:T(8,128)S(1)} collective-permute-done((f32[8,128]{1,0:T(8,128)S(1)}, f32[8,128]{1,0:T(8,128)S(1)}, u32[]{:S(2)}, u32[]{:S(2)}) %collective-permute-start.2) | collective-permute-done | bytes 4128 | tf_op jit(solution)/shard_map/ppermute | solution.py:421
  13.5 2.8 %collective-permute-start.3 = (f32[8,128]{1,0:T(8,128)S(1)}, f32[8,128]{1,0:T(8,128)S(1)}, u32[]{:S(2)}, u32[]{:S(2)}) collective-permute-start(f32[8,128]{1,0:T(8,128)S(1)} %log_add_fusion.1), channel_id=1, source_target_pairs={{0,9},{1,8},{2,11},{3,10},{4,13},{5,12},{6,15},{7,14},{8,1},{9,0},... | collective-permute-start | bytes 12296 | tf_op jit(solution)/shard_map/ppermute | solution.py:421
  16.3 0.0 copy-done
  16.3 0.3 %transform.1.transformed = f32[32,512]{1,0:T(8,128)S(1)} custom-call(f32[32,512]{1,0:T(8,128)S(1)} %get-tuple-element.5.scores, f32[8,128]{1,0:T(8,128)S(1)} %get-tuple-element.6.local, bf16[4,256,256]{2,1,0:T(8,128)(2,1)S(1)} %copy-done), custom_call_target="tpu_custom_call" | custom-call | flops 25165824 | bytes 524288 | tf_op jit(solution)/shard_map/transform/pallas_call | solution.py:437
  16.6 1.0 %collective-permute-done.3 = f32[8,128]{1,0:T(8,128)S(1)} collective-permute-done((f32[8,128]{1,0:T(8,128)S(1)}, f32[8,128]{1,0:T(8,128)S(1)}, u32[]{:S(2)}, u32[]{:S(2)}) %collective-permute-start.3) | collective-permute-done | bytes 4128 | tf_op jit(solution)/shard_map/ppermute | solution.py:421
  17.6 0.7 %back.1 = f32[520,128]{1,0:T(8,128)S(1)} custom-call(f32[16,64,512]{2,1,0:T(8,128)S(1)} %get-tuple-element.7.spec, f32[32,512]{1,0:T(8,128)S(1)} %transform.1.transformed, f32[8,128]{1,0:T(8,128)S(1)} %get-tuple-element.6.local, f32[8,128]{1,0:T(8,128)S(1)} %log_add_fusion.lse), custom_call_target="tpu_custom_call" | custom-call | flops 4194304 | bytes 2097152 | tf_op jit(solution)/shard_map/back/pallas_call | solution.py:368
  18.3 1.9 %collective-permute-start.4 = (f32[520,128]{1,0:T(8,128)S(1)}, f32[520,128]{1,0:T(8,128)S(1)}, u32[]{:S(2)}, u32[]{:S(2)}) collective-permute-start(f32[520,128]{1,0:T(8,128)S(1)} %back.1), channel_id=1, source_target_pairs={{0,16},{16,0},{1,17},{17,1},{2,18},{18,2},{3,19},{19,3},{4,20},{20... | collective-permute-start | bytes 798728 | tf_op jit(solution)/shard_map/ppermute | solution.py:452
  20.2 0.8 %log_resp.1 = f32[16,2,512]{2,1,0:T(2,128)} custom-call(f32[32,512]{1,0:T(8,128)S(1)} %get-tuple-element.5.scores, f32[8,128]{1,0:T(8,128)S(1)} %log_add_fusion.lse), custom_call_target="tpu_custom_call" | custom-call | tf_op jit(solution)/shard_map/log_resp/pallas_call | solution.py:457
  21.0 2.8 %back_own.1.own = f32[520,128]{1,0:T(8,128)S(1)} custom-call(f32[32,512]{1,0:T(8,128)S(1)} %transform.1.transformed, f32[8,128]{1,0:T(8,128)S(1)} %get-tuple-element.6.local, f32[8,128]{1,0:T(8,128)S(1)} %log_add_fusion.lse, s32[16,128,512]{2,1,0:T(8,128)} %frames.3, bf16[4,256,256]{2,1,0:T(8,128)(2,1)S(1)} %copy-done), custom_call_target="tpu_custom_call" | custom-call | flops 4194304 | bytes 2097152 | tf_op jit(solution)/shard_map/back_own/pallas_call | solution.py:369
  23.8 3.3 %collective-permute-done.4.other = f32[520,128]{1,0:T(8,128)S(1)} collective-permute-done((f32[520,128]{1,0:T(8,128)S(1)}, f32[520,128]{1,0:T(8,128)S(1)}, u32[]{:S(2)}, u32[]{:S(2)}) %collective-permute-start.4) | collective-permute-done | bytes 266272 | tf_op jit(solution)/shard_map/ppermute | solution.py:452
  27.0 0.0 copy-done.1
  27.0 1.0 %update.1 = f32[2,64,512]{2,1,0:T(8,128)} custom-call(f32[520,128]{1,0:T(8,128)S(1)} %back_own.1.own, f32[520,128]{1,0:T(8,128)S(1)} %collective-permute-done.4.other, f32[2,128,512]{2,1,0:T(8,128)S(1)} %copy-done.1, bf16[4,256,256]{2,1,0:T(8,128)(2,1)S(1)} %copy-done), custom_call_target="tpu_custom_call" | custom-call | tf_op jit(solution)/shard_map/update/pallas_call | solution.py:465
  (4 shorter events, 0.0 us)
Async XLA Ops:
  0.6 15.7 %copy-start = (bf16[4,256,256]{2,1,0:T(8,128)(2,1)S(1)}, bf16[4,256,256]{2,1,0:T(8,128)(2,1)}, u32[]{:S(2)}) copy-start(bf16[4,256,256]{2,1,0:T(8,128)(2,1)} %constant.4.clone.table) | copy-start | bytes 1572868
  5.0 22.0 %copy-start.1 = (f32[2,128,512]{2,1,0:T(8,128)S(1)}, f32[2,128,512]{2,1,0:T(8,128)}, u32[]{:S(2)}) copy-start(f32[2,128,512]{2,1,0:T(8,128)} %slices.3) | copy-start | bytes 1572868
  5.0 1.4 %collective-permute-start = (f32[8,128]{1,0:T(8,128)S(1)}, f32[8,128]{1,0:T(8,128)S(1)}, u32[]{:S(2)}, u32[]{:S(2)}) collective-permute-start(f32[8,128]{1,0:T(8,128)S(1)} %get-tuple-element.6.local), channel_id=1, source_target_pairs={{0,1},{1,0},{2,3},{3,2},{4,5},{5,4},{6,7},{7,6},{8,9},{9,8},{10,11... | collective-permute-start | bytes 12296 | tf_op jit(solution)/shard_map/ppermute | solution.py:421
  6.4 3.9 %collective-permute-start.1 = (f32[8,128]{1,0:T(8,128)S(1)}, f32[8,128]{1,0:T(8,128)S(1)}, u32[]{:S(2)}, u32[]{:S(2)}) collective-permute-start(f32[8,128]{1,0:T(8,128)S(1)} %log_add_fusion.3), channel_id=1, source_target_pairs={{0,3},{1,2},{2,1},{3,0},{4,7},{5,6},{6,5},{7,4},{8,11},{9,10},{10,... | collective-permute-start | bytes 12296 | tf_op jit(solution)/shard_map/ppermute | solution.py:421
  10.3 3.2 %collective-permute-start.2 = (f32[8,128]{1,0:T(8,128)S(1)}, f32[8,128]{1,0:T(8,128)S(1)}, u32[]{:S(2)}, u32[]{:S(2)}) collective-permute-start(f32[8,128]{1,0:T(8,128)S(1)} %log_add_fusion.2), channel_id=1, source_target_pairs={{0,5},{1,4},{2,7},{3,6},{4,1},{5,0},{6,3},{7,2},{8,13},{9,12},{10,... | collective-permute-start | bytes 12296 | tf_op jit(solution)/shard_map/ppermute | solution.py:421
  13.5 4.1 %collective-permute-start.3 = (f32[8,128]{1,0:T(8,128)S(1)}, f32[8,128]{1,0:T(8,128)S(1)}, u32[]{:S(2)}, u32[]{:S(2)}) collective-permute-start(f32[8,128]{1,0:T(8,128)S(1)} %log_add_fusion.1), channel_id=1, source_target_pairs={{0,9},{1,8},{2,11},{3,10},{4,13},{5,12},{6,15},{7,14},{8,1},{9,0},... | collective-permute-start | bytes 12296 | tf_op jit(solution)/shard_map/ppermute | solution.py:421
  18.3 8.7 %collective-permute-start.4 = (f32[520,128]{1,0:T(8,128)S(1)}, f32[520,128]{1,0:T(8,128)S(1)}, u32[]{:S(2)}, u32[]{:S(2)}) collective-permute-start(f32[520,128]{1,0:T(8,128)S(1)} %back.1), channel_id=1, source_target_pairs={{0,16},{16,0},{1,17},{17,1},{2,18},{18,2},{3,19},{19,3},{4,20},{20... | collective-permute-start | bytes 798728 | tf_op jit(solution)/shard_map/ppermute | solution.py:452

commit v2 on v1

--- a/solution.py
+++ b/solution.py
@@ -15,6 +15,7 @@
 LANES = 128
 SUB = 8
 VMEM_BYTES = 24 * 1024 * 1024
+VECTOR_COST = 128
 
 
 def spectrum_tables(n):
@@ -202,13 +203,16 @@
         yb[:, at] = im
         yc[:, at] = re - im
 
-    frame_copy(0).wait()
-    transform(0)
-    for c in range(1, chunks):
-        frame_copy(c).wait()
+    early = max(chunks - 2, 0)
+    waits = {c: (c,) for c in range(early)} | {early: range(early, chunks)}
+    for c in range(chunks):
+        for later in waits.get(c, ()):
+            frame_copy(later).wait()
         transform(c)
-        correlate(c - 1)
-    correlate(chunks - 1)
+        if c < early:
+            correlate(c)
+    for c in range(early, chunks):
+        correlate(c)
 
     spectrum = cross[...]
     dc = spectrum[:, :1]
@@ -278,9 +282,15 @@
     return other, scores, local
 
 
-def weights_kernel(scores, local, table, out):
+def weights_kernel(scores, local, table, forms):
     own = jnp.exp(scores[...] - unpack_rows(local[...], scores.shape[0] // SUB))
-    out[...] = jnp.concatenate(to_half_spectrum(own, table), axis=1)
+    quarter = own.shape[1] // 4
+    for odd, part in enumerate(to_half_spectrum(own, table)):
+        re, im = part[:, :quarter], part[:, quarter:]
+        at = slice(odd * quarter, (odd + 1) * quarter)
+        forms[0, :, at] = re
+        forms[1, :, at] = im
+        forms[2, :, at] = re - im
 
 
 def row_of(k, t, tilts):
@@ -288,19 +298,14 @@
     return k // chunk * SUB + t * chunk + k % chunk
 
 
-def back_project(spec, transformed, local, lse, out, fa, fb, fc):
+def back_project(first_tilt, spec, forms, local, lse, out, scaled):
     count, share, angles = spec.shape
     half, quarter = angles // 2, angles // 4
     sections = angles // LANES
-    tilts = transformed.shape[0] // count
-    rows = tilts * share
-    scaled = transformed[...] * unpack_rows(jnp.exp(local[...] - lse[...]), tilts * count // SUB)
-    for odd in range(2):
-        re, im = scaled[:, odd * half : odd * half + quarter], scaled[:, odd * half + quarter : (odd + 1) * half]
-        at = slice(odd * quarter, (odd + 1) * quarter)
-        fa[:, at] = re
-        fb[:, at] = im
-        fc[:, at] = re - im
+    all_tilts = forms.shape[1] // count
+    tilts = out.shape[0]
+    factor = unpack_rows(jnp.exp(local[...] - lse[...]), all_tilts * count // SUB)
+    scaled[...] = forms[...] * factor[None]
     for odd in range(2):
         for lanes in range(0, quarter, LANES):
             re_l = pl.ds(odd * half + lanes, LANES)
@@ -313,9 +318,9 @@
                     xr, xi = spec[k, r, re_l], spec[k, r, im_l]
                     xs = xr, xi, xr + xi
                     for t in range(tilts):
-                        row = pl.ds(row_of(k, t, tilts), 1)
-                        for i, form in enumerate((fa, fb, fc)):
-                            u = xs[i] * form[row, p_l]
+                        row = pl.ds(row_of(k, first_tilt + t, all_tilts), 1)
+                        for i in range(3):
+                            u = xs[i] * scaled[i, row, p_l]
                             sums[i][t] = u if k == 0 else sums[i][t] + u
                 for t in range(tilts):
                     m = [part[t] for part in sums]
@@ -323,16 +328,15 @@
                     if lanes == 0 and not odd:
                         first = lane_zero(re.shape)
                         re, im = jnp.where(first, m[0], re), jnp.where(first, m[1], im)
-                    at = t * share + g * SUB
-                    out[pl.ds((odd * half + lanes) // LANES * rows + at, SUB), :] = re
-                    out[pl.ds((odd * half + quarter + lanes) // LANES * rows + at, SUB), :] = im
-    tilt_of = lax.broadcasted_iota(jnp.int32, (tilts * count, 1), 0) % SUB // (SUB // tilts)
-    sums = [jnp.sum(jnp.where(tilt_of == t, scaled[:, :1], 0.0), axis=0, keepdims=True) for t in range(tilts)]
-    tail = jnp.concatenate(sums + [jnp.zeros((out.shape[0] - sections * rows - tilts, 1), F32)], axis=0)
-    out[pl.ds(sections * rows, tail.shape[0]), :] = jnp.broadcast_to(tail, (tail.shape[0], LANES))
-
-
-def back_own_kernel(transformed, local, lse, frames, table, out, counts, spec, fa, fb, fc, sem):
+                    out[t, pl.ds((odd * half + lanes) // LANES * share + g * SUB, SUB), :] = re
+                    out[t, pl.ds((odd * half + quarter + lanes) // LANES * share + g * SUB, SUB), :] = im
+    tilt_of = lax.broadcasted_iota(jnp.int32, (all_tilts * count, 1), 0) % SUB // (SUB // all_tilts)
+    for t in range(tilts):
+        weight = jnp.sum(jnp.where(tilt_of == first_tilt + t, scaled[0, :, :1], 0.0), axis=0, keepdims=True)
+        out[t, pl.ds(sections * share, SUB), :] = jnp.broadcast_to(weight, (SUB, LANES))
+
+
+def back_own_kernel(forms, local, lse, frames, table, out, counts, spec, scaled, sem):
     count, share, angles = spec.shape
     half = angles // 2
     copy = pltpu.make_async_copy(frames.at[:, pl.ds(own_shells(0, share), share), :], counts, sem)
@@ -347,39 +351,43 @@
         return carry
 
     lax.fori_loop(0, count // chunk, step, 0)
-    back_project(spec, transformed, local, lse, out, fa, fb, fc)
-
-
-def back(shape, transformed, local, lse, spec=None, frames=None, table=None):
+    back_project(0, spec, forms, local, lse, out, scaled)
+
+
+def back(shape, forms, local, lse, tilts, spec=None, frames=None, table=None):
     count, share, angles = shape
     half = angles // 2
-    tilts = transformed.shape[0] // count
-    rows = tilts * share * (angles // LANES) + -(-tilts // SUB) * SUB
+    all_tilts = forms.shape[1] // count
     vm = pl.BlockSpec(memory_space=pltpu.VMEM)
-    forms = [pltpu.VMEM((tilts * count, half), F32)] * 3
+    scaled = pltpu.VMEM(forms.shape, F32)
     call = functools.partial(
         pl.pallas_call,
-        out_shape=pltpu.VMEM((rows, LANES), F32),
+        out_shape=pltpu.VMEM((len(tilts), share * (angles // LANES) + SUB, LANES), F32),
         out_specs=vm,
         compiler_params=pltpu.CompilerParams(vmem_limit_bytes=VMEM_BYTES),
-        cost_estimate=pl.CostEstimate(flops=8 * count * tilts * share * half, bytes_accessed=count * share * angles * 4, transcendentals=0),
+        cost_estimate=pl.CostEstimate(
+            flops=0 if spec is None else VECTOR_COST * 8 * count * len(tilts) * share * half,
+            bytes_accessed=0 if spec is None else count * share * angles * 4,
+            transcendentals=0,
+        ),
     )
     if spec is not None:
-        return call(back_project, in_specs=[vm] * 4, scratch_shapes=forms, name="back")(spec, transformed, local, lse)
+        kernel = functools.partial(back_project, tilts[0])
+        return call(kernel, in_specs=[vm] * 4, scratch_shapes=[scaled], name="back")(spec, forms, local, lse)
     return call(
         back_own_kernel,
         in_specs=[vm] * 3 + [pl.BlockSpec(memory_space=pltpu.HBM), vm],
         scratch_shapes=[
             pltpu.VMEM(shape, jnp.int32),
             pltpu.VMEM(shape, F32),
-            *forms,
+            scaled,
             pltpu.SemaphoreType.DMA,
         ],
         name="back_own",
-    )(transformed, local, lse, in_hbm(frames), table)
-
-
-def log_kernel(scores, lse, out):
+    )(forms, local, lse, in_hbm(frames), table)
+
+
+def log_kernel(scores, lse, after, out):
     count, tilts, _ = out.shape
     chunk = SUB // tilts
     value = scores[...] - unpack_rows(lse[...], scores.shape[0] // SUB)
@@ -389,22 +397,40 @@
             out[pl.ds(c * chunk, chunk), t, :] = value[at : at + chunk]
 
 
-def update_kernel(own, other, slices, table, out):
-    tilts, share, angles = out.shape
-    half = angles // 2
+def update_kernel(t, own, other, slices, table, *refs):
+    out, result, sem = refs[-3:]
+    share, angles = result.shape
     sections = angles // LANES
-    rows = tilts * share
+
+    def total(at):
+        return own[t, at, :] + other[0, at, :]
 
     def columns(first, last):
-        at = [pl.ds(s * rows, rows) for s in range(first, last)]
-        return jnp.concatenate([own[r, :] + other[r, :] for r in at], axis=1)
+        return jnp.concatenate([total(pl.ds(s * share, share)) for s in range(first, last)], axis=1)
 
     numer = from_half_spectrum(columns(0, sections // 2), columns(sections // 2, sections), table)
-    base = own_shells(0, share)
-    for t in range(tilts):
-        at = pl.ds(sections * rows + t, 1)
-        weight = own[at, :1] + other[at, :1]
-        out[t] = (numer[t * share : (t + 1) * share] + slices[t, pl.ds(base, share), :]) / (weight + 1.0)
+    weight = total(pl.ds(sections * share, 1))[:, :1]
+    result[...] = (numer + slices[t, pl.ds(own_shells(0, share), share), :]) / (weight + 1.0)
+    copy = pltpu.make_async_copy(result, out.at[t], sem)
+    copy.start()
+    copy.wait()
+
+
+def update(t, own, other, slices, table, share, earlier):
+    tilts, _, angles = slices.shape
+    hbm = pl.BlockSpec(memory_space=pltpu.HBM)
+    vm = pl.BlockSpec(memory_space=pltpu.VMEM)
+    more = [] if earlier is None else [earlier]
+    return pl.pallas_call(
+        functools.partial(update_kernel, t),
+        out_shape=jax.ShapeDtypeStruct((tilts, share, angles), F32),
+        in_specs=[vm] * 4 + [hbm] * len(more),
+        out_specs=hbm,
+        scratch_shapes=[pltpu.VMEM((share, angles), F32), pltpu.SemaphoreType.DMA],
+        input_output_aliases={4: 0} if more else {},
+        compiler_params=pltpu.CompilerParams(vmem_limit_bytes=VMEM_BYTES),
+        name="update",
+    )(own, other, slices, table, *more)
 
 
 def log_sum(a, b):
@@ -434,9 +460,9 @@
     params = pltpu.CompilerParams(vmem_limit_bytes=VMEM_BYTES)
 
     spec, scores, local = expect(frames, slices, table, anneal, groups)
-    transformed = pl.pallas_call(
+    forms = pl.pallas_call(
         weights_kernel,
-        out_shape=pltpu.VMEM((tilts * count, angles), F32),
+        out_shape=pltpu.VMEM((3, tilts * count, angles // 2), F32),
         in_specs=[vm] * 3,
         out_specs=vm,
         compiler_params=params,
@@ -446,30 +472,28 @@
     lse = over_axis(local, "rot")
 
     shape = (count, share, angles)
-    others = None
-    for step in range(1, groups):
-        block = back(shape, transformed, local, lse, spec=spec[step - 1])
-        got = lax.ppermute(block, "dp", [(i, (i + step) % groups) for i in range(groups)])
-        others = got if others is None else others + got
-    own = back(shape, transformed, local, lse, frames=frames, table=table)
-    if others is None:
-        others = jnp.zeros_like(own)
+    others = []
+    for t in range(tilts):
+        got = None
+        for step in range(1, groups):
+            block = back(shape, forms, local, lse, range(t, t + 1), spec=spec[step - 1])
+            block = lax.ppermute(block, "dp", [(i, (i + step) % groups) for i in range(groups)])
+            got = block if got is None else got + block
+        others.append(got)
+    own = back(shape, forms, local, lse, range(tilts), frames=frames, table=table)
+    if groups == 1:
+        others = [jnp.zeros_like(own[:1])] * tilts
     log_resp = pl.pallas_call(
         log_kernel,
         out_shape=jax.ShapeDtypeStruct((count, tilts, angles), F32),
-        in_specs=[vm, vm],
+        in_specs=[vm, vm, pl.BlockSpec(memory_space=pl.ANY)],
         out_specs=vm,
         compiler_params=params,
         name="log_resp",
-    )(scores, lse)
-    new_slices = pl.pallas_call(
-        update_kernel,
-        out_shape=jax.ShapeDtypeStruct((tilts, share, angles), F32),
-        in_specs=[vm] * 4,
-        out_specs=vm,
-        compiler_params=params,
-        name="update",
-    )(own, others, slices, table)
+    )(scores, lse, others[0])
+    new_slices = None
+    for t in range(tilts):
+        new_slices = update(t, own, others[t], slices, table, share, new_slices)
     return (log_resp, new_slices)
 
 

time: 28.2 us -> 27.6 us (0.979)
  waiting for transfers between devices: 7.79 us -> 6.2 us
  Pallas kernels: 9.89 us -> 10.6 us
  starting transfers between devices: 9.64 us -> 9.93 us
    ppermute x1 -> x2, waiting for transfers between devices: 3.28 us -> 1.69 us  [on_device(): lax.ppermute(block, 'dp', [(i, (i + step) % groups) for i in range(groups)])]
    pallas_call x3 -> x5, Pallas kernels: 1.99 us -> 3.08 us  [the longest x2 1.92 us: update(): pl.pallas_call(functools.partial(update_kernel, t), out_shape=jax.ShapeDt...]
    pallas_call x1, Pallas kernels: 4.35 us -> 3.95 us  [expect(): pl.pallas_call(functools.partial(expect_kernel, anneal, chunk, groups), o...]
    ppermute x1 -> x2, starting transfers between devices: 1.87 us -> 2.16 us  [on_device(): lax.ppermute(block, 'dp', [(i, (i + step) % groups) for i in range(groups)])]
  transfers between devices with their start and end apart: 5 -> 6, of which waited for: 5 -> 6; matrix products, arithmetic and copies ran while one was open for 0% -> 0% of each run, Pallas kernels for 14% -> 19%
where the time goes in v2:
time: 27.6 us; the launch traced here: 27.4 us
  Pallas kernels  10.6 us (38%)
  starting transfers between devices  9.93 us (36%)
  waiting for transfers between devices  6.2 us (22%)
  between operations  0.69 us (2%)
    ppermute x4, starting transfers between devices, over_axis(): lax.ppermute(value, axis, [(i, i ^ step) for i in range(size)])  7.77 us
    ppermute x4, waiting for transfers between devices, over_axis(): lax.ppermute(value, axis, [(i, i ^ step) for i in range(size)])  4.51 us
    pallas_call x1, Pallas kernels, expect(): pl.pallas_call(functools.partial(expect_kernel, anneal, chunk, groups), o...  3.95 us
    pallas_call x1, Pallas kernels, back(): call(back_own_kernel, in_specs=[vm] * 3 + [pl.BlockSpec(memory_space=pltp...  2.77 us
    ppermute x2, starting transfers between devices, on_device(): lax.ppermute(block, 'dp', [(i, (i + step) % groups) for i in range(groups)])  2.16 us
    pallas_call x2, Pallas kernels, update(): pl.pallas_call(functools.partial(update_kernel, t), out_shape=jax.ShapeDt...  1.92 us
    ppermute x2, waiting for transfers between devices, on_device(): lax.ppermute(block, 'dp', [(i, (i + step) % groups) for i in range(groups)])  1.69 us
    pallas_call x2, Pallas kernels, back(): call(kernel, in_specs=[vm] * 4, scratch_shapes=[scaled], name='back')  0.86 us
  transfers between devices with their start and end apart: 6, of which 6 were waited for; matrix products, arithmetic and copies ran while one was open for 0% of the time, Pallas kernels for 19%

profile of v2, /device:TPU:0, one launch (start us, length us, event | category | flops | bytes accessed | tf_op | source)
XLA Modules:
  0.0 27.4 jit_solution(6679725893094772509)
XLA Ops:
  0.6 0.0 copy-start
  0.6 3.9 %expect.1 = (f32[16,64,512]{2,1,0:T(8,128)S(1)}, f32[32,512]{1,0:T(8,128)S(1)}, f32[8,128]{1,0:T(8,128)S(1)}) custom-call(s32[16,128,512]{2,1,0:T(8,128)} %frames.3, f32[2,128,512]{2,1,0:T(8,128)} %slices.5, bf16[4,256,256]{2,1,0:T(8,128)(2,1)} %constant.4.clone.table), custom_call_target="tpu_custom_call" | custom-call | tf_op jit(solution)/shard_map/expect/pallas_call | solution.py:259
  4.6 0.5 %collective-permute-start = (f32[8,128]{1,0:T(8,128)S(1)}, f32[8,128]{1,0:T(8,128)S(1)}, u32[]{:S(2)}, u32[]{:S(2)}) collective-permute-start(f32[8,128]{1,0:T(8,128)S(1)} %get-tuple-element.6.local), channel_id=1, source_target_pairs={{0,1},{1,0},{2,3},{3,2},{4,5},{5,4},{6,7},{7,6},{8,9},{9,8},{10,11... | collective-permute-start | bytes 12296 | tf_op jit(solution)/shard_map/ppermute | solution.py:447
  5.1 0.8 %collective-permute-done = f32[8,128]{1,0:T(8,128)S(1)} collective-permute-done((f32[8,128]{1,0:T(8,128)S(1)}, f32[8,128]{1,0:T(8,128)S(1)}, u32[]{:S(2)}, u32[]{:S(2)}) %collective-permute-start) | collective-permute-done | bytes 4128 | tf_op jit(solution)/shard_map/ppermute | solution.py:447
  6.0 2.6 %collective-permute-start.1 = (f32[8,128]{1,0:T(8,128)S(1)}, f32[8,128]{1,0:T(8,128)S(1)}, u32[]{:S(2)}, u32[]{:S(2)}) collective-permute-start(f32[8,128]{1,0:T(8,128)S(1)} %log_add_fusion.3), channel_id=1, source_target_pairs={{0,3},{1,2},{2,1},{3,0},{4,7},{5,6},{6,5},{7,4},{8,11},{9,10},{10,... | collective-permute-start | bytes 12296 | tf_op jit(solution)/shard_map/ppermute | solution.py:447
  8.6 1.3 %collective-permute-done.1 = f32[8,128]{1,0:T(8,128)S(1)} collective-permute-done((f32[8,128]{1,0:T(8,128)S(1)}, f32[8,128]{1,0:T(8,128)S(1)}, u32[]{:S(2)}, u32[]{:S(2)}) %collective-permute-start.1) | collective-permute-done | bytes 4128 | tf_op jit(solution)/shard_map/ppermute | solution.py:447
  9.9 1.8 %collective-permute-start.2 = (f32[8,128]{1,0:T(8,128)S(1)}, f32[8,128]{1,0:T(8,128)S(1)}, u32[]{:S(2)}, u32[]{:S(2)}) collective-permute-start(f32[8,128]{1,0:T(8,128)S(1)} %log_add_fusion.2), channel_id=1, source_target_pairs={{0,5},{1,4},{2,7},{3,6},{4,1},{5,0},{6,3},{7,2},{8,13},{9,12},{10,... | collective-permute-start | bytes 12296 | tf_op jit(solution)/shard_map/ppermute | solution.py:447
  11.8 1.3 %collective-permute-done.2 = f32[8,128]{1,0:T(8,128)S(1)} collective-permute-done((f32[8,128]{1,0:T(8,128)S(1)}, f32[8,128]{1,0:T(8,128)S(1)}, u32[]{:S(2)}, u32[]{:S(2)}) %collective-permute-start.2) | collective-permute-done | bytes 4128 | tf_op jit(solution)/shard_map/ppermute | solution.py:447
  13.1 2.8 %collective-permute-start.3 = (f32[8,128]{1,0:T(8,128)S(1)}, f32[8,128]{1,0:T(8,128)S(1)}, u32[]{:S(2)}, u32[]{:S(2)}) collective-permute-start(f32[8,128]{1,0:T(8,128)S(1)} %log_add_fusion.1), channel_id=1, source_target_pairs={{0,9},{1,8},{2,11},{3,10},{4,13},{5,12},{6,15},{7,14},{8,1},{9,0},... | collective-permute-start | bytes 12296 | tf_op jit(solution)/shard_map/ppermute | solution.py:447
  15.9 0.0 copy-done
  15.9 0.3 %transform.1.forms = f32[3,32,256]{2,1,0:T(8,128)S(1)} custom-call(f32[32,512]{1,0:T(8,128)S(1)} %get-tuple-element.5.scores, f32[8,128]{1,0:T(8,128)S(1)} %get-tuple-element.6.local, bf16[4,256,256]{2,1,0:T(8,128)(2,1)S(1)} %copy-done), custom_call_target="tpu_custom_call" | custom-call | flops 25165824 | bytes 524288 | tf_op jit(solution)/shard_map/transform/pallas_call | solution.py:463
  16.2 1.0 %collective-permute-done.3 = f32[8,128]{1,0:T(8,128)S(1)} collective-permute-done((f32[8,128]{1,0:T(8,128)S(1)}, f32[8,128]{1,0:T(8,128)S(1)}, u32[]{:S(2)}, u32[]{:S(2)}) %collective-permute-start.3) | collective-permute-done | bytes 4128 | tf_op jit(solution)/shard_map/ppermute | solution.py:447
  17.2 0.4 %back.2 = f32[1,264,128]{2,1,0:T(8,128)S(1)} custom-call(f32[16,64,512]{2,1,0:T(8,128)S(1)} %get-tuple-element.7.spec, f32[3,32,256]{2,1,0:T(8,128)S(1)} %transform.1.forms, f32[8,128]{1,0:T(8,128)S(1)} %get-tuple-element.6.local, f32[8,128]{1,0:T(8,128)S(1)} %log_add_fusion.lse), custom_call_target="tpu_custom_call" | custom-call | flops 268435456 | bytes 2097152 | tf_op jit(solution)/shard_map/back/pallas_call | solution.py:376
  17.7 0.0 copy-start.1
  17.7 1.9 %collective-permute-start.4 = (f32[1,264,128]{2,1,0:T(8,128)S(1)}, f32[1,264,128]{2,1,0:T(8,128)S(1)}, u32[]{:S(2)}, u32[]{:S(2)}) collective-permute-start(f32[1,264,128]{2,1,0:T(8,128)S(1)} %back.2), channel_id=1, source_target_pairs={{0,16},{16,0},{1,17},{17,1},{2,18},{18,2},{3,19},{19,3},{4,20},{20... | collective-permute-start | bytes 405512 | tf_op jit(solution)/shard_map/ppermute | solution.py:480
  19.6 0.4 %back.3 = f32[1,264,128]{2,1,0:T(8,128)S(1)} custom-call(f32[16,64,512]{2,1,0:T(8,128)S(1)} %get-tuple-element.7.spec, f32[3,32,256]{2,1,0:T(8,128)S(1)} %transform.1.forms, f32[8,128]{1,0:T(8,128)S(1)} %get-tuple-element.6.local, f32[8,128]{1,0:T(8,128)S(1)} %log_add_fusion.lse), custom_call_target="tpu_custom_call" | custom-call | flops 268435456 | bytes 2097152 | tf_op jit(solution)/shard_map/back/pallas_call | solution.py:376
  20.0 0.3 %collective-permute-start.5 = (f32[1,264,128]{2,1,0:T(8,128)S(1)}, f32[1,264,128]{2,1,0:T(8,128)S(1)}, u32[]{:S(2)}, u32[]{:S(2)}) collective-permute-start(f32[1,264,128]{2,1,0:T(8,128)S(1)} %back.3), channel_id=1, source_target_pairs={{0,16},{16,0},{1,17},{17,1},{2,18},{18,2},{3,19},{19,3},{4,20},{20... | collective-permute-start | bytes 405512 | tf_op jit(solution)/shard_map/ppermute | solution.py:480
  20.3 2.8 %back_own.1.own = f32[2,264,128]{2,1,0:T(8,128)S(1)} custom-call(f32[3,32,256]{2,1,0:T(8,128)S(1)} %transform.1.forms, f32[8,128]{1,0:T(8,128)S(1)} %get-tuple-element.6.local, f32[8,128]{1,0:T(8,128)S(1)} %log_add_fusion.lse, s32[16,128,512]{2,1,0:T(8,128)} %frames.3, bf16[4,256,256]{2,1,0:T(8,128)(2,1)S(1)} %copy-done), custom_call_target="tpu_custom_call" | custom-call | tf_op jit(solution)/shard_map/back_own/pallas_call | solution.py:377
  23.0 1.1 %collective-permute-done.4.after.other = f32[1,264,128]{2,1,0:T(8,128)S(1)} collective-permute-done((f32[1,264,128]{2,1,0:T(8,128)S(1)}, f32[1,264,128]{2,1,0:T(8,128)S(1)}, u32[]{:S(2)}, u32[]{:S(2)}) %collective-permute-start.4) | collective-permute-done | bytes 135200 | tf_op jit(solution)/shard_map/ppermute | solution.py:480
  24.1 0.8 %log_resp.1 = f32[16,2,512]{2,1,0:T(2,128)} custom-call(f32[32,512]{1,0:T(8,128)S(1)} %get-tuple-element.5.scores, f32[8,128]{1,0:T(8,128)S(1)} %log_add_fusion.lse, f32[1,264,128]{2,1,0:T(8,128)S(1)} %collective-permute-done.4.after.other), custom_call_target="tpu_custom_call" | custom-call | tf_op jit(solution)/shard_map/log_resp/pallas_call | solution.py:486
  24.9 0.0 copy-done.1
  24.9 1.0 %update.2.refs_0_ = f32[2,64,512]{2,1,0:T(8,128)} custom-call(f32[2,264,128]{2,1,0:T(8,128)S(1)} %back_own.1.own, f32[1,264,128]{2,1,0:T(8,128)S(1)} %collective-permute-done.4.after.other, f32[2,128,512]{2,1,0:T(8,128)S(1)} %copy-done.1, bf16[4,256,256]{2,1,0:T(8,128)(2,1)S(1)} %copy-done), custom_call_target="tpu_custom_call" | custom-call | tf_op jit(solution)/shard_map/update/pallas_call | solution.py:424
  25.9 0.6 %collective-permute-done.5.other = f32[1,264,128]{2,1,0:T(8,128)S(1)} collective-permute-done((f32[1,264,128]{2,1,0:T(8,128)S(1)}, f32[1,264,128]{2,1,0:T(8,128)S(1)}, u32[]{:S(2)}, u32[]{:S(2)}) %collective-permute-start.5) | collective-permute-done | bytes 135200 | tf_op jit(solution)/shard_map/ppermute | solution.py:480
  26.5 1.0 %update.3 = f32[2,64,512]{2,1,0:T(8,128)} custom-call(f32[2,264,128]{2,1,0:T(8,128)S(1)} %back_own.1.own, f32[1,264,128]{2,1,0:T(8,128)S(1)} %collective-permute-done.5.other, f32[2,128,512]{2,1,0:T(8,128)S(1)} %copy-done.1, bf16[4,256,256]{2,1,0:T(8,128)(2,1)S(1)} %copy-done, f32[2,64,512]{2,1,0:T(8,128)} %update.2.refs_0_), custom_call_target="tpu_custom_call", output_to_operand_aliasing={{}: (4, {})} | custom-call | tf_op jit(solution)/shard_map/update/pallas_call | solution.py:424
  (4 shorter events, 0.0 us)
Async XLA Ops:
  0.6 15.3 %copy-start = (bf16[4,256,256]{2,1,0:T(8,128)(2,1)S(1)}, bf16[4,256,256]{2,1,0:T(8,128)(2,1)}, u32[]{:S(2)}) copy-start(bf16[4,256,256]{2,1,0:T(8,128)(2,1)} %constant.4.clone.table) | copy-start | bytes 1572868
  4.6 1.4 %collective-permute-start = (f32[8,128]{1,0:T(8,128)S(1)}, f32[8,128]{1,0:T(8,128)S(1)}, u32[]{:S(2)}, u32[]{:S(2)}) collective-permute-start(f32[8,128]{1,0:T(8,128)S(1)} %get-tuple-element.6.local), channel_id=1, source_target_pairs={{0,1},{1,0},{2,3},{3,2},{4,5},{5,4},{6,7},{7,6},{8,9},{9,8},{10,11... | collective-permute-start | bytes 12296 | tf_op jit(solution)/shard_map/ppermute | solution.py:447
  6.0 3.9 %collective-permute-start.1 = (f32[8,128]{1,0:T(8,128)S(1)}, f32[8,128]{1,0:T(8,128)S(1)}, u32[]{:S(2)}, u32[]{:S(2)}) collective-permute-start(f32[8,128]{1,0:T(8,128)S(1)} %log_add_fusion.3), channel_id=1, source_target_pairs={{0,3},{1,2},{2,1},{3,0},{4,7},{5,6},{6,5},{7,4},{8,11},{9,10},{10,... | collective-permute-start | bytes 12296 | tf_op jit(solution)/shard_map/ppermute | solution.py:447
  9.9 3.2 %collective-permute-start.2 = (f32[8,128]{1,0:T(8,128)S(1)}, f32[8,128]{1,0:T(8,128)S(1)}, u32[]{:S(2)}, u32[]{:S(2)}) collective-permute-start(f32[8,128]{1,0:T(8,128)S(1)} %log_add_fusion.2), channel_id=1, source_target_pairs={{0,5},{1,4},{2,7},{3,6},{4,1},{5,0},{6,3},{7,2},{8,13},{9,12},{10,... | collective-permute-start | bytes 12296 | tf_op jit(solution)/shard_map/ppermute | solution.py:447
  13.1 4.1 %collective-permute-start.3 = (f32[8,128]{1,0:T(8,128)S(1)}, f32[8,128]{1,0:T(8,128)S(1)}, u32[]{:S(2)}, u32[]{:S(2)}) collective-permute-start(f32[8,128]{1,0:T(8,128)S(1)} %log_add_fusion.1), channel_id=1, source_target_pairs={{0,9},{1,8},{2,11},{3,10},{4,13},{5,12},{6,15},{7,14},{8,1},{9,0},... | collective-permute-start | bytes 12296 | tf_op jit(solution)/shard_map/ppermute | solution.py:447
  17.7 7.3 %copy-start.1 = (f32[2,128,512]{2,1,0:T(8,128)S(1)}, f32[2,128,512]{2,1,0:T(8,128)}, u32[]{:S(2)}) copy-start(f32[2,128,512]{2,1,0:T(8,128)} %slices.5) | copy-start | bytes 1572868
  17.7 6.5 %collective-permute-start.4 = (f32[1,264,128]{2,1,0:T(8,128)S(1)}, f32[1,264,128]{2,1,0:T(8,128)S(1)}, u32[]{:S(2)}, u32[]{:S(2)}) collective-permute-start(f32[1,264,128]{2,1,0:T(8,128)S(1)} %back.2), channel_id=1, source_target_pairs={{0,16},{16,0},{1,17},{17,1},{2,18},{18,2},{3,19},{19,3},{4,20},{20... | collective-permute-start | bytes 405512 | tf_op jit(solution)/shard_map/ppermute | solution.py:480
  20.0 6.5 %collective-permute-start.5 = (f32[1,264,128]{2,1,0:T(8,128)S(1)}, f32[1,264,128]{2,1,0:T(8,128)S(1)}, u32[]{:S(2)}, u32[]{:S(2)}) collective-permute-start(f32[1,264,128]{2,1,0:T(8,128)S(1)} %back.3), channel_id=1, source_target_pairs={{0,16},{16,0},{1,17},{17,1},{2,18},{18,2},{3,19},{19,3},{4,20},{20... | collective-permute-start | bytes 405512 | tf_op jit(solution)/shard_map/ppermute | solution.py:480

commit v3 on v2

--- a/solution.py
+++ b/solution.py
@@ -91,18 +91,33 @@
     return parts[0]
 
 
-def pack_rows(x):
+def frame_lanes(groups, tilts, group):
+    frames = SUB // tilts
+    step = LANES // (groups * frames)
+    lane = lax.broadcasted_iota(jnp.int32, (SUB, LANES), 1)
+    row = lax.broadcasted_iota(jnp.int32, (SUB, LANES), 0)
+    return lane, (group * frames + row % frames) * step, step
+
+
+def pack_rows(x, tilts):
     groups = x.shape[0] // SUB
-    lane = lax.broadcasted_iota(jnp.int32, (SUB, LANES), 1)
-    packed = x[:SUB]
-    for i in range(1, groups):
-        packed = jnp.where(lane >= i * (LANES // groups), x[i * SUB : (i + 1) * SUB], packed)
-    return packed
-
-
-def unpack_rows(packed, groups):
-    step = LANES // groups
-    return jnp.concatenate([packed[:, i * step : i * step + 1] for i in range(groups)], axis=0)
+    row = lax.broadcasted_iota(jnp.int32, (SUB, LANES), 0)
+    packed = jnp.zeros((SUB, LANES), F32)
+    for i in range(groups):
+        lane, first, step = frame_lanes(groups, tilts, i)
+        here = (lane >= first) & (lane < first + step) & (row < SUB // tilts)
+        packed = jnp.where(here, x[i * SUB : (i + 1) * SUB], packed)
+    return jnp.sum(packed, axis=0, keepdims=True)
+
+
+def unpack_rows(packed, groups, tilts, width):
+    wide = jnp.broadcast_to(packed, (SUB, LANES))
+    rows = []
+    for i in range(groups):
+        _, first, _ = frame_lanes(groups, tilts, i)
+        row = jnp.take_along_axis(wide, first, axis=1, mode="promise_in_bounds")
+        rows.append(jnp.concatenate([row] * (width // LANES), axis=1))
+    return jnp.concatenate(rows, axis=0)
 
 
 def lane_zero(shape):
@@ -240,7 +255,7 @@
     wide = (tilts * count, LANES)
     top = over_tilts(jnp.broadcast_to(jnp.max(part, axis=1, keepdims=True), wide), jnp.maximum)
     total = jnp.sum(jnp.exp(part - top[:, :1]), axis=1, keepdims=True)
-    local[...] = pack_rows(top + jnp.log(over_tilts(jnp.broadcast_to(total, wide), jnp.add)))
+    local[...] = pack_rows(top + jnp.log(over_tilts(jnp.broadcast_to(total, wide), jnp.add)), tilts)
 
 
 def in_hbm(x):
@@ -261,7 +276,7 @@
         out_shape=(
             *[pltpu.VMEM((count, share, angles), F32)] * (groups - 1),
             pltpu.VMEM((tilts * count, angles), F32),
-            pltpu.VMEM((SUB, LANES), F32),
+            pltpu.VMEM((1, LANES), F32),
         ),
         in_specs=[hbm] * 3,
         out_specs=(*[vm] * (groups - 1), vm, vm),
@@ -282,8 +297,8 @@
     return other, scores, local
 
 
-def weights_kernel(scores, local, table, forms):
-    own = jnp.exp(scores[...] - unpack_rows(local[...], scores.shape[0] // SUB))
+def weights_kernel(tilts, scores, local, table, forms):
+    own = jnp.exp(scores[...] - unpack_rows(local[...], scores.shape[0] // SUB, tilts, scores.shape[1]))
     quarter = own.shape[1] // 4
     for odd, part in enumerate(to_half_spectrum(own, table)):
         re, im = part[:, :quarter], part[:, quarter:]
@@ -298,27 +313,27 @@
     return k // chunk * SUB + t * chunk + k % chunk
 
 
-def back_project(first_tilt, spec, forms, local, lse, out, scaled):
-    count, share, angles = spec.shape
+def back_project(first, spec, forms, local, lse, out, scaled):
+    count, _, angles = spec.shape
     half, quarter = angles // 2, angles // 4
     sections = angles // LANES
-    all_tilts = forms.shape[1] // count
-    tilts = out.shape[0]
-    factor = unpack_rows(jnp.exp(local[...] - lse[...]), all_tilts * count // SUB)
+    tilts = forms.shape[1] // count
+    rows = out.shape[0] // SUB * SUB // sections // (SUB * tilts) * SUB
+    factor = unpack_rows(jnp.exp(local[...] - lse[...]), tilts * count // SUB, tilts, half)
     scaled[...] = forms[...] * factor[None]
     for odd in range(2):
         for lanes in range(0, quarter, LANES):
             re_l = pl.ds(odd * half + lanes, LANES)
             im_l = pl.ds(odd * half + quarter + lanes, LANES)
             p_l = pl.ds(odd * quarter + lanes, LANES)
-            for g in range(share // SUB):
-                r = pl.ds(g * SUB, SUB)
+            for g in range(rows // SUB):
+                r = pl.ds(first + g * SUB, SUB)
                 sums = [[None] * tilts for _ in range(3)]
                 for k in range(count):
                     xr, xi = spec[k, r, re_l], spec[k, r, im_l]
                     xs = xr, xi, xr + xi
                     for t in range(tilts):
-                        row = pl.ds(row_of(k, first_tilt + t, all_tilts), 1)
+                        row = pl.ds(row_of(k, t, tilts), 1)
                         for i in range(3):
                             u = xs[i] * scaled[i, row, p_l]
                             sums[i][t] = u if k == 0 else sums[i][t] + u
@@ -326,14 +341,27 @@
                     m = [part[t] for part in sums]
                     re, im = m[0] + m[1], m[2] - m[0] + m[1]
                     if lanes == 0 and not odd:
-                        first = lane_zero(re.shape)
-                        re, im = jnp.where(first, m[0], re), jnp.where(first, m[1], im)
-                    out[t, pl.ds((odd * half + lanes) // LANES * share + g * SUB, SUB), :] = re
-                    out[t, pl.ds((odd * half + quarter + lanes) // LANES * share + g * SUB, SUB), :] = im
-    tilt_of = lax.broadcasted_iota(jnp.int32, (all_tilts * count, 1), 0) % SUB // (SUB // all_tilts)
-    for t in range(tilts):
-        weight = jnp.sum(jnp.where(tilt_of == first_tilt + t, scaled[0, :, :1], 0.0), axis=0, keepdims=True)
-        out[t, pl.ds(sections * share, SUB), :] = jnp.broadcast_to(weight, (SUB, LANES))
+                        first_lane = lane_zero(re.shape)
+                        re, im = jnp.where(first_lane, m[0], re), jnp.where(first_lane, m[1], im)
+                    at = t * rows + g * SUB
+                    out[pl.ds((odd * half + lanes) // LANES * tilts * rows + at, SUB), :] = re
+                    out[pl.ds((odd * half + quarter + lanes) // LANES * tilts * rows + at, SUB), :] = im
+    if out.shape[0] > sections * tilts * rows:
+        tilt_of = lax.broadcasted_iota(jnp.int32, (tilts * count, 1), 0) % SUB // (SUB // tilts)
+        dc = scaled[0, :, :1]
+        sums = [jnp.sum(jnp.where(tilt_of == t, dc, 0.0), axis=0, keepdims=True) for t in range(tilts)]
+        tail = jnp.concatenate(sums + [jnp.zeros((SUB - tilts, 1), F32)], axis=0)
+        out[pl.ds(sections * tilts * rows, SUB), :] = jnp.broadcast_to(tail, (SUB, LANES))
+
+
+def back_signal_kernel(first, spec, forms, local, lse, table, out, scaled, half_spectrum):
+    back_project(first, spec, forms, local, lse, half_spectrum, scaled)
+    rows = out.shape[0]
+    sections = out.shape[1] // LANES
+    parts = [half_spectrum[pl.ds(s * rows, rows), :] for s in range(sections)]
+    even = jnp.concatenate(parts[: sections // 2], axis=1)
+    odd = jnp.concatenate(parts[sections // 2 :], axis=1)
+    out[...] = from_half_spectrum(even, odd, table)
 
 
 def back_own_kernel(forms, local, lse, frames, table, out, counts, spec, scaled, sem):
@@ -354,26 +382,34 @@
     back_project(0, spec, forms, local, lse, out, scaled)
 
 
-def back(shape, forms, local, lse, tilts, spec=None, frames=None, table=None):
+def back(shape, forms, local, lse, first, rows, spec=None, frames=None, table=None):
     count, share, angles = shape
     half = angles // 2
-    all_tilts = forms.shape[1] // count
+    tilts = forms.shape[1] // count
     vm = pl.BlockSpec(memory_space=pltpu.VMEM)
     scaled = pltpu.VMEM(forms.shape, F32)
     call = functools.partial(
         pl.pallas_call,
-        out_shape=pltpu.VMEM((len(tilts), share * (angles // LANES) + SUB, LANES), F32),
+        out_shape=pltpu.VMEM((tilts * rows * (angles // LANES) + (0 if first else SUB), LANES), F32),
         out_specs=vm,
         compiler_params=pltpu.CompilerParams(vmem_limit_bytes=VMEM_BYTES),
         cost_estimate=pl.CostEstimate(
-            flops=0 if spec is None else VECTOR_COST * 8 * count * len(tilts) * share * half,
-            bytes_accessed=0 if spec is None else count * share * angles * 4,
+            flops=0 if spec is None else VECTOR_COST * 8 * count * tilts * rows * half,
+            bytes_accessed=0 if spec is None else count * rows * angles * 4,
             transcendentals=0,
         ),
     )
     if spec is not None:
-        kernel = functools.partial(back_project, tilts[0])
-        return call(kernel, in_specs=[vm] * 4, scratch_shapes=[scaled], name="back")(spec, forms, local, lse)
+        if table is None:
+            kernel = functools.partial(back_project, first)
+            return call(kernel, in_specs=[vm] * 4, scratch_shapes=[scaled], name="back")(spec, forms, local, lse)
+        return call(
+            functools.partial(back_signal_kernel, first),
+            out_shape=pltpu.VMEM((tilts * rows, angles), F32),
+            in_specs=[vm] * 5,
+            scratch_shapes=[scaled, pltpu.VMEM((tilts * rows * (angles // LANES), LANES), F32)],
+            name="back_signal",
+        )(spec, forms, local, lse, table)
     return call(
         back_own_kernel,
         in_specs=[vm] * 3 + [pl.BlockSpec(memory_space=pltpu.HBM), vm],
@@ -390,47 +426,84 @@
 def log_kernel(scores, lse, after, out):
     count, tilts, _ = out.shape
     chunk = SUB // tilts
-    value = scores[...] - unpack_rows(lse[...], scores.shape[0] // SUB)
+    value = scores[...] - unpack_rows(lse[...], scores.shape[0] // SUB, tilts, scores.shape[1])
     for c in range(count // chunk):
         for t in range(tilts):
             at = c * SUB + t * chunk
             out[pl.ds(c * chunk, chunk), t, :] = value[at : at + chunk]
 
 
-def update_kernel(t, own, other, slices, table, *refs):
-    out, result, sem = refs[-3:]
-    share, angles = result.shape
+def update_kernel(own, other, slices, table, out, rest, factor, result, sem):
+    tilts, rows, angles = result.shape
+    share = out.shape[1]
     sections = angles // LANES
 
-    def total(at):
-        return own[t, at, :] + other[0, at, :]
-
-    def columns(first, last):
-        return jnp.concatenate([total(pl.ds(s * share, share)) for s in range(first, last)], axis=1)
-
-    numer = from_half_spectrum(columns(0, sections // 2), columns(sections // 2, sections), table)
-    weight = total(pl.ds(sections * share, 1))[:, :1]
-    result[...] = (numer + slices[t, pl.ds(own_shells(0, share), share), :]) / (weight + 1.0)
-    copy = pltpu.make_async_copy(result, out.at[t], sem)
+    def numer(first, count, extra):
+        columns = []
+        for s in range(sections):
+            mine = [own[pl.ds((s * tilts + t) * share + first, count), :] for t in range(tilts)]
+            column = jnp.concatenate(mine, axis=0)
+            columns.append(column + extra[pl.ds(s * tilts * count, tilts * count), :] if extra is not None else column)
+        even = jnp.concatenate(columns[: sections // 2], axis=1)
+        odd = jnp.concatenate(columns[sections // 2 :], axis=1)
+        return from_half_spectrum(even, odd, table)
+
+    at = [ref[pl.ds(ref.shape[0] - SUB, SUB), :] for ref in (own, other)]
+    scale = 1.0 / (at[0] + at[1] + 1.0)
+    base = own_shells(0, share)
+    done = numer(0, rows, other)
+    for t in range(tilts):
+        before = slices[t, pl.ds(base, rows), :]
+        result[t] = (done[t * rows : (t + 1) * rows] + before) * scale[t : t + 1, :1]
+    copy = pltpu.make_async_copy(result, out.at[:, pl.ds(0, rows), :], sem)
+    copy.start()
+    left = share - rows
+    part = numer(rows, left, None)
+    for t in range(tilts):
+        to = slice(t * left, (t + 1) * left)
+        before = slices[t, pl.ds(base + rows, left), :]
+        rest[to, :] = (part[to] + before) * scale[t : t + 1, :1]
+        factor[to, :] = jnp.broadcast_to(scale[t : t + 1, :], (left, LANES))
+    copy.wait()
+
+
+def finish_kernel(other, rest, factor, earlier, out, result, sem):
+    tilts, rows, angles = result.shape
+    share = out.shape[1]
+    for lanes in range(0, angles, LANES):
+        at = pl.ds(lanes, LANES)
+        result[:, :, at] = (other[:, at] * factor[...] + rest[:, at]).reshape(tilts, rows, LANES)
+    copy = pltpu.make_async_copy(result, out.at[:, pl.ds(share - rows, rows), :], sem)
     copy.start()
     copy.wait()
 
 
-def update(t, own, other, slices, table, share, earlier):
+def update(own, others, slices, table, share, rows):
     tilts, _, angles = slices.shape
+    left = share - rows
     hbm = pl.BlockSpec(memory_space=pltpu.HBM)
     vm = pl.BlockSpec(memory_space=pltpu.VMEM)
-    more = [] if earlier is None else [earlier]
+    params = pltpu.CompilerParams(vmem_limit_bytes=VMEM_BYTES)
+    whole = jax.ShapeDtypeStruct((tilts, share, angles), F32)
+    new, rest, factor = pl.pallas_call(
+        update_kernel,
+        out_shape=(whole, pltpu.VMEM((tilts * left, angles), F32), pltpu.VMEM((tilts * left, LANES), F32)),
+        in_specs=[vm] * 4,
+        out_specs=(hbm, vm, vm),
+        scratch_shapes=[pltpu.VMEM((tilts, rows, angles), F32), pltpu.SemaphoreType.DMA],
+        compiler_params=params,
+        name="update",
+    )(own, others[0], slices, table)
     return pl.pallas_call(
-        functools.partial(update_kernel, t),
-        out_shape=jax.ShapeDtypeStruct((tilts, share, angles), F32),
-        in_specs=[vm] * 4 + [hbm] * len(more),
+        finish_kernel,
+        out_shape=whole,
+        in_specs=[vm] * 3 + [hbm],
         out_specs=hbm,
-        scratch_shapes=[pltpu.VMEM((share, angles), F32), pltpu.SemaphoreType.DMA],
-        input_output_aliases={4: 0} if more else {},
-        compiler_params=pltpu.CompilerParams(vmem_limit_bytes=VMEM_BYTES),
-        name="update",
-    )(own, other, slices, table, *more)
+        scratch_shapes=[pltpu.VMEM((tilts, left, angles), F32), pltpu.SemaphoreType.DMA],
+        input_output_aliases={3: 0},
+        compiler_params=params,
+        name="finish",
+    )(others[1], rest, factor, new)
 
 
 def log_sum(a, b):
@@ -461,7 +534,7 @@
 
     spec, scores, local = expect(frames, slices, table, anneal, groups)
     forms = pl.pallas_call(
-        weights_kernel,
+        functools.partial(weights_kernel, tilts),
         out_shape=pltpu.VMEM((3, tilts * count, angles // 2), F32),
         in_specs=[vm] * 3,
         out_specs=vm,
@@ -472,17 +545,16 @@
     lse = over_axis(local, "rot")
 
     shape = (count, share, angles)
+    rows = share // 2 // SUB * SUB
     others = []
-    for t in range(tilts):
+    for first, shells_, signal in ((0, rows, None), (rows, share - rows, table)):
         got = None
         for step in range(1, groups):
-            block = back(shape, forms, local, lse, range(t, t + 1), spec=spec[step - 1])
+            block = back(shape, forms, local, lse, first, shells_, spec=spec[step - 1], table=signal)
             block = lax.ppermute(block, "dp", [(i, (i + step) % groups) for i in range(groups)])
             got = block if got is None else got + block
         others.append(got)
-    own = back(shape, forms, local, lse, range(tilts), frames=frames, table=table)
-    if groups == 1:
-        others = [jnp.zeros_like(own[:1])] * tilts
+    own = back(shape, forms, local, lse, 0, share, frames=frames, table=table)
     log_resp = pl.pallas_call(
         log_kernel,
         out_shape=jax.ShapeDtypeStruct((count, tilts, angles), F32),
@@ -491,9 +563,7 @@
         compiler_params=params,
         name="log_resp",
     )(scores, lse, others[0])
-    new_slices = None
-    for t in range(tilts):
-        new_slices = update(t, own, others[t], slices, table, share, new_slices)
+    new_slices = update(own, others, slices, table, share, rows)
     return (log_resp, new_slices)
 
 

time: 27.6 us -> 26.9 us (0.975)
  waiting for transfers between devices: 6.2 us -> 5.85 us
  Pallas kernels: 10.6 us -> 10.3 us
    pallas_call x2 -> x1, Pallas kernels: 0.86 us -> 0.37 us  [back(): call(kernel, in_specs=[vm] * 4, scratch_shapes=[scaled], name='back')]
    pallas_call x3 -> x4, Pallas kernels: 2.22 us -> 2.56 us  [the longest x1 0.98 us: update(): pl.pallas_call(update_kernel, out_shape=(whole, pltpu.VMEM((tilts * left,...]
    ppermute x2, waiting for transfers between devices: 1.69 us -> 1.39 us  [on_device(): lax.ppermute(block, 'dp', [(i, (i + step) % groups) for i in range(groups)])]
  transfers between devices with their start and end apart: 6 -> 6, of which waited for: 6 -> 6; matrix products, arithmetic and copies ran while one was open for 0% -> 0% of each run, Pallas kernels for 19% -> 20%
where the time goes in v3:
time: 26.9 us; the launch traced here: 26.8 us
  Pallas kernels  10.3 us (38%)
  starting transfers between devices  9.86 us (37%)
  waiting for transfers between devices  5.85 us (22%)
  between operations  0.69 us (3%)
    ppermute x4, starting transfers between devices, over_axis(): lax.ppermute(value, axis, [(i, i ^ step) for i in range(size)])  7.71 us
    ppermute x4, waiting for transfers between devices, over_axis(): lax.ppermute(value, axis, [(i, i ^ step) for i in range(size)])  4.46 us
    pallas_call x1, Pallas kernels, expect(): pl.pallas_call(functools.partial(expect_kernel, anneal, chunk, groups), o...  3.93 us
    pallas_call x1, Pallas kernels, back(): call(back_own_kernel, in_specs=[vm] * 3 + [pl.BlockSpec(memory_space=pltp...  2.73 us
    ppermute x2, starting transfers between devices, on_device(): lax.ppermute(block, 'dp', [(i, (i + step) % groups) for i in range(groups)])  2.15 us
    ppermute x2, waiting for transfers between devices, on_device(): lax.ppermute(block, 'dp', [(i, (i + step) % groups) for i in range(groups)])  1.39 us
    pallas_call x1, Pallas kernels, update(): pl.pallas_call(update_kernel, out_shape=(whole, pltpu.VMEM((tilts * left,...  0.98 us
    pallas_call x1, Pallas kernels, on_device(): pl.pallas_call(log_kernel, out_shape=jax.ShapeDtypeStruct((count, tilts,...  0.72 us
  transfers between devices with their start and end apart: 6, of which 6 were waited for; matrix products, arithmetic and copies ran while one was open for 0% of the time, Pallas kernels for 20%

profile of v3, /device:TPU:0, one launch (start us, length us, event | category | flops | bytes accessed | tf_op | source)
XLA Modules:
  0.0 26.8 jit_solution(12387546976971379135)
XLA Ops:
  0.6 0.0 copy-start
  0.6 3.9 %expect.1 = (f32[16,64,512]{2,1,0:T(8,128)S(1)}, f32[32,512]{1,0:T(8,128)S(1)}, f32[1,128]{1,0:T(1,128)S(1)}) custom-call(s32[16,128,512]{2,1,0:T(8,128)} %frames.3, f32[2,128,512]{2,1,0:T(8,128)} %slices.3, bf16[4,256,256]{2,1,0:T(8,128)(2,1)} %constant.4.clone.table), custom_call_target="tpu_custom_call" | custom-call | tf_op jit(solution)/shard_map/expect/pallas_call | solution.py:274
  4.6 0.5 %collective-permute-start = (f32[1,128]{1,0:T(1,128)S(1)}, f32[1,128]{1,0:T(1,128)S(1)}, u32[]{:S(2)}, u32[]{:S(2)}) collective-permute-start(f32[1,128]{1,0:T(1,128)S(1)} %get-tuple-element.9.local), channel_id=1, source_target_pairs={{0,1},{1,0},{2,3},{3,2},{4,5},{5,4},{6,7},{7,6},{8,9},{9,8},{10,11... | collective-permute-start | bytes 1544 | tf_op jit(solution)/shard_map/ppermute | solution.py:520
  5.1 0.8 %collective-permute-done = f32[1,128]{1,0:T(1,128)S(1)} collective-permute-done((f32[1,128]{1,0:T(1,128)S(1)}, f32[1,128]{1,0:T(1,128)S(1)}, u32[]{:S(2)}, u32[]{:S(2)}) %collective-permute-start) | collective-permute-done | bytes 544 | tf_op jit(solution)/shard_map/ppermute | solution.py:520
  5.9 2.6 %collective-permute-start.1 = (f32[1,128]{1,0:T(1,128)S(1)}, f32[1,128]{1,0:T(1,128)S(1)}, u32[]{:S(2)}, u32[]{:S(2)}) collective-permute-start(f32[1,128]{1,0:T(1,128)S(1)} %log_add_fusion.3), channel_id=1, source_target_pairs={{0,3},{1,2},{2,1},{3,0},{4,7},{5,6},{6,5},{7,4},{8,11},{9,10},{10,... | collective-permute-start | bytes 1544 | tf_op jit(solution)/shard_map/ppermute | solution.py:520
  8.6 1.3 %collective-permute-done.1 = f32[1,128]{1,0:T(1,128)S(1)} collective-permute-done((f32[1,128]{1,0:T(1,128)S(1)}, f32[1,128]{1,0:T(1,128)S(1)}, u32[]{:S(2)}, u32[]{:S(2)}) %collective-permute-start.1) | collective-permute-done | bytes 544 | tf_op jit(solution)/shard_map/ppermute | solution.py:520
  9.9 1.8 %collective-permute-start.2 = (f32[1,128]{1,0:T(1,128)S(1)}, f32[1,128]{1,0:T(1,128)S(1)}, u32[]{:S(2)}, u32[]{:S(2)}) collective-permute-start(f32[1,128]{1,0:T(1,128)S(1)} %log_add_fusion.2), channel_id=1, source_target_pairs={{0,5},{1,4},{2,7},{3,6},{4,1},{5,0},{6,3},{7,2},{8,13},{9,12},{10,... | collective-permute-start | bytes 1544 | tf_op jit(solution)/shard_map/ppermute | solution.py:520
  11.7 1.3 %collective-permute-done.2 = f32[1,128]{1,0:T(1,128)S(1)} collective-permute-done((f32[1,128]{1,0:T(1,128)S(1)}, f32[1,128]{1,0:T(1,128)S(1)}, u32[]{:S(2)}, u32[]{:S(2)}) %collective-permute-start.2) | collective-permute-done | bytes 544 | tf_op jit(solution)/shard_map/ppermute | solution.py:520
  13.0 2.8 %collective-permute-start.3 = (f32[1,128]{1,0:T(1,128)S(1)}, f32[1,128]{1,0:T(1,128)S(1)}, u32[]{:S(2)}, u32[]{:S(2)}) collective-permute-start(f32[1,128]{1,0:T(1,128)S(1)} %log_add_fusion.1), channel_id=1, source_target_pairs={{0,9},{1,8},{2,11},{3,10},{4,13},{5,12},{6,15},{7,14},{8,1},{9,0},... | collective-permute-start | bytes 1544 | tf_op jit(solution)/shard_map/ppermute | solution.py:520
  15.7 0.0 copy-done
  15.7 0.2 transform.1.forms
  16.0 1.1 %collective-permute-done.3 = f32[1,128]{1,0:T(1,128)S(1)} collective-permute-done((f32[1,128]{1,0:T(1,128)S(1)}, f32[1,128]{1,0:T(1,128)S(1)}, u32[]{:S(2)}, u32[]{:S(2)}) %collective-permute-start.3) | collective-permute-done | bytes 544 | tf_op jit(solution)/shard_map/ppermute | solution.py:520
  17.0 0.4 %back.1 = f32[264,128]{1,0:T(8,128)S(1)} custom-call(f32[16,64,512]{2,1,0:T(8,128)S(1)} %get-tuple-element.10.spec, f32[3,32,256]{2,1,0:T(8,128)S(1)} %transform.1.forms, f32[1,128]{1,0:T(1,128)S(1)} %get-tuple-element.9.local, f32[1,128]{1,0:T(1,128)S(1)} %log_add_fusion.lse), custom_call_target="tpu_custom_call" | custom-call | flops 268435456 | bytes 1048576 | tf_op jit(solution)/shard_map/back/pallas_call | solution.py:405
  17.4 0.0 copy-start.1
  17.4 1.8 %collective-permute-start.4 = (f32[264,128]{1,0:T(8,128)S(1)}, f32[264,128]{1,0:T(8,128)S(1)}, u32[]{:S(2)}, u32[]{:S(2)}) collective-permute-start(f32[264,128]{1,0:T(8,128)S(1)} %back.1), channel_id=1, source_target_pairs={{0,16},{16,0},{1,17},{17,1},{2,18},{18,2},{3,19},{19,3},{4,20},{20... | collective-permute-start | bytes 405512 | tf_op jit(solution)/shard_map/ppermute | solution.py:554
  19.2 0.6 %back_signal.1 = f32[64,512]{1,0:T(8,128)S(1)} custom-call(f32[16,64,512]{2,1,0:T(8,128)S(1)} %get-tuple-element.10.spec, f32[3,32,256]{2,1,0:T(8,128)S(1)} %transform.1.forms, f32[1,128]{1,0:T(1,128)S(1)} %get-tuple-element.9.local, f32[1,128]{1,0:T(1,128)S(1)} %log_add_fusion.lse, bf16[4,256,256]{2,1,0:T(8,128)(2,1)S(1)} %copy-done), custom_call_target="tpu_custom_call" | custom-call | flops 268435456 | bytes 1048576 | tf_op jit(solution)/shard_map/back_signal/pallas_call | solution.py:406
  19.9 0.4 %collective-permute-start.5 = (f32[64,512]{1,0:T(8,128)S(1)}, f32[64,512]{1,0:T(8,128)S(1)}, u32[]{:S(2)}, u32[]{:S(2)}) collective-permute-start(f32[64,512]{1,0:T(8,128)S(1)} %back_signal.1), channel_id=1, source_target_pairs={{0,16},{16,0},{1,17},{17,1},{2,18},{18,2},{3,19},{19,3},{4,20},{20... | collective-permute-start | bytes 393224 | tf_op jit(solution)/shard_map/ppermute | solution.py:554
  20.2 2.7 %back_own.1.own = f32[520,128]{1,0:T(8,128)S(1)} custom-call(f32[3,32,256]{2,1,0:T(8,128)S(1)} %transform.1.forms, f32[1,128]{1,0:T(1,128)S(1)} %get-tuple-element.9.local, f32[1,128]{1,0:T(1,128)S(1)} %log_add_fusion.lse, s32[16,128,512]{2,1,0:T(8,128)} %frames.3, bf16[4,256,256]{2,1,0:T(8,128)(2,1)S(1)} %copy-done), custom_call_target="tpu_custom_call" | custom-call | tf_op jit(solution)/shard_map/back_own/pallas_call | solution.py:413
  23.0 0.9 %collective-permute-done.4.after.other = f32[264,128]{1,0:T(8,128)S(1)} collective-permute-done((f32[264,128]{1,0:T(8,128)S(1)}, f32[264,128]{1,0:T(8,128)S(1)}, u32[]{:S(2)}, u32[]{:S(2)}) %collective-permute-start.4) | collective-permute-done | bytes 135200 | tf_op jit(solution)/shard_map/ppermute | solution.py:554
  23.9 0.7 %log_resp.1 = f32[16,2,512]{2,1,0:T(2,128)} custom-call(f32[32,512]{1,0:T(8,128)S(1)} %get-tuple-element.8.scores, f32[1,128]{1,0:T(1,128)S(1)} %log_add_fusion.lse, f32[264,128]{1,0:T(8,128)S(1)} %collective-permute-done.4.after.other), custom_call_target="tpu_custom_call" | custom-call | tf_op jit(solution)/shard_map/log_resp/pallas_call | solution.py:558
  24.6 0.0 copy-done.1
  24.6 1.0 %update.1 = (f32[2,64,512]{2,1,0:T(8,128)}, f32[64,512]{1,0:T(8,128)S(1)}, f32[64,128]{1,0:T(8,128)S(1)}) custom-call(f32[520,128]{1,0:T(8,128)S(1)} %back_own.1.own, f32[264,128]{1,0:T(8,128)S(1)} %collective-permute-done.4.after.other, f32[2,128,512]{2,1,0:T(8,128)S(1)} %copy-done.1, bf16[4,256,256]{2,1,0:T(8,128)(2,1)S(1)} %copy-done), custom_call_target="tpu_custom_call" | custom-call | tf_op jit(solution)/shard_map/update/pallas_call | solution.py:488
  25.6 0.5 %collective-permute-done.5.other = f32[64,512]{1,0:T(8,128)S(1)} collective-permute-done((f32[64,512]{1,0:T(8,128)S(1)}, f32[64,512]{1,0:T(8,128)S(1)}, u32[]{:S(2)}, u32[]{:S(2)}) %collective-permute-start.5) | collective-permute-done | bytes 131104 | tf_op jit(solution)/shard_map/ppermute | solution.py:554
  26.1 0.7 %finish.1 = f32[2,64,512]{2,1,0:T(8,128)} custom-call(f32[64,512]{1,0:T(8,128)S(1)} %collective-permute-done.5.other, f32[64,512]{1,0:T(8,128)S(1)} %get-tuple-element.11.rest, f32[64,128]{1,0:T(8,128)S(1)} %get-tuple-element.12.factor, f32[2,64,512]{2,1,0:T(8,128)} %get-tuple-element.13.earlier), custom_call_target="tpu_custom_call", output_to_operand_aliasing={{}: (3, {})} | custom-call | tf_op jit(solution)/shard_map/finish/pallas_call | solution.py:497
  (4 shorter events, 0.0 us)
Async XLA Ops:
  0.6 15.1 %copy-start = (bf16[4,256,256]{2,1,0:T(8,128)(2,1)S(1)}, bf16[4,256,256]{2,1,0:T(8,128)(2,1)}, u32[]{:S(2)}) copy-start(bf16[4,256,256]{2,1,0:T(8,128)(2,1)} %constant.4.clone.table) | copy-start | bytes 1572868
  4.6 1.3 %collective-permute-start = (f32[1,128]{1,0:T(1,128)S(1)}, f32[1,128]{1,0:T(1,128)S(1)}, u32[]{:S(2)}, u32[]{:S(2)}) collective-permute-start(f32[1,128]{1,0:T(1,128)S(1)} %get-tuple-element.9.local), channel_id=1, source_target_pairs={{0,1},{1,0},{2,3},{3,2},{4,5},{5,4},{6,7},{7,6},{8,9},{9,8},{10,11... | collective-permute-start | bytes 1544 | tf_op jit(solution)/shard_map/ppermute | solution.py:520
  5.9 3.9 %collective-permute-start.1 = (f32[1,128]{1,0:T(1,128)S(1)}, f32[1,128]{1,0:T(1,128)S(1)}, u32[]{:S(2)}, u32[]{:S(2)}) collective-permute-start(f32[1,128]{1,0:T(1,128)S(1)} %log_add_fusion.3), channel_id=1, source_target_pairs={{0,3},{1,2},{2,1},{3,0},{4,7},{5,6},{6,5},{7,4},{8,11},{9,10},{10,... | collective-permute-start | bytes 1544 | tf_op jit(solution)/shard_map/ppermute | solution.py:520
  9.9 3.1 %collective-permute-start.2 = (f32[1,128]{1,0:T(1,128)S(1)}, f32[1,128]{1,0:T(1,128)S(1)}, u32[]{:S(2)}, u32[]{:S(2)}) collective-permute-start(f32[1,128]{1,0:T(1,128)S(1)} %log_add_fusion.2), channel_id=1, source_target_pairs={{0,5},{1,4},{2,7},{3,6},{4,1},{5,0},{6,3},{7,2},{8,13},{9,12},{10,... | collective-permute-start | bytes 1544 | tf_op jit(solution)/shard_map/ppermute | solution.py:520
  13.0 4.0 %collective-permute-start.3 = (f32[1,128]{1,0:T(1,128)S(1)}, f32[1,128]{1,0:T(1,128)S(1)}, u32[]{:S(2)}, u32[]{:S(2)}) collective-permute-start(f32[1,128]{1,0:T(1,128)S(1)} %log_add_fusion.1), channel_id=1, source_target_pairs={{0,9},{1,8},{2,11},{3,10},{4,13},{5,12},{6,15},{7,14},{8,1},{9,0},... | collective-permute-start | bytes 1544 | tf_op jit(solution)/shard_map/ppermute | solution.py:520
  17.4 7.2 %copy-start.1 = (f32[2,128,512]{2,1,0:T(8,128)S(1)}, f32[2,128,512]{2,1,0:T(8,128)}, u32[]{:S(2)}) copy-start(f32[2,128,512]{2,1,0:T(8,128)} %slices.3) | copy-start | bytes 1572868
  17.4 6.5 %collective-permute-start.4 = (f32[264,128]{1,0:T(8,128)S(1)}, f32[264,128]{1,0:T(8,128)S(1)}, u32[]{:S(2)}, u32[]{:S(2)}) collective-permute-start(f32[264,128]{1,0:T(8,128)S(1)} %back.1), channel_id=1, source_target_pairs={{0,16},{16,0},{1,17},{17,1},{2,18},{18,2},{3,19},{19,3},{4,20},{20... | collective-permute-start | bytes 405512 | tf_op jit(solution)/shard_map/ppermute | solution.py:554
  19.9 6.2 %collective-permute-start.5 = (f32[64,512]{1,0:T(8,128)S(1)}, f32[64,512]{1,0:T(8,128)S(1)}, u32[]{:S(2)}, u32[]{:S(2)}) collective-permute-start(f32[64,512]{1,0:T(8,128)S(1)} %back_signal.1), channel_id=1, source_target_pairs={{0,16},{16,0},{1,17},{17,1},{2,18},{18,2},{3,19},{19,3},{4,20},{20... | collective-permute-start | bytes 393224 | tf_op jit(solution)/shard_map/ppermute | solution.py:554

commit v4 on v3

--- a/solution.py
+++ b/solution.py
@@ -506,19 +506,21 @@
     )(others[1], rest, factor, new)
 
 
-def log_sum(a, b):
-    return jnp.maximum(a, b) + jnp.log(1.0 + jnp.exp(-jnp.abs(a - b)))
+def log_sum(values):
+    top = functools.reduce(jnp.maximum, values)
+    return top + jnp.log(sum(jnp.exp(value - top) for value in values))
 
 
 def over_axis(value, axis):
     size = lax.axis_size(axis)
     if size & (size - 1):
         return jax.nn.logsumexp(lax.all_gather(value, axis), axis=0)
-    bit = 1
-    while bit < size:
-        step = bit | 1
-        value = log_sum(value, lax.ppermute(value, axis, [(i, i ^ step) for i in range(size)]))
-        bit *= 2
+    bits = [1 << i for i in range(size.bit_length() - 1)]
+    rounds = [[bit] for bit in bits[:1]] + [bits[i : i + 2] for i in range(1, len(bits), 2)]
+    for bits in rounds:
+        steps = [step | 1 for step in ([*bits, sum(bits)] if len(bits) == 2 else bits)]
+        parts = [lax.ppermute(value, axis, [(i, i ^ step) for i in range(size)]) for step in steps]
+        value = log_sum([value, *parts])
     return value
 
 

time: 26.9 us -> 26.7 us (level)
  starting transfers between devices: 9.86 us -> 9.36 us
  waiting for transfers between devices: 5.85 us -> 6.14 us
    ppermute x4 -> x5, starting transfers between devices: 7.71 us -> 7.21 us  [over_axis(): lax.ppermute(value, axis, [(i, i ^ step) for i in range(size)])]
    ppermute x4 -> x5, waiting for transfers between devices: 4.46 us -> 4.83 us  [over_axis(): lax.ppermute(value, axis, [(i, i ^ step) for i in range(size)])]
  transfers between devices with their start and end apart: 6 -> 7, of which waited for: 6 -> 7; matrix products, arithmetic and copies ran while one was open for 0% -> 0% of each run, Pallas kernels for 20% -> 20%
where the time goes in v4:
time: 26.7 us; the launch traced here: 26.6 us
  Pallas kernels  10.3 us (39%)
  starting transfers between devices  9.36 us (35%)
  waiting for transfers between devices  6.14 us (23%)
  between operations  0.69 us (3%)
    ppermute x5, starting transfers between devices, over_axis(): lax.ppermute(value, axis, [(i, i ^ step) for i in range(size)])  7.21 us
    ppermute x5, waiting for transfers between devices, over_axis(): lax.ppermute(value, axis, [(i, i ^ step) for i in range(size)])  4.83 us
    pallas_call x1, Pallas kernels, expect(): pl.pallas_call(functools.partial(expect_kernel, anneal, chunk, groups), o...  3.93 us
    pallas_call x1, Pallas kernels, back(): call(back_own_kernel, in_specs=[vm] * 3 + [pl.BlockSpec(memory_space=pltp...  2.73 us
    ppermute x2, starting transfers between devices, on_device(): lax.ppermute(block, 'dp', [(i, (i + step) % groups) for i in range(groups)])  2.16 us
    ppermute x2, waiting for transfers between devices, on_device(): lax.ppermute(block, 'dp', [(i, (i + step) % groups) for i in range(groups)])  1.31 us
    pallas_call x1, Pallas kernels, update(): pl.pallas_call(update_kernel, out_shape=(whole, pltpu.VMEM((tilts * left,...  0.98 us
    pallas_call x1, Pallas kernels, on_device(): pl.pallas_call(log_kernel, out_shape=jax.ShapeDtypeStruct((count, tilts,...  0.72 us
  transfers between devices with their start and end apart: 7, of which 7 were waited for; matrix products, arithmetic and copies ran while one was open for 0% of the time, Pallas kernels for 20%

profile of v4, /device:TPU:0, one launch (start us, length us, event | category | flops | bytes accessed | tf_op | source)
XLA Modules:
  0.0 26.6 jit_solution(14236638899182958351)
XLA Ops:
  0.6 0.0 copy-start
  0.6 3.9 %expect.1 = (f32[16,64,512]{2,1,0:T(8,128)S(1)}, f32[32,512]{1,0:T(8,128)S(1)}, f32[1,128]{1,0:T(1,128)S(1)}) custom-call(s32[16,128,512]{2,1,0:T(8,128)} %frames.3, f32[2,128,512]{2,1,0:T(8,128)} %slices.3, bf16[4,256,256]{2,1,0:T(8,128)(2,1)} %constant.2.clone.table), custom_call_target="tpu_custom_call" | custom-call | tf_op jit(solution)/shard_map/expect/pallas_call | solution.py:274
  4.6 0.5 %collective-permute-start = (f32[1,128]{1,0:T(1,128)S(1)}, f32[1,128]{1,0:T(1,128)S(1)}, u32[]{:S(2)}, u32[]{:S(2)}) collective-permute-start(f32[1,128]{1,0:T(1,128)S(1)} %get-tuple-element.9.local), channel_id=1, source_target_pairs={{0,1},{1,0},{2,3},{3,2},{4,5},{5,4},{6,7},{7,6},{8,9},{9,8},{10,11... | collective-permute-start | bytes 1544 | tf_op jit(solution)/shard_map/ppermute | solution.py:522
  5.1 0.8 %collective-permute-done = f32[1,128]{1,0:T(1,128)S(1)} collective-permute-done((f32[1,128]{1,0:T(1,128)S(1)}, f32[1,128]{1,0:T(1,128)S(1)}, u32[]{:S(2)}, u32[]{:S(2)}) %collective-permute-start) | collective-permute-done | bytes 544 | tf_op jit(solution)/shard_map/ppermute | solution.py:522
  5.9 3.7 %collective-permute-start.3 = (f32[1,128]{1,0:T(1,128)S(1)}, f32[1,128]{1,0:T(1,128)S(1)}, u32[]{:S(2)}, u32[]{:S(2)}) collective-permute-start(f32[1,128]{1,0:T(1,128)S(1)} %log_add_fusion.2), channel_id=1, source_target_pairs={{0,7},{1,6},{2,5},{3,4},{4,3},{5,2},{6,1},{7,0},{8,15},{9,14},{10,... | collective-permute-start | bytes 1544 | tf_op jit(solution)/shard_map/ppermute | solution.py:522
  9.6 0.4 %collective-permute-start.2 = (f32[1,128]{1,0:T(1,128)S(1)}, f32[1,128]{1,0:T(1,128)S(1)}, u32[]{:S(2)}, u32[]{:S(2)}) collective-permute-start(f32[1,128]{1,0:T(1,128)S(1)} %log_add_fusion.2), channel_id=1, source_target_pairs={{0,5},{1,4},{2,7},{3,6},{4,1},{5,0},{6,3},{7,2},{8,13},{9,12},{10,... | collective-permute-start | bytes 1544 | tf_op jit(solution)/shard_map/ppermute | solution.py:522
  10.0 0.2 collective-permute-start.1
  10.2 0.7 %collective-permute-done.3 = f32[1,128]{1,0:T(1,128)S(1)} collective-permute-done((f32[1,128]{1,0:T(1,128)S(1)}, f32[1,128]{1,0:T(1,128)S(1)}, u32[]{:S(2)}, u32[]{:S(2)}) %collective-permute-start.3) | collective-permute-done | bytes 544 | tf_op jit(solution)/shard_map/ppermute | solution.py:522
  10.9 1.7 %collective-permute-done.2 = f32[1,128]{1,0:T(1,128)S(1)} collective-permute-done((f32[1,128]{1,0:T(1,128)S(1)}, f32[1,128]{1,0:T(1,128)S(1)}, u32[]{:S(2)}, u32[]{:S(2)}) %collective-permute-start.2) | collective-permute-done | bytes 544 | tf_op jit(solution)/shard_map/ppermute | solution.py:522
  12.6 0.4 %collective-permute-done.1 = f32[1,128]{1,0:T(1,128)S(1)} collective-permute-done((f32[1,128]{1,0:T(1,128)S(1)}, f32[1,128]{1,0:T(1,128)S(1)}, u32[]{:S(2)}, u32[]{:S(2)}) %collective-permute-start.1) | collective-permute-done | bytes 544 | tf_op jit(solution)/shard_map/ppermute | solution.py:522
  13.0 2.5 %collective-permute-start.4 = (f32[1,128]{1,0:T(1,128)S(1)}, f32[1,128]{1,0:T(1,128)S(1)}, u32[]{:S(2)}, u32[]{:S(2)}) collective-permute-start(f32[1,128]{1,0:T(1,128)S(1)} %log_add_fusion.1), channel_id=1, source_target_pairs={{0,9},{1,8},{2,11},{3,10},{4,13},{5,12},{6,15},{7,14},{8,1},{9,0},... | collective-permute-start | bytes 1544 | tf_op jit(solution)/shard_map/ppermute | solution.py:522
  15.4 0.0 copy-done
  15.4 0.2 transform.1.forms
  15.7 1.2 %collective-permute-done.4 = f32[1,128]{1,0:T(1,128)S(1)} collective-permute-done((f32[1,128]{1,0:T(1,128)S(1)}, f32[1,128]{1,0:T(1,128)S(1)}, u32[]{:S(2)}, u32[]{:S(2)}) %collective-permute-start.4) | collective-permute-done | bytes 544 | tf_op jit(solution)/shard_map/ppermute | solution.py:522
  16.9 0.4 %back.1 = f32[264,128]{1,0:T(8,128)S(1)} custom-call(f32[16,64,512]{2,1,0:T(8,128)S(1)} %get-tuple-element.10.spec, f32[3,32,256]{2,1,0:T(8,128)S(1)} %transform.1.forms, f32[1,128]{1,0:T(1,128)S(1)} %get-tuple-element.9.local, f32[1,128]{1,0:T(1,128)S(1)} %log_add_fusion.lse), custom_call_target="tpu_custom_call" | custom-call | flops 268435456 | bytes 1048576 | tf_op jit(solution)/shard_map/back/pallas_call | solution.py:405
  17.3 0.0 copy-start.1
  17.3 1.6 %collective-permute-start.5 = (f32[264,128]{1,0:T(8,128)S(1)}, f32[264,128]{1,0:T(8,128)S(1)}, u32[]{:S(2)}, u32[]{:S(2)}) collective-permute-start(f32[264,128]{1,0:T(8,128)S(1)} %back.1), channel_id=1, source_target_pairs={{0,16},{16,0},{1,17},{17,1},{2,18},{18,2},{3,19},{19,3},{4,20},{20... | collective-permute-start | bytes 405512 | tf_op jit(solution)/shard_map/ppermute | solution.py:556
  18.9 0.6 %back_signal.1 = f32[64,512]{1,0:T(8,128)S(1)} custom-call(f32[16,64,512]{2,1,0:T(8,128)S(1)} %get-tuple-element.10.spec, f32[3,32,256]{2,1,0:T(8,128)S(1)} %transform.1.forms, f32[1,128]{1,0:T(1,128)S(1)} %get-tuple-element.9.local, f32[1,128]{1,0:T(1,128)S(1)} %log_add_fusion.lse, bf16[4,256,256]{2,1,0:T(8,128)(2,1)S(1)} %copy-done), custom_call_target="tpu_custom_call" | custom-call | flops 268435456 | bytes 1048576 | tf_op jit(solution)/shard_map/back_signal/pallas_call | solution.py:406
  19.5 0.6 %collective-permute-start.6 = (f32[64,512]{1,0:T(8,128)S(1)}, f32[64,512]{1,0:T(8,128)S(1)}, u32[]{:S(2)}, u32[]{:S(2)}) collective-permute-start(f32[64,512]{1,0:T(8,128)S(1)} %back_signal.1), channel_id=1, source_target_pairs={{0,16},{16,0},{1,17},{17,1},{2,18},{18,2},{3,19},{19,3},{4,20},{20... | collective-permute-start | bytes 393224 | tf_op jit(solution)/shard_map/ppermute | solution.py:556
  20.1 2.7 %back_own.1.own = f32[520,128]{1,0:T(8,128)S(1)} custom-call(f32[3,32,256]{2,1,0:T(8,128)S(1)} %transform.1.forms, f32[1,128]{1,0:T(1,128)S(1)} %get-tuple-element.9.local, f32[1,128]{1,0:T(1,128)S(1)} %log_add_fusion.lse, s32[16,128,512]{2,1,0:T(8,128)} %frames.3, bf16[4,256,256]{2,1,0:T(8,128)(2,1)S(1)} %copy-done), custom_call_target="tpu_custom_call" | custom-call | tf_op jit(solution)/shard_map/back_own/pallas_call | solution.py:413
  22.8 0.9 %collective-permute-done.5.after.other = f32[264,128]{1,0:T(8,128)S(1)} collective-permute-done((f32[264,128]{1,0:T(8,128)S(1)}, f32[264,128]{1,0:T(8,128)S(1)}, u32[]{:S(2)}, u32[]{:S(2)}) %collective-permute-start.5) | collective-permute-done | bytes 135200 | tf_op jit(solution)/shard_map/ppermute | solution.py:556
  23.8 0.7 %log_resp.1 = f32[16,2,512]{2,1,0:T(2,128)} custom-call(f32[32,512]{1,0:T(8,128)S(1)} %get-tuple-element.8.scores, f32[1,128]{1,0:T(1,128)S(1)} %log_add_fusion.lse, f32[264,128]{1,0:T(8,128)S(1)} %collective-permute-done.5.after.other), custom_call_target="tpu_custom_call" | custom-call | tf_op jit(solution)/shard_map/log_resp/pallas_call | solution.py:560
  24.5 0.0 copy-done.1
  24.5 1.0 %update.1 = (f32[2,64,512]{2,1,0:T(8,128)}, f32[64,512]{1,0:T(8,128)S(1)}, f32[64,128]{1,0:T(8,128)S(1)}) custom-call(f32[520,128]{1,0:T(8,128)S(1)} %back_own.1.own, f32[264,128]{1,0:T(8,128)S(1)} %collective-permute-done.5.after.other, f32[2,128,512]{2,1,0:T(8,128)S(1)} %copy-done.1, bf16[4,256,256]{2,1,0:T(8,128)(2,1)S(1)} %copy-done), custom_call_target="tpu_custom_call" | custom-call | tf_op jit(solution)/shard_map/update/pallas_call | solution.py:488
  25.5 0.4 %collective-permute-done.6.other = f32[64,512]{1,0:T(8,128)S(1)} collective-permute-done((f32[64,512]{1,0:T(8,128)S(1)}, f32[64,512]{1,0:T(8,128)S(1)}, u32[]{:S(2)}, u32[]{:S(2)}) %collective-permute-start.6) | collective-permute-done | bytes 131104 | tf_op jit(solution)/shard_map/ppermute | solution.py:556
  25.9 0.7 %finish.1 = f32[2,64,512]{2,1,0:T(8,128)} custom-call(f32[64,512]{1,0:T(8,128)S(1)} %collective-permute-done.6.other, f32[64,512]{1,0:T(8,128)S(1)} %get-tuple-element.11.rest, f32[64,128]{1,0:T(8,128)S(1)} %get-tuple-element.12.factor, f32[2,64,512]{2,1,0:T(8,128)} %get-tuple-element.13.earlier), custom_call_target="tpu_custom_call", output_to_operand_aliasing={{}: (3, {})} | custom-call | tf_op jit(solution)/shard_map/finish/pallas_call | solution.py:497
  (3 shorter events, 0.0 us)
Async XLA Ops:
  0.6 14.8 %copy-start = (bf16[4,256,256]{2,1,0:T(8,128)(2,1)S(1)}, bf16[4,256,256]{2,1,0:T(8,128)(2,1)}, u32[]{:S(2)}) copy-start(bf16[4,256,256]{2,1,0:T(8,128)(2,1)} %constant.2.clone.table) | copy-start | bytes 1572868
  4.6 1.3 %collective-permute-start = (f32[1,128]{1,0:T(1,128)S(1)}, f32[1,128]{1,0:T(1,128)S(1)}, u32[]{:S(2)}, u32[]{:S(2)}) collective-permute-start(f32[1,128]{1,0:T(1,128)S(1)} %get-tuple-element.9.local), channel_id=1, source_target_pairs={{0,1},{1,0},{2,3},{3,2},{4,5},{5,4},{6,7},{7,6},{8,9},{9,8},{10,11... | collective-permute-start | bytes 1544 | tf_op jit(solution)/shard_map/ppermute | solution.py:522
  5.9 5.0 %collective-permute-start.3 = (f32[1,128]{1,0:T(1,128)S(1)}, f32[1,128]{1,0:T(1,128)S(1)}, u32[]{:S(2)}, u32[]{:S(2)}) collective-permute-start(f32[1,128]{1,0:T(1,128)S(1)} %log_add_fusion.2), channel_id=1, source_target_pairs={{0,7},{1,6},{2,5},{3,4},{4,3},{5,2},{6,1},{7,0},{8,15},{9,14},{10,... | collective-permute-start | bytes 1544 | tf_op jit(solution)/shard_map/ppermute | solution.py:522
  9.6 3.0 %collective-permute-start.2 = (f32[1,128]{1,0:T(1,128)S(1)}, f32[1,128]{1,0:T(1,128)S(1)}, u32[]{:S(2)}, u32[]{:S(2)}) collective-permute-start(f32[1,128]{1,0:T(1,128)S(1)} %log_add_fusion.2), channel_id=1, source_target_pairs={{0,5},{1,4},{2,7},{3,6},{4,1},{5,0},{6,3},{7,2},{8,13},{9,12},{10,... | collective-permute-start | bytes 1544 | tf_op jit(solution)/shard_map/ppermute | solution.py:522
  10.0 3.0 %collective-permute-start.1 = (f32[1,128]{1,0:T(1,128)S(1)}, f32[1,128]{1,0:T(1,128)S(1)}, u32[]{:S(2)}, u32[]{:S(2)}) collective-permute-start(f32[1,128]{1,0:T(1,128)S(1)} %log_add_fusion.2), channel_id=1, source_target_pairs={{0,3},{1,2},{2,1},{3,0},{4,7},{5,6},{6,5},{7,4},{8,11},{9,10},{10,... | collective-permute-start | bytes 1544 | tf_op jit(solution)/shard_map/ppermute | solution.py:522
  13.0 3.9 %collective-permute-start.4 = (f32[1,128]{1,0:T(1,128)S(1)}, f32[1,128]{1,0:T(1,128)S(1)}, u32[]{:S(2)}, u32[]{:S(2)}) collective-permute-start(f32[1,128]{1,0:T(1,128)S(1)} %log_add_fusion.1), channel_id=1, source_target_pairs={{0,9},{1,8},{2,11},{3,10},{4,13},{5,12},{6,15},{7,14},{8,1},{9,0},... | collective-permute-start | bytes 1544 | tf_op jit(solution)/shard_map/ppermute | solution.py:522
  17.3 7.2 %copy-start.1 = (f32[2,128,512]{2,1,0:T(8,128)S(1)}, f32[2,128,512]{2,1,0:T(8,128)}, u32[]{:S(2)}) copy-start(f32[2,128,512]{2,1,0:T(8,128)} %slices.3) | copy-start | bytes 1572868
  17.3 6.5 %collective-permute-start.5 = (f32[264,128]{1,0:T(8,128)S(1)}, f32[264,128]{1,0:T(8,128)S(1)}, u32[]{:S(2)}, u32[]{:S(2)}) collective-permute-start(f32[264,128]{1,0:T(8,128)S(1)} %back.1), channel_id=1, source_target_pairs={{0,16},{16,0},{1,17},{17,1},{2,18},{18,2},{3,19},{19,3},{4,20},{20... | collective-permute-start | bytes 405512 | tf_op jit(solution)/shard_map/ppermute | solution.py:556
  19.5 6.3 %collective-permute-start.6 = (f32[64,512]{1,0:T(8,128)S(1)}, f32[64,512]{1,0:T(8,128)S(1)}, u32[]{:S(2)}, u32[]{:S(2)}) collective-permute-start(f32[64,512]{1,0:T(8,128)S(1)} %back_signal.1), channel_id=1, source_target_pairs={{0,16},{16,0},{1,17},{17,1},{2,18},{18,2},{3,19},{19,3},{4,20},{20... | collective-permute-start | bytes 393224 | tf_op jit(solution)/shard_map/ppermute | solution.py:556

commit v5 on v4

--- a/solution.py
+++ b/solution.py
@@ -151,7 +151,7 @@
     share = shells // groups
     rows = tilts * shells
     other, refs = refs[: groups - 1], refs[groups - 1 :]
-    scores, local, own, fbuf, sbuf, tv, ya, yb, yc, cross, sems = refs
+    scores, local, tv, own, fbuf, sbuf, ya, yb, yc, cross, sems = refs
     spec = (own, *other)
     bases = [own_shells(s, share) for s in range(groups)]
 
@@ -271,20 +271,20 @@
     hbm = pl.BlockSpec(memory_space=pltpu.HBM)
     vm = pl.BlockSpec(memory_space=pltpu.VMEM)
     form = pltpu.VMEM((tilts * shells, half), F32)
-    *other, scores, local = pl.pallas_call(
+    *other, scores, local, table = pl.pallas_call(
         functools.partial(expect_kernel, anneal, chunk, groups),
         out_shape=(
             *[pltpu.VMEM((count, share, angles), F32)] * (groups - 1),
             pltpu.VMEM((tilts * count, angles), F32),
             pltpu.VMEM((1, LANES), F32),
+            pltpu.VMEM(table.shape, BF),
         ),
         in_specs=[hbm] * 3,
-        out_specs=(*[vm] * (groups - 1), vm, vm),
+        out_specs=(*[vm] * (groups - 1), vm, vm, vm),
         scratch_shapes=[
             pltpu.VMEM((count, share, angles), F32),
             pltpu.VMEM((count, shells, angles), jnp.int32),
             pltpu.VMEM((tilts, shells, angles), F32),
-            pltpu.VMEM(table.shape, BF),
             form,
             form,
             form,
@@ -294,7 +294,7 @@
         compiler_params=pltpu.CompilerParams(vmem_limit_bytes=VMEM_BYTES),
         name="expect",
     )(*(in_hbm(x) for x in (frames, slices, table)))
-    return other, scores, local
+    return other, scores, local, table
 
 
 def weights_kernel(tilts, scores, local, table, forms):
@@ -534,7 +534,7 @@
     vm = pl.BlockSpec(memory_space=pltpu.VMEM)
     params = pltpu.CompilerParams(vmem_limit_bytes=VMEM_BYTES)
 
-    spec, scores, local = expect(frames, slices, table, anneal, groups)
+    spec, scores, local, table = expect(frames, slices, table, anneal, groups)
     forms = pl.pallas_call(
         functools.partial(weights_kernel, tilts),
         out_shape=pltpu.VMEM((3, tilts * count, angles // 2), F32),

time: 26.7 us -> 26.7 us (level)
  no operation moved by 1% of the time
where the time goes in v5:
time: 26.7 us; the launch traced here: 26.5 us
  Pallas kernels  10.3 us (39%)
  starting transfers between devices  9.37 us (35%)
  waiting for transfers between devices  6.13 us (23%)
  between operations  0.69 us (3%)
    ppermute x5, starting transfers between devices, over_axis(): lax.ppermute(value, axis, [(i, i ^ step) for i in range(size)])  7.21 us
    ppermute x5, waiting for transfers between devices, over_axis(): lax.ppermute(value, axis, [(i, i ^ step) for i in range(size)])  4.81 us
    pallas_call x1, Pallas kernels, expect(): pl.pallas_call(functools.partial(expect_kernel, anneal, chunk, groups), o...  3.92 us
    pallas_call x1, Pallas kernels, back(): call(back_own_kernel, in_specs=[vm] * 3 + [pl.BlockSpec(memory_space=pltp...  2.73 us
    ppermute x2, starting transfers between devices, on_device(): lax.ppermute(block, 'dp', [(i, (i + step) % groups) for i in range(groups)])  2.16 us
    ppermute x2, waiting for transfers between devices, on_device(): lax.ppermute(block, 'dp', [(i, (i + step) % groups) for i in range(groups)])  1.32 us
    pallas_call x1, Pallas kernels, update(): pl.pallas_call(update_kernel, out_shape=(whole, pltpu.VMEM((tilts * left,...  0.97 us
    pallas_call x1, Pallas kernels, on_device(): pl.pallas_call(log_kernel, out_shape=jax.ShapeDtypeStruct((count, tilts,...  0.72 us
  transfers between devices with their start and end apart: 7, of which 7 were waited for; matrix products, arithmetic and copies ran while one was open for 0% of the time, Pallas kernels for 20%

profile of v5, /device:TPU:0, one launch (start us, length us, event | category | flops | bytes accessed | tf_op | source)
XLA Modules:
  0.0 26.5 jit_solution(10960048994615390203)
XLA Ops:
  0.6 3.9 %expect.1 = (f32[16,64,512]{2,1,0:T(8,128)S(1)}, f32[32,512]{1,0:T(8,128)S(1)}, f32[1,128]{1,0:T(1,128)S(1)}, bf16[4,256,256]{2,1,0:T(8,128)(2,1)S(1)}) custom-call(s32[16,128,512]{2,1,0:T(8,128)} %frames.3, f32[2,128,512]{2,1,0:T(8,128)} %slices.3, bf16[4,256,256]{2,1,0:T(8,128)(2,1)} %constant.2.clone.table), custom_call_target="tpu_custom_call" | custom-call | tf_op jit(solution)/shard_map/expect/pallas_call | solution.py:274
  4.6 0.5 %collective-permute-start = (f32[1,128]{1,0:T(1,128)S(1)}, f32[1,128]{1,0:T(1,128)S(1)}, u32[]{:S(2)}, u32[]{:S(2)}) collective-permute-start(f32[1,128]{1,0:T(1,128)S(1)} %get-tuple-element.10.local), channel_id=1, source_target_pairs={{0,1},{1,0},{2,3},{3,2},{4,5},{5,4},{6,7},{7,6},{8,9},{9,8},{10,11... | collective-permute-start | bytes 1544 | tf_op jit(solution)/shard_map/ppermute | solution.py:522
  5.1 0.8 %collective-permute-done = f32[1,128]{1,0:T(1,128)S(1)} collective-permute-done((f32[1,128]{1,0:T(1,128)S(1)}, f32[1,128]{1,0:T(1,128)S(1)}, u32[]{:S(2)}, u32[]{:S(2)}) %collective-permute-start) | collective-permute-done | bytes 544 | tf_op jit(solution)/shard_map/ppermute | solution.py:522
  5.9 3.7 %collective-permute-start.3 = (f32[1,128]{1,0:T(1,128)S(1)}, f32[1,128]{1,0:T(1,128)S(1)}, u32[]{:S(2)}, u32[]{:S(2)}) collective-permute-start(f32[1,128]{1,0:T(1,128)S(1)} %log_add_fusion.2), channel_id=1, source_target_pairs={{0,7},{1,6},{2,5},{3,4},{4,3},{5,2},{6,1},{7,0},{8,15},{9,14},{10,... | collective-permute-start | bytes 1544 | tf_op jit(solution)/shard_map/ppermute | solution.py:522
  9.6 0.4 %collective-permute-start.2 = (f32[1,128]{1,0:T(1,128)S(1)}, f32[1,128]{1,0:T(1,128)S(1)}, u32[]{:S(2)}, u32[]{:S(2)}) collective-permute-start(f32[1,128]{1,0:T(1,128)S(1)} %log_add_fusion.2), channel_id=1, source_target_pairs={{0,5},{1,4},{2,7},{3,6},{4,1},{5,0},{6,3},{7,2},{8,13},{9,12},{10,... | collective-permute-start | bytes 1544 | tf_op jit(solution)/shard_map/ppermute | solution.py:522
  9.9 0.2 collective-permute-start.1
  10.1 0.7 %collective-permute-done.3 = f32[1,128]{1,0:T(1,128)S(1)} collective-permute-done((f32[1,128]{1,0:T(1,128)S(1)}, f32[1,128]{1,0:T(1,128)S(1)}, u32[]{:S(2)}, u32[]{:S(2)}) %collective-permute-start.3) | collective-permute-done | bytes 544 | tf_op jit(solution)/shard_map/ppermute | solution.py:522
  10.9 1.7 %collective-permute-done.2 = f32[1,128]{1,0:T(1,128)S(1)} collective-permute-done((f32[1,128]{1,0:T(1,128)S(1)}, f32[1,128]{1,0:T(1,128)S(1)}, u32[]{:S(2)}, u32[]{:S(2)}) %collective-permute-start.2) | collective-permute-done | bytes 544 | tf_op jit(solution)/shard_map/ppermute | solution.py:522
  12.5 0.4 %collective-permute-done.1 = f32[1,128]{1,0:T(1,128)S(1)} collective-permute-done((f32[1,128]{1,0:T(1,128)S(1)}, f32[1,128]{1,0:T(1,128)S(1)}, u32[]{:S(2)}, u32[]{:S(2)}) %collective-permute-start.1) | collective-permute-done | bytes 544 | tf_op jit(solution)/shard_map/ppermute | solution.py:522
  12.9 2.5 %collective-permute-start.4 = (f32[1,128]{1,0:T(1,128)S(1)}, f32[1,128]{1,0:T(1,128)S(1)}, u32[]{:S(2)}, u32[]{:S(2)}) collective-permute-start(f32[1,128]{1,0:T(1,128)S(1)} %log_add_fusion.1), channel_id=1, source_target_pairs={{0,9},{1,8},{2,11},{3,10},{4,13},{5,12},{6,15},{7,14},{8,1},{9,0},... | collective-permute-start | bytes 1544 | tf_op jit(solution)/shard_map/ppermute | solution.py:522
  15.4 0.2 transform.1.forms
  15.6 1.2 %collective-permute-done.4 = f32[1,128]{1,0:T(1,128)S(1)} collective-permute-done((f32[1,128]{1,0:T(1,128)S(1)}, f32[1,128]{1,0:T(1,128)S(1)}, u32[]{:S(2)}, u32[]{:S(2)}) %collective-permute-start.4) | collective-permute-done | bytes 544 | tf_op jit(solution)/shard_map/ppermute | solution.py:522
  16.9 0.4 %back.1 = f32[264,128]{1,0:T(8,128)S(1)} custom-call(f32[16,64,512]{2,1,0:T(8,128)S(1)} %get-tuple-element.11.spec, f32[3,32,256]{2,1,0:T(8,128)S(1)} %transform.1.forms, f32[1,128]{1,0:T(1,128)S(1)} %get-tuple-element.10.local, f32[1,128]{1,0:T(1,128)S(1)} %log_add_fusion.lse), custom_call_target="tpu_custom_call" | custom-call | flops 268435456 | bytes 1048576 | tf_op jit(solution)/shard_map/back/pallas_call | solution.py:405
  17.2 0.0 copy-start
  17.3 1.6 %collective-permute-start.5 = (f32[264,128]{1,0:T(8,128)S(1)}, f32[264,128]{1,0:T(8,128)S(1)}, u32[]{:S(2)}, u32[]{:S(2)}) collective-permute-start(f32[264,128]{1,0:T(8,128)S(1)} %back.1), channel_id=1, source_target_pairs={{0,16},{16,0},{1,17},{17,1},{2,18},{18,2},{3,19},{19,3},{4,20},{20... | collective-permute-start | bytes 405512 | tf_op jit(solution)/shard_map/ppermute | solution.py:556
  18.8 0.6 %back_signal.1 = f32[64,512]{1,0:T(8,128)S(1)} custom-call(f32[16,64,512]{2,1,0:T(8,128)S(1)} %get-tuple-element.11.spec, f32[3,32,256]{2,1,0:T(8,128)S(1)} %transform.1.forms, f32[1,128]{1,0:T(1,128)S(1)} %get-tuple-element.10.local, f32[1,128]{1,0:T(1,128)S(1)} %log_add_fusion.lse, bf16[4,256,256]{2,1,0:T(8,128)(2,1)S(1)} %get-tuple-element.12.table), custom_call_target="tpu_custom_call" | custom-call | flops 268435456 | bytes 1048576 | tf_op jit(solution)/shard_map/back_signal/pallas_call | solution.py:406
  19.5 0.6 %collective-permute-start.6 = (f32[64,512]{1,0:T(8,128)S(1)}, f32[64,512]{1,0:T(8,128)S(1)}, u32[]{:S(2)}, u32[]{:S(2)}) collective-permute-start(f32[64,512]{1,0:T(8,128)S(1)} %back_signal.1), channel_id=1, source_target_pairs={{0,16},{16,0},{1,17},{17,1},{2,18},{18,2},{3,19},{19,3},{4,20},{20... | collective-permute-start | bytes 393224 | tf_op jit(solution)/shard_map/ppermute | solution.py:556
  20.1 2.7 %back_own.1.own = f32[520,128]{1,0:T(8,128)S(1)} custom-call(f32[3,32,256]{2,1,0:T(8,128)S(1)} %transform.1.forms, f32[1,128]{1,0:T(1,128)S(1)} %get-tuple-element.10.local, f32[1,128]{1,0:T(1,128)S(1)} %log_add_fusion.lse, s32[16,128,512]{2,1,0:T(8,128)} %frames.3, bf16[4,256,256]{2,1,0:T(8,128)(2,1)S(1)} %get-tuple-element.12.table), custom_call_target="tpu_custom_call" | custom-call | tf_op jit(solution)/shard_map/back_own/pallas_call | solution.py:413
  22.8 0.9 %collective-permute-done.5.after.other = f32[264,128]{1,0:T(8,128)S(1)} collective-permute-done((f32[264,128]{1,0:T(8,128)S(1)}, f32[264,128]{1,0:T(8,128)S(1)}, u32[]{:S(2)}, u32[]{:S(2)}) %collective-permute-start.5) | collective-permute-done | bytes 135200 | tf_op jit(solution)/shard_map/ppermute | solution.py:556
  23.7 0.7 %log_resp.1 = f32[16,2,512]{2,1,0:T(2,128)} custom-call(f32[32,512]{1,0:T(8,128)S(1)} %get-tuple-element.9.scores, f32[1,128]{1,0:T(1,128)S(1)} %log_add_fusion.lse, f32[264,128]{1,0:T(8,128)S(1)} %collective-permute-done.5.after.other), custom_call_target="tpu_custom_call" | custom-call | tf_op jit(solution)/shard_map/log_resp/pallas_call | solution.py:560
  24.5 0.0 copy-done
  24.5 1.0 %update.1 = (f32[2,64,512]{2,1,0:T(8,128)}, f32[64,512]{1,0:T(8,128)S(1)}, f32[64,128]{1,0:T(8,128)S(1)}) custom-call(f32[520,128]{1,0:T(8,128)S(1)} %back_own.1.own, f32[264,128]{1,0:T(8,128)S(1)} %collective-permute-done.5.after.other, f32[2,128,512]{2,1,0:T(8,128)S(1)} %copy-done, bf16[4,256,256]{2,1,0:T(8,128)(2,1)S(1)} %get-tuple-element.12.table), custom_call_target="tpu_custom_call" | custom-call | tf_op jit(solution)/shard_map/update/pallas_call | solution.py:488
  25.5 0.4 %collective-permute-done.6.other = f32[64,512]{1,0:T(8,128)S(1)} collective-permute-done((f32[64,512]{1,0:T(8,128)S(1)}, f32[64,512]{1,0:T(8,128)S(1)}, u32[]{:S(2)}, u32[]{:S(2)}) %collective-permute-start.6) | collective-permute-done | bytes 131104 | tf_op jit(solution)/shard_map/ppermute | solution.py:556
  25.8 0.7 %finish.1 = f32[2,64,512]{2,1,0:T(8,128)} custom-call(f32[64,512]{1,0:T(8,128)S(1)} %collective-permute-done.6.other, f32[64,512]{1,0:T(8,128)S(1)} %get-tuple-element.13.rest, f32[64,128]{1,0:T(8,128)S(1)} %get-tuple-element.14.factor, f32[2,64,512]{2,1,0:T(8,128)} %get-tuple-element.15.earlier), custom_call_target="tpu_custom_call", output_to_operand_aliasing={{}: (3, {})} | custom-call | tf_op jit(solution)/shard_map/finish/pallas_call | solution.py:497
  (3 shorter events, 0.0 us)
Async XLA Ops:
  4.6 1.3 %collective-permute-start = (f32[1,128]{1,0:T(1,128)S(1)}, f32[1,128]{1,0:T(1,128)S(1)}, u32[]{:S(2)}, u32[]{:S(2)}) collective-permute-start(f32[1,128]{1,0:T(1,128)S(1)} %get-tuple-element.10.local), channel_id=1, source_target_pairs={{0,1},{1,0},{2,3},{3,2},{4,5},{5,4},{6,7},{7,6},{8,9},{9,8},{10,11... | collective-permute-start | bytes 1544 | tf_op jit(solution)/shard_map/ppermute | solution.py:522
  5.9 5.0 %collective-permute-start.3 = (f32[1,128]{1,0:T(1,128)S(1)}, f32[1,128]{1,0:T(1,128)S(1)}, u32[]{:S(2)}, u32[]{:S(2)}) collective-permute-start(f32[1,128]{1,0:T(1,128)S(1)} %log_add_fusion.2), channel_id=1, source_target_pairs={{0,7},{1,6},{2,5},{3,4},{4,3},{5,2},{6,1},{7,0},{8,15},{9,14},{10,... | collective-permute-start | bytes 1544 | tf_op jit(solution)/shard_map/ppermute | solution.py:522
  9.6 3.0 %collective-permute-start.2 = (f32[1,128]{1,0:T(1,128)S(1)}, f32[1,128]{1,0:T(1,128)S(1)}, u32[]{:S(2)}, u32[]{:S(2)}) collective-permute-start(f32[1,128]{1,0:T(1,128)S(1)} %log_add_fusion.2), channel_id=1, source_target_pairs={{0,5},{1,4},{2,7},{3,6},{4,1},{5,0},{6,3},{7,2},{8,13},{9,12},{10,... | collective-permute-start | bytes 1544 | tf_op jit(solution)/shard_map/ppermute | solution.py:522
  9.9 3.0 %collective-permute-start.1 = (f32[1,128]{1,0:T(1,128)S(1)}, f32[1,128]{1,0:T(1,128)S(1)}, u32[]{:S(2)}, u32[]{:S(2)}) collective-permute-start(f32[1,128]{1,0:T(1,128)S(1)} %log_add_fusion.2), channel_id=1, source_target_pairs={{0,3},{1,2},{2,1},{3,0},{4,7},{5,6},{6,5},{7,4},{8,11},{9,10},{10,... | collective-permute-start | bytes 1544 | tf_op jit(solution)/shard_map/ppermute | solution.py:522
  12.9 3.9 %collective-permute-start.4 = (f32[1,128]{1,0:T(1,128)S(1)}, f32[1,128]{1,0:T(1,128)S(1)}, u32[]{:S(2)}, u32[]{:S(2)}) collective-permute-start(f32[1,128]{1,0:T(1,128)S(1)} %log_add_fusion.1), channel_id=1, source_target_pairs={{0,9},{1,8},{2,11},{3,10},{4,13},{5,12},{6,15},{7,14},{8,1},{9,0},... | collective-permute-start | bytes 1544 | tf_op jit(solution)/shard_map/ppermute | solution.py:522
  17.2 7.2 %copy-start = (f32[2,128,512]{2,1,0:T(8,128)S(1)}, f32[2,128,512]{2,1,0:T(8,128)}, u32[]{:S(2)}) copy-start(f32[2,128,512]{2,1,0:T(8,128)} %slices.3) | copy-start | bytes 1572868
  17.3 6.5 %collective-permute-start.5 = (f32[264,128]{1,0:T(8,128)S(1)}, f32[264,128]{1,0:T(8,128)S(1)}, u32[]{:S(2)}, u32[]{:S(2)}) collective-permute-start(f32[264,128]{1,0:T(8,128)S(1)} %back.1), channel_id=1, source_target_pairs={{0,16},{16,0},{1,17},{17,1},{2,18},{18,2},{3,19},{19,3},{4,20},{20... | collective-permute-start | bytes 405512 | tf_op jit(solution)/shard_map/ppermute | solution.py:556
  19.5 6.3 %collective-permute-start.6 = (f32[64,512]{1,0:T(8,128)S(1)}, f32[64,512]{1,0:T(8,128)S(1)}, u32[]{:S(2)}, u32[]{:S(2)}) collective-permute-start(f32[64,512]{1,0:T(8,128)S(1)} %back_signal.1), channel_id=1, source_target_pairs={{0,16},{16,0},{1,17},{17,1},{2,18},{18,2},{3,19},{19,3},{4,20},{20... | collective-permute-start | bytes 393224 | tf_op jit(solution)/shard_map/ppermute | solution.py:556

commit v6 on v5

--- a/solution.py
+++ b/solution.py
@@ -15,6 +15,7 @@
 LANES = 128
 SUB = 8
 VMEM_BYTES = 24 * 1024 * 1024
+OWN_LOADS = 4
 VECTOR_COST = 128
 
 
@@ -367,18 +368,18 @@
 def back_own_kernel(forms, local, lse, frames, table, out, counts, spec, scaled, sem):
     count, share, angles = spec.shape
     half = angles // 2
-    copy = pltpu.make_async_copy(frames.at[:, pl.ds(own_shells(0, share), share), :], counts, sem)
-    copy.start()
-    copy.wait()
-    chunk = min(count, 8)
-
-    def step(c, carry):
-        at = pl.ds(c * chunk, chunk)
+    chunk = count // OWN_LOADS
+    parts = [pl.ds(c * chunk, chunk) for c in range(OWN_LOADS)]
+    copies = [
+        pltpu.make_async_copy(frames.at[at, pl.ds(own_shells(0, share), share), :], counts.at[at], sem.at[c])
+        for c, at in enumerate(parts)
+    ]
+    for copy in copies:
+        copy.start()
+    for at, copy in zip(parts, copies):
+        copy.wait()
         for odd, part in enumerate(spectra(counts[at], table)):
             spec[at, :, odd * half : (odd + 1) * half] = part
-        return carry
-
-    lax.fori_loop(0, count // chunk, step, 0)
     back_project(0, spec, forms, local, lse, out, scaled)
 
 
@@ -417,13 +418,13 @@
             pltpu.VMEM(shape, jnp.int32),
             pltpu.VMEM(shape, F32),
             scaled,
-            pltpu.SemaphoreType.DMA,
+            pltpu.SemaphoreType.DMA((OWN_LOADS,)),
         ],
         name="back_own",
     )(forms, local, lse, in_hbm(frames), table)
 
 
-def log_kernel(scores, lse, after, out):
+def log_responsibilities(scores, lse, out):
     count, tilts, _ = out.shape
     chunk = SUB // tilts
     value = scores[...] - unpack_rows(lse[...], scores.shape[0] // SUB, tilts, scores.shape[1])
@@ -433,10 +434,13 @@
             out[pl.ds(c * chunk, chunk), t, :] = value[at : at + chunk]
 
 
-def update_kernel(own, other, slices, table, out, rest, factor, result, sem):
+def update_kernel(own, other, slices, table, scores, lse, out, logs, rest, factor, result, value, sem, log_sem):
     tilts, rows, angles = result.shape
     share = out.shape[1]
     sections = angles // LANES
+    log_responsibilities(scores, lse, value)
+    log_copy = pltpu.make_async_copy(value, logs, log_sem)
+    log_copy.start()
 
     def numer(first, count, extra):
         columns = []
@@ -465,45 +469,64 @@
         rest[to, :] = (part[to] + before) * scale[t : t + 1, :1]
         factor[to, :] = jnp.broadcast_to(scale[t : t + 1, :], (left, LANES))
     copy.wait()
-
-
-def finish_kernel(other, rest, factor, earlier, out, result, sem):
-    tilts, rows, angles = result.shape
+    log_copy.wait()
+
+
+def finish_kernel(*refs):
+    *others, rest, factor, earlier, out, result, sem = refs
+    tilts, left, angles = result.shape
     share = out.shape[1]
-    for lanes in range(0, angles, LANES):
-        at = pl.ds(lanes, LANES)
-        result[:, :, at] = (other[:, at] * factor[...] + rest[:, at]).reshape(tilts, rows, LANES)
-    copy = pltpu.make_async_copy(result, out.at[:, pl.ds(share - rows, rows), :], sem)
+    first = 0
+    for other in others:
+        rows = other.shape[0] // tilts
+        for t in range(tilts):
+            at = pl.ds(t * left + first, rows)
+            scale = jnp.concatenate([factor[at, :]] * (angles // LANES), axis=1)
+            result[t, pl.ds(first, rows), :] = other[pl.ds(t * rows, rows), :] * scale + rest[at, :]
+        first += rows
+    copy = pltpu.make_async_copy(result, out.at[:, pl.ds(share - left, left), :], sem)
     copy.start()
     copy.wait()
 
 
-def update(own, others, slices, table, share, rows):
+def update(own, others, slices, table, scores, lse, share, rows):
     tilts, _, angles = slices.shape
     left = share - rows
     hbm = pl.BlockSpec(memory_space=pltpu.HBM)
     vm = pl.BlockSpec(memory_space=pltpu.VMEM)
     params = pltpu.CompilerParams(vmem_limit_bytes=VMEM_BYTES)
     whole = jax.ShapeDtypeStruct((tilts, share, angles), F32)
-    new, rest, factor = pl.pallas_call(
+    log_shape = (scores.shape[0] // tilts, tilts, angles)
+    new, log_resp, rest, factor = pl.pallas_call(
         update_kernel,
-        out_shape=(whole, pltpu.VMEM((tilts * left, angles), F32), pltpu.VMEM((tilts * left, LANES), F32)),
-        in_specs=[vm] * 4,
-        out_specs=(hbm, vm, vm),
-        scratch_shapes=[pltpu.VMEM((tilts, rows, angles), F32), pltpu.SemaphoreType.DMA],
+        out_shape=(
+            whole,
+            jax.ShapeDtypeStruct(log_shape, F32),
+            pltpu.VMEM((tilts * left, angles), F32),
+            pltpu.VMEM((tilts * left, LANES), F32),
+        ),
+        in_specs=[vm] * 6,
+        out_specs=(hbm, hbm, vm, vm),
+        scratch_shapes=[
+            pltpu.VMEM((tilts, rows, angles), F32),
+            pltpu.VMEM(log_shape, F32),
+            pltpu.SemaphoreType.DMA,
+            pltpu.SemaphoreType.DMA,
+        ],
         compiler_params=params,
         name="update",
-    )(own, others[0], slices, table)
-    return pl.pallas_call(
+    )(own, others[0], slices, table, scores, lse)
+    new = pl.pallas_call(
         finish_kernel,
         out_shape=whole,
-        in_specs=[vm] * 3 + [hbm],
+        in_specs=[vm] * (len(others) + 1) + [hbm],
         out_specs=hbm,
         scratch_shapes=[pltpu.VMEM((tilts, left, angles), F32), pltpu.SemaphoreType.DMA],
-        input_output_aliases={3: 0},
+        input_output_aliases={len(others) + 1: 0},
         compiler_params=params,
         name="finish",
-    )(others[1], rest, factor, new)
+    )(*others[1:], rest, factor, new)
+    return log_resp, new
 
 
 def log_sum(values):
@@ -547,9 +570,11 @@
     lse = over_axis(local, "rot")
 
     shape = (count, share, angles)
-    rows = share // 2 // SUB * SUB
+    units = share // SUB
+    rows = max(3 * units // 8, 1) * SUB
     others = []
-    for first, shells_, signal in ((0, rows, None), (rows, share - rows, table)):
+    for first in range(0, share, rows):
+        shells_, signal = min(rows, share - first), table if first else None
         got = None
         for step in range(1, groups):
             block = back(shape, forms, local, lse, first, shells_, spec=spec[step - 1], table=signal)
@@ -557,16 +582,7 @@
             got = block if got is None else got + block
         others.append(got)
     own = back(shape, forms, local, lse, 0, share, frames=frames, table=table)
-    log_resp = pl.pallas_call(
-        log_kernel,
-        out_shape=jax.ShapeDtypeStruct((count, tilts, angles), F32),
-        in_specs=[vm, vm, pl.BlockSpec(memory_space=pl.ANY)],
-        out_specs=vm,
-        compiler_params=params,
-        name="log_resp",
-    )(scores, lse, others[0])
-    new_slices = update(own, others, slices, table, share, rows)
-    return (log_resp, new_slices)
+    return update(own, others, slices, table, scores, lse, share, rows)
 
 
 def solution(mesh):

time: 26.7 us -> 26.6 us (level)
  starting transfers between devices: 9.37 us -> 11 us
  waiting for transfers between devices: 6.13 us -> 5.21 us
  Pallas kernels: 10.3 us -> 9.53 us
    ppermute x2 -> x3, starting transfers between devices: 2.16 us -> 3.74 us  [on_device(): lax.ppermute(block, 'dp', [(i, (i + step) % groups) for i in range(groups)])]
    ppermute x2 -> x3, waiting for transfers between devices: 1.32 us -> 0.4 us  [on_device(): lax.ppermute(block, 'dp', [(i, (i + step) % groups) for i in range(groups)])]
    pallas_call x3 -> x2, Pallas kernels: 2.38 us -> 1.74 us  [the longest x1 1.04 us: update(): pl.pallas_call(update_kernel, out_shape=(whole, jax.ShapeDtypeStruct(log_...]
    pallas_call x1, Pallas kernels: 2.73 us -> 2.4 us  [back(): call(back_own_kernel, in_specs=[vm] * 3 + [pl.BlockSpec(memory_space=pltp...]
    pallas_call x1 -> x2, Pallas kernels: 0.64 us -> 0.93 us  [back(): call(functools.partial(back_signal_kernel, first), out_shape=pltpu.VMEM((...]
  transfers between devices with their start and end apart: 7 -> 8, of which waited for: 7 -> 6; matrix products, arithmetic and copies ran while one was open for 0% -> 0% of each run, Pallas kernels for 20% -> 17%
where the time goes in v6:
time: 26.6 us; the launch traced here: 26.4 us
  starting transfers between devices  11 us (41%)
  Pallas kernels  9.53 us (36%)
  waiting for transfers between devices  5.21 us (20%)
  between operations  0.71 us (3%)
    ppermute x5, starting transfers between devices, over_axis(): lax.ppermute(value, axis, [(i, i ^ step) for i in range(size)])  7.21 us
    ppermute x5, waiting for transfers between devices, over_axis(): lax.ppermute(value, axis, [(i, i ^ step) for i in range(size)])  4.81 us
    pallas_call x1, Pallas kernels, expect(): pl.pallas_call(functools.partial(expect_kernel, anneal, chunk, groups), o...  3.92 us
    ppermute x3, starting transfers between devices, on_device(): lax.ppermute(block, 'dp', [(i, (i + step) % groups) for i in range(groups)])  3.74 us
    pallas_call x1, Pallas kernels, back(): call(back_own_kernel, in_specs=[vm] * 3 + [pl.BlockSpec(memory_space=pltp...  2.4 us
    pallas_call x1, Pallas kernels, update(): pl.pallas_call(update_kernel, out_shape=(whole, jax.ShapeDtypeStruct(log_...  1.04 us
    pallas_call x2, Pallas kernels, back(): call(functools.partial(back_signal_kernel, first), out_shape=pltpu.VMEM((...  0.93 us
    pallas_call x1, Pallas kernels, update(): pl.pallas_call(finish_kernel, out_shape=whole, in_specs=[vm] * (len(other...  0.7 us
  transfers between devices with their start and end apart: 8, of which 6 were waited for; matrix products, arithmetic and copies ran while one was open for 0% of the time, Pallas kernels for 17%

profile of v6, /device:TPU:0, one launch (start us, length us, event | category | flops | bytes accessed | tf_op | source)
XLA Modules:
  0.0 26.4 jit_solution(15877182604072719614)
XLA Ops:
  0.6 3.9 %expect.1 = (f32[16,64,512]{2,1,0:T(8,128)S(1)}, f32[32,512]{1,0:T(8,128)S(1)}, f32[1,128]{1,0:T(1,128)S(1)}, bf16[4,256,256]{2,1,0:T(8,128)(2,1)S(1)}) custom-call(s32[16,128,512]{2,1,0:T(8,128)} %frames.3, f32[2,128,512]{2,1,0:T(8,128)} %slices.3, bf16[4,256,256]{2,1,0:T(8,128)(2,1)} %constant.2.clone.table), custom_call_target="tpu_custom_call" | custom-call | tf_op jit(solution)/shard_map/expect/pallas_call | solution.py:275
  4.6 0.5 %collective-permute-start = (f32[1,128]{1,0:T(1,128)S(1)}, f32[1,128]{1,0:T(1,128)S(1)}, u32[]{:S(2)}, u32[]{:S(2)}) collective-permute-start(f32[1,128]{1,0:T(1,128)S(1)} %get-tuple-element.11.local), channel_id=1, source_target_pairs={{0,1},{1,0},{2,3},{3,2},{4,5},{5,4},{6,7},{7,6},{8,9},{9,8},{10,11... | collective-permute-start | bytes 1544 | tf_op jit(solution)/shard_map/ppermute | solution.py:545
  5.1 0.8 %collective-permute-done = f32[1,128]{1,0:T(1,128)S(1)} collective-permute-done((f32[1,128]{1,0:T(1,128)S(1)}, f32[1,128]{1,0:T(1,128)S(1)}, u32[]{:S(2)}, u32[]{:S(2)}) %collective-permute-start) | collective-permute-done | bytes 544 | tf_op jit(solution)/shard_map/ppermute | solution.py:545
  5.9 3.7 %collective-permute-start.3 = (f32[1,128]{1,0:T(1,128)S(1)}, f32[1,128]{1,0:T(1,128)S(1)}, u32[]{:S(2)}, u32[]{:S(2)}) collective-permute-start(f32[1,128]{1,0:T(1,128)S(1)} %log_add_fusion.2), channel_id=1, source_target_pairs={{0,7},{1,6},{2,5},{3,4},{4,3},{5,2},{6,1},{7,0},{8,15},{9,14},{10,... | collective-permute-start | bytes 1544 | tf_op jit(solution)/shard_map/ppermute | solution.py:545
  9.6 0.4 %collective-permute-start.2 = (f32[1,128]{1,0:T(1,128)S(1)}, f32[1,128]{1,0:T(1,128)S(1)}, u32[]{:S(2)}, u32[]{:S(2)}) collective-permute-start(f32[1,128]{1,0:T(1,128)S(1)} %log_add_fusion.2), channel_id=1, source_target_pairs={{0,5},{1,4},{2,7},{3,6},{4,1},{5,0},{6,3},{7,2},{8,13},{9,12},{10,... | collective-permute-start | bytes 1544 | tf_op jit(solution)/shard_map/ppermute | solution.py:545
  9.9 0.2 collective-permute-start.1
  10.1 0.7 %collective-permute-done.3 = f32[1,128]{1,0:T(1,128)S(1)} collective-permute-done((f32[1,128]{1,0:T(1,128)S(1)}, f32[1,128]{1,0:T(1,128)S(1)}, u32[]{:S(2)}, u32[]{:S(2)}) %collective-permute-start.3) | collective-permute-done | bytes 544 | tf_op jit(solution)/shard_map/ppermute | solution.py:545
  10.9 1.7 %collective-permute-done.2 = f32[1,128]{1,0:T(1,128)S(1)} collective-permute-done((f32[1,128]{1,0:T(1,128)S(1)}, f32[1,128]{1,0:T(1,128)S(1)}, u32[]{:S(2)}, u32[]{:S(2)}) %collective-permute-start.2) | collective-permute-done | bytes 544 | tf_op jit(solution)/shard_map/ppermute | solution.py:545
  12.5 0.4 %collective-permute-done.1 = f32[1,128]{1,0:T(1,128)S(1)} collective-permute-done((f32[1,128]{1,0:T(1,128)S(1)}, f32[1,128]{1,0:T(1,128)S(1)}, u32[]{:S(2)}, u32[]{:S(2)}) %collective-permute-start.1) | collective-permute-done | bytes 544 | tf_op jit(solution)/shard_map/ppermute | solution.py:545
  12.9 2.5 %collective-permute-start.4 = (f32[1,128]{1,0:T(1,128)S(1)}, f32[1,128]{1,0:T(1,128)S(1)}, u32[]{:S(2)}, u32[]{:S(2)}) collective-permute-start(f32[1,128]{1,0:T(1,128)S(1)} %log_add_fusion.1), channel_id=1, source_target_pairs={{0,9},{1,8},{2,11},{3,10},{4,13},{5,12},{6,15},{7,14},{8,1},{9,0},... | collective-permute-start | bytes 1544 | tf_op jit(solution)/shard_map/ppermute | solution.py:545
  15.4 0.2 transform.1.forms
  15.6 1.2 %collective-permute-done.4 = f32[1,128]{1,0:T(1,128)S(1)} collective-permute-done((f32[1,128]{1,0:T(1,128)S(1)}, f32[1,128]{1,0:T(1,128)S(1)}, u32[]{:S(2)}, u32[]{:S(2)}) %collective-permute-start.4) | collective-permute-done | bytes 544 | tf_op jit(solution)/shard_map/ppermute | solution.py:545
  16.9 0.3 %back.1 = f32[200,128]{1,0:T(8,128)S(1)} custom-call(f32[16,64,512]{2,1,0:T(8,128)S(1)} %get-tuple-element.13.spec, f32[3,32,256]{2,1,0:T(8,128)S(1)} %transform.1.forms, f32[1,128]{1,0:T(1,128)S(1)} %get-tuple-element.11.local, f32[1,128]{1,0:T(1,128)S(1)} %log_add_fusion.lse), custom_call_target="tpu_custom_call" | custom-call | flops 201326592 | bytes 786432 | tf_op jit(solution)/shard_map/back/pallas_call | solution.py:406
  17.2 1.6 %collective-permute-start.5 = (f32[200,128]{1,0:T(8,128)S(1)}, f32[200,128]{1,0:T(8,128)S(1)}, u32[]{:S(2)}, u32[]{:S(2)}) collective-permute-start(f32[200,128]{1,0:T(8,128)S(1)} %back.1), channel_id=1, source_target_pairs={{0,16},{16,0},{1,17},{17,1},{2,18},{18,2},{3,19},{19,3},{4,20},{20... | collective-permute-start | bytes 307208 | tf_op jit(solution)/shard_map/ppermute | solution.py:581
  18.8 0.5 %back_signal.2 = f32[48,512]{1,0:T(8,128)S(1)} custom-call(f32[16,64,512]{2,1,0:T(8,128)S(1)} %get-tuple-element.13.spec, f32[3,32,256]{2,1,0:T(8,128)S(1)} %transform.1.forms, f32[1,128]{1,0:T(1,128)S(1)} %get-tuple-element.11.local, f32[1,128]{1,0:T(1,128)S(1)} %log_add_fusion.lse, bf16[4,256,256]{2,1,0:T(8,128)(2,1)S(1)} %get-tuple-element.12.table), custom_call_target="tpu_custom_call" | custom-call | flops 201326592 | bytes 786432 | tf_op jit(solution)/shard_map/back_signal/pallas_call | solution.py:407
  19.3 0.0 copy-start
  19.3 0.6 %collective-permute-start.6 = (f32[48,512]{1,0:T(8,128)S(1)}, f32[48,512]{1,0:T(8,128)S(1)}, u32[]{:S(2)}, u32[]{:S(2)}) collective-permute-start(f32[48,512]{1,0:T(8,128)S(1)} %back_signal.2), channel_id=1, source_target_pairs={{0,16},{16,0},{1,17},{17,1},{2,18},{18,2},{3,19},{19,3},{4,20},{20... | collective-permute-start | bytes 294920 | tf_op jit(solution)/shard_map/ppermute | solution.py:581
  19.9 0.4 %back_signal.3 = f32[32,512]{1,0:T(8,128)S(1)} custom-call(f32[16,64,512]{2,1,0:T(8,128)S(1)} %get-tuple-element.13.spec, f32[3,32,256]{2,1,0:T(8,128)S(1)} %transform.1.forms, f32[1,128]{1,0:T(1,128)S(1)} %get-tuple-element.11.local, f32[1,128]{1,0:T(1,128)S(1)} %log_add_fusion.lse, bf16[4,256,256]{2,1,0:T(8,128)(2,1)S(1)} %get-tuple-element.12.table), custom_call_target="tpu_custom_call" | custom-call | flops 134217728 | bytes 524288 | tf_op jit(solution)/shard_map/back_signal/pallas_call | solution.py:407
  20.3 1.6 %collective-permute-start.7 = (f32[32,512]{1,0:T(8,128)S(1)}, f32[32,512]{1,0:T(8,128)S(1)}, u32[]{:S(2)}, u32[]{:S(2)}) collective-permute-start(f32[32,512]{1,0:T(8,128)S(1)} %back_signal.3), channel_id=1, source_target_pairs={{0,16},{16,0},{1,17},{17,1},{2,18},{18,2},{3,19},{19,3},{4,20},{20... | collective-permute-start | bytes 196616 | tf_op jit(solution)/shard_map/ppermute | solution.py:581
  21.9 2.4 %back_own.1.own = f32[520,128]{1,0:T(8,128)S(1)} custom-call(f32[3,32,256]{2,1,0:T(8,128)S(1)} %transform.1.forms, f32[1,128]{1,0:T(1,128)S(1)} %get-tuple-element.11.local, f32[1,128]{1,0:T(1,128)S(1)} %log_add_fusion.lse, s32[16,128,512]{2,1,0:T(8,128)} %frames.3, bf16[4,256,256]{2,1,0:T(8,128)(2,1)S(1)} %get-tuple-element.12.table), custom_call_target="tpu_custom_call" | custom-call | tf_op jit(solution)/shard_map/back_own/pallas_call | solution.py:414
  24.3 0.0 collective-permute-done.5.other
  24.3 0.0 copy-done
  24.3 1.0 %update.1 = (f32[2,64,512]{2,1,0:T(8,128)}, f32[16,2,512]{2,1,0:T(2,128)}, f32[80,512]{1,0:T(8,128)S(1)}, f32[80,128]{1,0:T(8,128)S(1)}) custom-call(f32[520,128]{1,0:T(8,128)S(1)} %back_own.1.own, f32[200,128]{1,0:T(8,128)S(1)} %collective-permute-done.5.other, f32[2,128,512]{2,1,0:T(8,128)S(1)} %copy-done, ...), custom_call_target="tpu_custom_call" | custom-call | tf_op jit(solution)/shard_map/update/pallas_call | solution.py:500
  25.4 0.4 %collective-permute-done.7.refs_1_ = f32[32,512]{1,0:T(8,128)S(1)} collective-permute-done((f32[32,512]{1,0:T(8,128)S(1)}, f32[32,512]{1,0:T(8,128)S(1)}, u32[]{:S(2)}, u32[]{:S(2)}) %collective-permute-start.7) | collective-permute-done | bytes 65568 | tf_op jit(solution)/shard_map/ppermute | solution.py:581
  25.7 0.0 collective-permute-done.6.refs_0_
  25.7 0.7 %finish.1 = f32[2,64,512]{2,1,0:T(8,128)} custom-call(f32[48,512]{1,0:T(8,128)S(1)} %collective-permute-done.6.refs_0_, f32[32,512]{1,0:T(8,128)S(1)} %collective-permute-done.7.refs_1_, f32[80,512]{1,0:T(8,128)S(1)} %get-tuple-element.15.refs_2_, f32[80,128]{1,0:T(8,128)S(1)} %get-tuple-element.16.refs_3_, ...), custom_call_target="tpu_custom_call", output_to_operand_aliasing={{}: (4, {})} | custom-call | tf_op jit(solution)/shard_map/finish/pallas_call | solution.py:519
  (3 shorter events, 0.0 us)
Async XLA Ops:
  4.6 1.3 %collective-permute-start = (f32[1,128]{1,0:T(1,128)S(1)}, f32[1,128]{1,0:T(1,128)S(1)}, u32[]{:S(2)}, u32[]{:S(2)}) collective-permute-start(f32[1,128]{1,0:T(1,128)S(1)} %get-tuple-element.11.local), channel_id=1, source_target_pairs={{0,1},{1,0},{2,3},{3,2},{4,5},{5,4},{6,7},{7,6},{8,9},{9,8},{10,11... | collective-permute-start | bytes 1544 | tf_op jit(solution)/shard_map/ppermute | solution.py:545
  5.9 5.0 %collective-permute-start.3 = (f32[1,128]{1,0:T(1,128)S(1)}, f32[1,128]{1,0:T(1,128)S(1)}, u32[]{:S(2)}, u32[]{:S(2)}) collective-permute-start(f32[1,128]{1,0:T(1,128)S(1)} %log_add_fusion.2), channel_id=1, source_target_pairs={{0,7},{1,6},{2,5},{3,4},{4,3},{5,2},{6,1},{7,0},{8,15},{9,14},{10,... | collective-permute-start | bytes 1544 | tf_op jit(solution)/shard_map/ppermute | solution.py:545
  9.6 3.0 %collective-permute-start.2 = (f32[1,128]{1,0:T(1,128)S(1)}, f32[1,128]{1,0:T(1,128)S(1)}, u32[]{:S(2)}, u32[]{:S(2)}) collective-permute-start(f32[1,128]{1,0:T(1,128)S(1)} %log_add_fusion.2), channel_id=1, source_target_pairs={{0,5},{1,4},{2,7},{3,6},{4,1},{5,0},{6,3},{7,2},{8,13},{9,12},{10,... | collective-permute-start | bytes 1544 | tf_op jit(solution)/shard_map/ppermute | solution.py:545
  9.9 3.0 %collective-permute-start.1 = (f32[1,128]{1,0:T(1,128)S(1)}, f32[1,128]{1,0:T(1,128)S(1)}, u32[]{:S(2)}, u32[]{:S(2)}) collective-permute-start(f32[1,128]{1,0:T(1,128)S(1)} %log_add_fusion.2), channel_id=1, source_target_pairs={{0,3},{1,2},{2,1},{3,0},{4,7},{5,6},{6,5},{7,4},{8,11},{9,10},{10,... | collective-permute-start | bytes 1544 | tf_op jit(solution)/shard_map/ppermute | solution.py:545
  12.9 3.9 %collective-permute-start.4 = (f32[1,128]{1,0:T(1,128)S(1)}, f32[1,128]{1,0:T(1,128)S(1)}, u32[]{:S(2)}, u32[]{:S(2)}) collective-permute-start(f32[1,128]{1,0:T(1,128)S(1)} %log_add_fusion.1), channel_id=1, source_target_pairs={{0,9},{1,8},{2,11},{3,10},{4,13},{5,12},{6,15},{7,14},{8,1},{9,0},... | collective-permute-start | bytes 1544 | tf_op jit(solution)/shard_map/ppermute | solution.py:545
  17.2 7.1 %collective-permute-start.5 = (f32[200,128]{1,0:T(8,128)S(1)}, f32[200,128]{1,0:T(8,128)S(1)}, u32[]{:S(2)}, u32[]{:S(2)}) collective-permute-start(f32[200,128]{1,0:T(8,128)S(1)} %back.1), channel_id=1, source_target_pairs={{0,16},{16,0},{1,17},{17,1},{2,18},{18,2},{3,19},{19,3},{4,20},{20... | collective-permute-start | bytes 307208 | tf_op jit(solution)/shard_map/ppermute | solution.py:581
  19.3 5.0 %copy-start = (f32[2,128,512]{2,1,0:T(8,128)S(1)}, f32[2,128,512]{2,1,0:T(8,128)}, u32[]{:S(2)}) copy-start(f32[2,128,512]{2,1,0:T(8,128)} %slices.3) | copy-start | bytes 1572868
  19.3 6.4 %collective-permute-start.6 = (f32[48,512]{1,0:T(8,128)S(1)}, f32[48,512]{1,0:T(8,128)S(1)}, u32[]{:S(2)}, u32[]{:S(2)}) collective-permute-start(f32[48,512]{1,0:T(8,128)S(1)} %back_signal.2), channel_id=1, source_target_pairs={{0,16},{16,0},{1,17},{17,1},{2,18},{18,2},{3,19},{19,3},{4,20},{20... | collective-permute-start | bytes 294920 | tf_op jit(solution)/shard_map/ppermute | solution.py:581
  20.3 5.5 %collective-permute-start.7 = (f32[32,512]{1,0:T(8,128)S(1)}, f32[32,512]{1,0:T(8,128)S(1)}, u32[]{:S(2)}, u32[]{:S(2)}) collective-permute-start(f32[32,512]{1,0:T(8,128)S(1)} %back_signal.3), channel_id=1, source_target_pairs={{0,16},{16,0},{1,17},{17,1},{2,18},{18,2},{3,19},{19,3},{4,20},{20... | collective-permute-start | bytes 196616 | tf_op jit(solution)/shard_map/ppermute | solution.py:581

commit v7 on v6

--- a/solution.py
+++ b/solution.py
@@ -541,7 +541,7 @@
     bits = [1 << i for i in range(size.bit_length() - 1)]
     rounds = [[bit] for bit in bits[:1]] + [bits[i : i + 2] for i in range(1, len(bits), 2)]
     for bits in rounds:
-        steps = [step | 1 for step in ([*bits, sum(bits)] if len(bits) == 2 else bits)]
+        steps = [step | 1 for step in bits] + ([sum(bits)] if len(bits) == 2 else [])
         parts = [lax.ppermute(value, axis, [(i, i ^ step) for i in range(size)]) for step in steps]
         value = log_sum([value, *parts])
     return value

time: 26.6 us -> 26.8 us (level)
  starting transfers between devices: 11 us -> 11.3 us
    ppermute x5, starting transfers between devices: 7.21 us -> 7.57 us  [over_axis(): lax.ppermute(value, axis, [(i, i ^ step) for i in range(size)])]
    ppermute x5, waiting for transfers between devices: 4.81 us -> 4.48 us  [over_axis(): lax.ppermute(value, axis, [(i, i ^ step) for i in range(size)])]
  transfers between devices with their start and end apart: 8 -> 8, of which waited for: 6 -> 5; matrix products, arithmetic and copies ran while one was open for 0% -> 0% of each run, Pallas kernels for 17% -> 17%
where the time goes in v7:
time: 26.8 us; the launch traced here: 26.6 us
  starting transfers between devices  11.3 us (42%)
  Pallas kernels  9.52 us (36%)
  waiting for transfers between devices  5.03 us (19%)
  between operations  0.71 us (3%)
    ppermute x5, starting transfers between devices, over_axis(): lax.ppermute(value, axis, [(i, i ^ step) for i in range(size)])  7.57 us
    ppermute x5, waiting for transfers between devices, over_axis(): lax.ppermute(value, axis, [(i, i ^ step) for i in range(size)])  4.48 us
    pallas_call x1, Pallas kernels, expect(): pl.pallas_call(functools.partial(expect_kernel, anneal, chunk, groups), o...  3.92 us
    ppermute x3, starting transfers between devices, on_device(): lax.ppermute(block, 'dp', [(i, (i + step) % groups) for i in range(groups)])  3.75 us
    pallas_call x1, Pallas kernels, back(): call(back_own_kernel, in_specs=[vm] * 3 + [pl.BlockSpec(memory_space=pltp...  2.4 us
    pallas_call x1, Pallas kernels, update(): pl.pallas_call(update_kernel, out_shape=(whole, jax.ShapeDtypeStruct(log_...  1.04 us
    pallas_call x2, Pallas kernels, back(): call(functools.partial(back_signal_kernel, first), out_shape=pltpu.VMEM((...  0.93 us
    pallas_call x1, Pallas kernels, update(): pl.pallas_call(finish_kernel, out_shape=whole, in_specs=[vm] * (len(other...  0.7 us
  transfers between devices with their start and end apart: 8, of which 5 were waited for; matrix products, arithmetic and copies ran while one was open for 0% of the time, Pallas kernels for 17%

profile of v7, /device:TPU:0, one launch (start us, length us, event | category | flops | bytes accessed | tf_op | source)
XLA Modules:
  0.0 26.6 jit_solution(13884845016648320456)
XLA Ops:
  0.6 3.9 %expect.1 = (f32[16,64,512]{2,1,0:T(8,128)S(1)}, f32[32,512]{1,0:T(8,128)S(1)}, f32[1,128]{1,0:T(1,128)S(1)}, bf16[4,256,256]{2,1,0:T(8,128)(2,1)S(1)}) custom-call(s32[16,128,512]{2,1,0:T(8,128)} %frames.3, f32[2,128,512]{2,1,0:T(8,128)} %slices.3, bf16[4,256,256]{2,1,0:T(8,128)(2,1)} %constant.2.clone.table), custom_call_target="tpu_custom_call" | custom-call | tf_op jit(solution)/shard_map/expect/pallas_call | solution.py:275
  4.6 0.5 %collective-permute-start = (f32[1,128]{1,0:T(1,128)S(1)}, f32[1,128]{1,0:T(1,128)S(1)}, u32[]{:S(2)}, u32[]{:S(2)}) collective-permute-start(f32[1,128]{1,0:T(1,128)S(1)} %get-tuple-element.11.local), channel_id=1, source_target_pairs={{0,1},{1,0},{2,3},{3,2},{4,5},{5,4},{6,7},{7,6},{8,9},{9,8},{10,11... | collective-permute-start | bytes 1544 | tf_op jit(solution)/shard_map/ppermute | solution.py:545
  5.1 0.8 %collective-permute-done = f32[1,128]{1,0:T(1,128)S(1)} collective-permute-done((f32[1,128]{1,0:T(1,128)S(1)}, f32[1,128]{1,0:T(1,128)S(1)}, u32[]{:S(2)}, u32[]{:S(2)}) %collective-permute-start) | collective-permute-done | bytes 544 | tf_op jit(solution)/shard_map/ppermute | solution.py:545
  5.9 3.9 %collective-permute-start.3 = (f32[1,128]{1,0:T(1,128)S(1)}, f32[1,128]{1,0:T(1,128)S(1)}, u32[]{:S(2)}, u32[]{:S(2)}) collective-permute-start(f32[1,128]{1,0:T(1,128)S(1)} %log_add_fusion.2), channel_id=1, source_target_pairs={{0,6},{1,7},{2,4},{3,5},{4,2},{5,3},{6,0},{7,1},{8,14},{9,15},{10,... | collective-permute-start | bytes 1544 | tf_op jit(solution)/shard_map/ppermute | solution.py:545
  9.8 0.0 collective-permute-start.2
  9.8 0.4 %collective-permute-start.1 = (f32[1,128]{1,0:T(1,128)S(1)}, f32[1,128]{1,0:T(1,128)S(1)}, u32[]{:S(2)}, u32[]{:S(2)}) collective-permute-start(f32[1,128]{1,0:T(1,128)S(1)} %log_add_fusion.2), channel_id=1, source_target_pairs={{0,3},{1,2},{2,1},{3,0},{4,7},{5,6},{6,5},{7,4},{8,11},{9,10},{10,... | collective-permute-start | bytes 1544 | tf_op jit(solution)/shard_map/ppermute | solution.py:545
  10.1 1.2 %collective-permute-done.3 = f32[1,128]{1,0:T(1,128)S(1)} collective-permute-done((f32[1,128]{1,0:T(1,128)S(1)}, f32[1,128]{1,0:T(1,128)S(1)}, u32[]{:S(2)}, u32[]{:S(2)}) %collective-permute-start.3) | collective-permute-done | bytes 544 | tf_op jit(solution)/shard_map/ppermute | solution.py:545
  11.3 1.4 %collective-permute-done.2 = f32[1,128]{1,0:T(1,128)S(1)} collective-permute-done((f32[1,128]{1,0:T(1,128)S(1)}, f32[1,128]{1,0:T(1,128)S(1)}, u32[]{:S(2)}, u32[]{:S(2)}) %collective-permute-start.2) | collective-permute-done | bytes 544 | tf_op jit(solution)/shard_map/ppermute | solution.py:545
  12.7 0.0 collective-permute-done.1
  12.8 2.8 %collective-permute-start.4 = (f32[1,128]{1,0:T(1,128)S(1)}, f32[1,128]{1,0:T(1,128)S(1)}, u32[]{:S(2)}, u32[]{:S(2)}) collective-permute-start(f32[1,128]{1,0:T(1,128)S(1)} %log_add_fusion.1), channel_id=1, source_target_pairs={{0,9},{1,8},{2,11},{3,10},{4,13},{5,12},{6,15},{7,14},{8,1},{9,0},... | collective-permute-start | bytes 1544 | tf_op jit(solution)/shard_map/ppermute | solution.py:545
  15.6 0.2 transform.1.forms
  15.8 1.1 %collective-permute-done.4 = f32[1,128]{1,0:T(1,128)S(1)} collective-permute-done((f32[1,128]{1,0:T(1,128)S(1)}, f32[1,128]{1,0:T(1,128)S(1)}, u32[]{:S(2)}, u32[]{:S(2)}) %collective-permute-start.4) | collective-permute-done | bytes 544 | tf_op jit(solution)/shard_map/ppermute | solution.py:545
  16.9 0.3 %back.1 = f32[200,128]{1,0:T(8,128)S(1)} custom-call(f32[16,64,512]{2,1,0:T(8,128)S(1)} %get-tuple-element.13.spec, f32[3,32,256]{2,1,0:T(8,128)S(1)} %transform.1.forms, f32[1,128]{1,0:T(1,128)S(1)} %get-tuple-element.11.local, f32[1,128]{1,0:T(1,128)S(1)} %log_add_fusion.lse), custom_call_target="tpu_custom_call" | custom-call | flops 201326592 | bytes 786432 | tf_op jit(solution)/shard_map/back/pallas_call | solution.py:406
  17.2 1.6 %collective-permute-start.5 = (f32[200,128]{1,0:T(8,128)S(1)}, f32[200,128]{1,0:T(8,128)S(1)}, u32[]{:S(2)}, u32[]{:S(2)}) collective-permute-start(f32[200,128]{1,0:T(8,128)S(1)} %back.1), channel_id=1, source_target_pairs={{0,16},{16,0},{1,17},{17,1},{2,18},{18,2},{3,19},{19,3},{4,20},{20... | collective-permute-start | bytes 307208 | tf_op jit(solution)/shard_map/ppermute | solution.py:581
  18.8 0.5 %back_signal.2 = f32[48,512]{1,0:T(8,128)S(1)} custom-call(f32[16,64,512]{2,1,0:T(8,128)S(1)} %get-tuple-element.13.spec, f32[3,32,256]{2,1,0:T(8,128)S(1)} %transform.1.forms, f32[1,128]{1,0:T(1,128)S(1)} %get-tuple-element.11.local, f32[1,128]{1,0:T(1,128)S(1)} %log_add_fusion.lse, bf16[4,256,256]{2,1,0:T(8,128)(2,1)S(1)} %get-tuple-element.12.table), custom_call_target="tpu_custom_call" | custom-call | flops 201326592 | bytes 786432 | tf_op jit(solution)/shard_map/back_signal/pallas_call | solution.py:407
  19.3 0.0 copy-start
  19.3 0.6 %collective-permute-start.6 = (f32[48,512]{1,0:T(8,128)S(1)}, f32[48,512]{1,0:T(8,128)S(1)}, u32[]{:S(2)}, u32[]{:S(2)}) collective-permute-start(f32[48,512]{1,0:T(8,128)S(1)} %back_signal.2), channel_id=1, source_target_pairs={{0,16},{16,0},{1,17},{17,1},{2,18},{18,2},{3,19},{19,3},{4,20},{20... | collective-permute-start | bytes 294920 | tf_op jit(solution)/shard_map/ppermute | solution.py:581
  19.9 0.4 %back_signal.3 = f32[32,512]{1,0:T(8,128)S(1)} custom-call(f32[16,64,512]{2,1,0:T(8,128)S(1)} %get-tuple-element.13.spec, f32[3,32,256]{2,1,0:T(8,128)S(1)} %transform.1.forms, f32[1,128]{1,0:T(1,128)S(1)} %get-tuple-element.11.local, f32[1,128]{1,0:T(1,128)S(1)} %log_add_fusion.lse, bf16[4,256,256]{2,1,0:T(8,128)(2,1)S(1)} %get-tuple-element.12.table), custom_call_target="tpu_custom_call" | custom-call | flops 134217728 | bytes 524288 | tf_op jit(solution)/shard_map/back_signal/pallas_call | solution.py:407
  20.3 1.6 %collective-permute-start.7 = (f32[32,512]{1,0:T(8,128)S(1)}, f32[32,512]{1,0:T(8,128)S(1)}, u32[]{:S(2)}, u32[]{:S(2)}) collective-permute-start(f32[32,512]{1,0:T(8,128)S(1)} %back_signal.3), channel_id=1, source_target_pairs={{0,16},{16,0},{1,17},{17,1},{2,18},{18,2},{3,19},{19,3},{4,20},{20... | collective-permute-start | bytes 196616 | tf_op jit(solution)/shard_map/ppermute | solution.py:581
  21.9 2.4 %back_own.1.own = f32[520,128]{1,0:T(8,128)S(1)} custom-call(f32[3,32,256]{2,1,0:T(8,128)S(1)} %transform.1.forms, f32[1,128]{1,0:T(1,128)S(1)} %get-tuple-element.11.local, f32[1,128]{1,0:T(1,128)S(1)} %log_add_fusion.lse, s32[16,128,512]{2,1,0:T(8,128)} %frames.3, bf16[4,256,256]{2,1,0:T(8,128)(2,1)S(1)} %get-tuple-element.12.table), custom_call_target="tpu_custom_call" | custom-call | tf_op jit(solution)/shard_map/back_own/pallas_call | solution.py:414
  24.3 0.0 collective-permute-done.5.other
  24.3 0.0 copy-done
  24.3 1.0 %update.1 = (f32[2,64,512]{2,1,0:T(8,128)}, f32[16,2,512]{2,1,0:T(2,128)}, f32[80,512]{1,0:T(8,128)S(1)}, f32[80,128]{1,0:T(8,128)S(1)}) custom-call(f32[520,128]{1,0:T(8,128)S(1)} %back_own.1.own, f32[200,128]{1,0:T(8,128)S(1)} %collective-permute-done.5.other, f32[2,128,512]{2,1,0:T(8,128)S(1)} %copy-done, ...), custom_call_target="tpu_custom_call" | custom-call | tf_op jit(solution)/shard_map/update/pallas_call | solution.py:500
  25.4 0.5 %collective-permute-done.7.refs_1_ = f32[32,512]{1,0:T(8,128)S(1)} collective-permute-done((f32[32,512]{1,0:T(8,128)S(1)}, f32[32,512]{1,0:T(8,128)S(1)}, u32[]{:S(2)}, u32[]{:S(2)}) %collective-permute-start.7) | collective-permute-done | bytes 65568 | tf_op jit(solution)/shard_map/ppermute | solution.py:581
  25.9 0.0 collective-permute-done.6.refs_0_
  25.9 0.7 %finish.1 = f32[2,64,512]{2,1,0:T(8,128)} custom-call(f32[48,512]{1,0:T(8,128)S(1)} %collective-permute-done.6.refs_0_, f32[32,512]{1,0:T(8,128)S(1)} %collective-permute-done.7.refs_1_, f32[80,512]{1,0:T(8,128)S(1)} %get-tuple-element.15.refs_2_, f32[80,128]{1,0:T(8,128)S(1)} %get-tuple-element.16.refs_3_, ...), custom_call_target="tpu_custom_call", output_to_operand_aliasing={{}: (4, {})} | custom-call | tf_op jit(solution)/shard_map/finish/pallas_call | solution.py:519
  (3 shorter events, 0.0 us)
Async XLA Ops:
  4.6 1.3 %collective-permute-start = (f32[1,128]{1,0:T(1,128)S(1)}, f32[1,128]{1,0:T(1,128)S(1)}, u32[]{:S(2)}, u32[]{:S(2)}) collective-permute-start(f32[1,128]{1,0:T(1,128)S(1)} %get-tuple-element.11.local), channel_id=1, source_target_pairs={{0,1},{1,0},{2,3},{3,2},{4,5},{5,4},{6,7},{7,6},{8,9},{9,8},{10,11... | collective-permute-start | bytes 1544 | tf_op jit(solution)/shard_map/ppermute | solution.py:545
  5.9 5.4 %collective-permute-start.3 = (f32[1,128]{1,0:T(1,128)S(1)}, f32[1,128]{1,0:T(1,128)S(1)}, u32[]{:S(2)}, u32[]{:S(2)}) collective-permute-start(f32[1,128]{1,0:T(1,128)S(1)} %log_add_fusion.2), channel_id=1, source_target_pairs={{0,6},{1,7},{2,4},{3,5},{4,2},{5,3},{6,0},{7,1},{8,14},{9,15},{10,... | collective-permute-start | bytes 1544 | tf_op jit(solution)/shard_map/ppermute | solution.py:545
  9.8 3.0 %collective-permute-start.2 = (f32[1,128]{1,0:T(1,128)S(1)}, f32[1,128]{1,0:T(1,128)S(1)}, u32[]{:S(2)}, u32[]{:S(2)}) collective-permute-start(f32[1,128]{1,0:T(1,128)S(1)} %log_add_fusion.2), channel_id=1, source_target_pairs={{0,5},{1,4},{2,7},{3,6},{4,1},{5,0},{6,3},{7,2},{8,13},{9,12},{10,... | collective-permute-start | bytes 1544 | tf_op jit(solution)/shard_map/ppermute | solution.py:545
  9.8 3.0 %collective-permute-start.1 = (f32[1,128]{1,0:T(1,128)S(1)}, f32[1,128]{1,0:T(1,128)S(1)}, u32[]{:S(2)}, u32[]{:S(2)}) collective-permute-start(f32[1,128]{1,0:T(1,128)S(1)} %log_add_fusion.2), channel_id=1, source_target_pairs={{0,3},{1,2},{2,1},{3,0},{4,7},{5,6},{6,5},{7,4},{8,11},{9,10},{10,... | collective-permute-start | bytes 1544 | tf_op jit(solution)/shard_map/ppermute | solution.py:545
  12.8 4.1 %collective-permute-start.4 = (f32[1,128]{1,0:T(1,128)S(1)}, f32[1,128]{1,0:T(1,128)S(1)}, u32[]{:S(2)}, u32[]{:S(2)}) collective-permute-start(f32[1,128]{1,0:T(1,128)S(1)} %log_add_fusion.1), channel_id=1, source_target_pairs={{0,9},{1,8},{2,11},{3,10},{4,13},{5,12},{6,15},{7,14},{8,1},{9,0},... | collective-permute-start | bytes 1544 | tf_op jit(solution)/shard_map/ppermute | solution.py:545
  17.2 7.1 %collective-permute-start.5 = (f32[200,128]{1,0:T(8,128)S(1)}, f32[200,128]{1,0:T(8,128)S(1)}, u32[]{:S(2)}, u32[]{:S(2)}) collective-permute-start(f32[200,128]{1,0:T(8,128)S(1)} %back.1), channel_id=1, source_target_pairs={{0,16},{16,0},{1,17},{17,1},{2,18},{18,2},{3,19},{19,3},{4,20},{20... | collective-permute-start | bytes 307208 | tf_op jit(solution)/shard_map/ppermute | solution.py:581
  19.3 5.0 %copy-start = (f32[2,128,512]{2,1,0:T(8,128)S(1)}, f32[2,128,512]{2,1,0:T(8,128)}, u32[]{:S(2)}) copy-start(f32[2,128,512]{2,1,0:T(8,128)} %slices.3) | copy-start | bytes 1572868
  19.3 6.6 %collective-permute-start.6 = (f32[48,512]{1,0:T(8,128)S(1)}, f32[48,512]{1,0:T(8,128)S(1)}, u32[]{:S(2)}, u32[]{:S(2)}) collective-permute-start(f32[48,512]{1,0:T(8,128)S(1)} %back_signal.2), channel_id=1, source_target_pairs={{0,16},{16,0},{1,17},{17,1},{2,18},{18,2},{3,19},{19,3},{4,20},{20... | collective-permute-start | bytes 294920 | tf_op jit(solution)/shard_map/ppermute | solution.py:581
  20.3 5.6 %collective-permute-start.7 = (f32[32,512]{1,0:T(8,128)S(1)}, f32[32,512]{1,0:T(8,128)S(1)}, u32[]{:S(2)}, u32[]{:S(2)}) collective-permute-start(f32[32,512]{1,0:T(8,128)S(1)} %back_signal.3), channel_id=1, source_target_pairs={{0,16},{16,0},{1,17},{17,1},{2,18},{18,2},{3,19},{19,3},{4,20},{20... | collective-permute-start | bytes 196616 | tf_op jit(solution)/shard_map/ppermute | solution.py:581
